TPU v7x, 256 devices: a whole 4x4x8 slice. The times are simulated.
256 devices in a mesh: dp: 32 (over z, y_lo, core), orient: 8 (over x, y_hi).
Axes of the slice: x: 4, y: 4 (y_hi: 2, y_lo: 2; y = y_hi * 2 + y_lo), z: 8, core: 2. Of those that a mesh axis runs over, the one named last changes fastest.
Arguments:
- images: bfloat16 [16384, 8448], P(('dp', 'orient')), may hold values from -180 to 180
- groups: int32 [16384], P(('dp', 'orient')), may hold values from 0 to 63, as said below
- panel_slots: bfloat16 [32, 512, 8448], P('dp', 'orient'), may hold values from -0.12 to 0.12
- owners: int32 [8], replicated, may hold values from 0 to 31, as said below
- contrast: float32 [64, 4224], replicated, may hold values from -1 to 1
- noise_weight: float32 [4224], replicated, may hold values from 0.5 to 4
- class_prior: float32 [8], replicated, may hold values from -1.5 to 0
Outputs:
- log_evidence: float32 [16384], P(('dp', 'orient'))
- class_posterior: float32 [8, 16384], P(None, ('dp', 'orient'))
- orientation_mass: float32 [8, 512], P(None, 'orient')
Inputs may be any that keep to these rules, and one draw needn't show every extreme that they name: `owners`: distinct; the largest index 31 owns some class. `groups`: group 64 - 1 holds some particle.
All inputs are finite; a program needn't handle non-finite values.
Results may differ from a plain program's by a relative error of at most 0.0021.
Values may be sent and summed in bfloat16 or wider, within the bound.
No kernel may reach another device: no remote copies, remote signals or barrier semaphores. Data moves between devices by JAX's collectives and lax.ppermute only.
A program may use at most 128 MiB of HBM per device.

v0:
```python
import jax
import jax.numpy as jnp
from jax import lax
from jax.sharding import PartitionSpec as P


def broadcast(block, axis, owner):
    block = jnp.where(lax.axis_index(axis) == owner, block, jnp.zeros_like(block))
    return lax.psum(block, axis)


def combined_all(array, axis, combine):
    everything = jax.tree.map(lambda part: lax.all_gather(part, axis), array)
    leading = jax.tree.map(lambda part: part[0], everything)

    def turn(k, so_far):
        return combine(so_far, jax.tree.map(lambda part: part[k], everything))

    return lax.fori_loop(1, lax.axis_size(axis), turn, leading)


def combine_pairs(first, second):
    maximum = jnp.maximum(first[0], second[0])
    totals = first[1] * jnp.exp(first[0] - maximum) + second[1] * jnp.exp(second[0] - maximum)
    return (maximum, totals)


def partial_norms(scores, axis_num):
    maximum = jnp.max(scores, axis=axis_num)
    totals = jnp.sum(jnp.exp(scores - jnp.expand_dims(maximum, axis_num)), axis=axis_num)
    return (maximum, totals)


def one_hot(row_groups, group_count):
    return (row_groups[:, None] == jnp.arange(group_count, dtype=jnp.int32)[None, :]).astype(
        jnp.float32
    )


def per_device(images, groups, panel_slots, owners, contrast, noise_weight, class_prior):
    classes = owners.shape[0]
    group_count = contrast.shape[0]
    pixels = contrast.shape[1]
    part_rows = images.shape[0]
    orient_rows = panel_slots.shape[1]
    orient_count = lax.axis_size("orient")
    dp_count = lax.axis_size("dp")
    local_hot = one_hot(groups, group_count)
    row_contrast = jnp.dot(local_hot, contrast, precision=lax.Precision.HIGHEST)
    factor = row_contrast * noise_weight[None, :]
    weighted = (images.astype(jnp.float32) * jnp.concatenate([factor, factor], axis=1)).astype(
        jnp.bfloat16
    )
    power = contrast * contrast * noise_weight[None, :]

    def reduce_class(maximum, totals):
        return combined_all((maximum, totals), "orient", combine_pairs)

    norm_list = []
    whole_images, whole_groups = (
        lax.all_gather(weighted, "orient", axis=0, tiled=True),
        lax.all_gather(groups, "orient", axis=0, tiled=True),
    )
    whole_hot = one_hot(whole_groups, group_count)
    score_list = []
    for class_id in range(classes):
        panel = broadcast(panel_slots[0], "dp", owners[class_id])
        squared = panel.astype(jnp.float32) ** 2
        power_sum = squared[:, :pixels] + squared[:, pixels:]
        table = lax.dot_general(
            power, power_sum, (((1,), (1,)), ((), ())), precision=lax.Precision.HIGHEST
        )
        crossed = lax.dot_general(
            panel, whole_images, (((1,), (1,)), ((), ())), preferred_element_type=jnp.float32
        )
        penalty = lax.dot_general(
            table, whole_hot, (((0,), (1,)), ((), ())), precision=lax.Precision.HIGHEST
        )
        scored = crossed - 0.5 * penalty + class_prior[class_id]
        score_list.append(scored)
        norm_list.append(reduce_class(*partial_norms(scored, 0)))
    scores = jnp.stack(score_list)
    maximum = jnp.stack([pair[0] for pair in norm_list])
    totals = jnp.stack([pair[1] for pair in norm_list])
    class_lse = maximum + jnp.log(totals)
    top = jnp.max(class_lse, axis=0)
    evidence = top + jnp.log(jnp.sum(jnp.exp(class_lse - top[None, :]), axis=0))
    posterior = jnp.exp(class_lse - evidence[None, :])
    mass_local = jnp.sum(jnp.exp(scores - evidence[None, None, :]), axis=2)
    normalise = classes * orient_rows * orient_count / (part_rows * orient_count * dp_count)
    orientation_mass = lax.psum(mass_local, "dp") * normalise
    first_row = lax.axis_index("orient") * part_rows
    log_evidence = lax.dynamic_slice_in_dim(evidence, first_row, part_rows, 0)
    class_posterior = lax.dynamic_slice_in_dim(posterior, first_row, part_rows, 1)
    return (log_evidence, class_posterior, orientation_mass)


def solution(mesh):
    return jax.shard_map(
        per_device,
        mesh=mesh,
        in_specs=(
            P(("dp", "orient"), None),
            P(("dp", "orient")),
            P("dp", "orient", None),
            P(),
            P(),
            P(),
            P(),
        ),
        out_specs=(P(("dp", "orient")), P(None, ("dp", "orient")), P(None, "orient")),
        check_vma=False,
    )
```

profile of v0, /device:TPU:1, one launch (start us, length us, event | category | flops | bytes accessed | tf_op | source)
XLA Modules:
  0.0 960.9 jit_solution(2944390753565848813)
XLA Ops:
  8.0 1.6 fusion.37
  14.8 4.8 select_bitcast_fusion
  19.7 1.1 copy-done.1
  21.5 1.2 fusion
  24.9 11.1 %all-reduce = s32[512]{0:T(512)S(1)} all-reduce(s32[512]{0:T(512)S(1)} %dynamic-update-slice), channel_id=1, replica_groups=mesh['dp'=32,'orient'=8] {'orient'}, use_global_device_ids=true, to_apply=%add | all-reduce | flops 512 | bytes 4096
  36.7 299.8 %all-reduce.4.cloned.1.call-done = (bf16[64,8448]{1,0:T(8,128)(2,1)}, bf16[64,8448]{1,0:T(8,128)(2,1)}, bf16[64,8448]{1,0:T(8,128)(2,1)}, bf16[64,8448]{1,0:T(8,...) async-done(((bf16[64,8448]{1,0:T(8,128)(2,1)}, bf16[64,8448]{1,0:T(8,128)(2,1)}, ...) | async-done | bytes 8650768 | tf_op jit(solution)/shard_map/psum | solution.py:9
  336.5 1.8 convert_multiply_fusion.6
  338.3 1.2 fusion.23
  339.6 1.0 convolution_multiply_fusion.8
  340.6 1.2 fusion.21
  342.6 1.2 fusion.19
  344.9 1.2 fusion.17
  346.1 1.1 convolution_multiply_fusion.5
  347.5 1.2 fusion.15
  349.8 1.2 fusion.13
  351.0 1.1 convolution_multiply_fusion.3
  352.4 1.2 fusion.11
  354.6 1.5 fusion.9
  357.2 7.6 fusion.38
  364.8 25.1 %all-gather.16 = f32[8,1,512]{2,1,0:T(1,128)S(1)} all-gather(f32[1,1,512]{2,1,0:T(1,128)S(1)} %bitcast.283), channel_id=2, replica_groups=mesh['dp'=32,'orient'=8] {'orient'}, dimensions={0}, use_global_device_ids=true | all-gather | bytes 18432 | tf_op jit(solution)/shard_map/all_gather | solution.py:13
  390.5 25.1 %all-gather.17 = f32[8,1,512]{2,1,0:T(1,128)S(1)} all-gather(f32[1,1,512]{2,1,0:T(1,128)S(1)} %bitcast.290), channel_id=3, replica_groups=mesh['dp'=32,'orient'=8] {'orient'}, dimensions={0}, use_global_device_ids=true | all-gather | bytes 18432 | tf_op jit(solution)/shard_map/all_gather | solution.py:13
  416.2 3.4 fusion.39
  419.6 25.1 %all-gather.18 = f32[8,1,512]{2,1,0:T(1,128)S(1)} all-gather(f32[1,1,512]{2,1,0:T(1,128)S(1)} %bitcast.284), channel_id=4, replica_groups=mesh['dp'=32,'orient'=8] {'orient'}, dimensions={0}, use_global_device_ids=true | all-gather | bytes 18432 | tf_op jit(solution)/shard_map/all_gather | solution.py:13
  445.4 25.1 %all-gather.19 = f32[8,1,512]{2,1,0:T(1,128)S(1)} all-gather(f32[1,1,512]{2,1,0:T(1,128)S(1)} %bitcast.291), channel_id=5, replica_groups=mesh['dp'=32,'orient'=8] {'orient'}, dimensions={0}, use_global_device_ids=true | all-gather | bytes 18432 | tf_op jit(solution)/shard_map/all_gather | solution.py:13
  471.1 3.5 fusion.40
  474.6 25.1 %all-gather.20 = f32[8,1,512]{2,1,0:T(1,128)S(1)} all-gather(f32[1,1,512]{2,1,0:T(1,128)S(1)} %bitcast.285), channel_id=6, replica_groups=mesh['dp'=32,'orient'=8] {'orient'}, dimensions={0}, use_global_device_ids=true | all-gather | bytes 18432 | tf_op jit(solution)/shard_map/all_gather | solution.py:13
  500.3 25.1 %all-gather.21 = f32[8,1,512]{2,1,0:T(1,128)S(1)} all-gather(f32[1,1,512]{2,1,0:T(1,128)S(1)} %bitcast.292), channel_id=7, replica_groups=mesh['dp'=32,'orient'=8] {'orient'}, dimensions={0}, use_global_device_ids=true | all-gather | bytes 18432 | tf_op jit(solution)/shard_map/all_gather | solution.py:13
  526.0 3.4 fusion.41
  529.5 25.1 %all-gather.22 = f32[8,1,512]{2,1,0:T(1,128)S(1)} all-gather(f32[1,1,512]{2,1,0:T(1,128)S(1)} %bitcast.286), channel_id=8, replica_groups=mesh['dp'=32,'orient'=8] {'orient'}, dimensions={0}, use_global_device_ids=true | all-gather | bytes 18432 | tf_op jit(solution)/shard_map/all_gather | solution.py:13
  555.2 25.1 %all-gather.23 = f32[8,1,512]{2,1,0:T(1,128)S(1)} all-gather(f32[1,1,512]{2,1,0:T(1,128)S(1)} %bitcast.293), channel_id=9, replica_groups=mesh['dp'=32,'orient'=8] {'orient'}, dimensions={0}, use_global_device_ids=true | all-gather | bytes 18432 | tf_op jit(solution)/shard_map/all_gather | solution.py:13
  580.9 3.4 fusion.42
  584.3 25.1 %all-gather.24 = f32[8,1,512]{2,1,0:T(1,128)S(1)} all-gather(f32[1,1,512]{2,1,0:T(1,128)S(1)} %bitcast.287), channel_id=10, replica_groups=mesh['dp'=32,'orient'=8] {'orient'}, dimensions={0}, use_global_device_ids=true | all-gather | bytes 18432 | tf_op jit(solution)/shard_map/all_gather | solution.py:13
  609.4 25.1 %all-gather.25 = f32[8,1,512]{2,1,0:T(1,128)S(1)} all-gather(f32[1,1,512]{2,1,0:T(1,128)S(1)} %bitcast.294), channel_id=11, replica_groups=mesh['dp'=32,'orient'=8] {'orient'}, dimensions={0}, use_global_device_ids=true | all-gather | bytes 18432 | tf_op jit(solution)/shard_map/all_gather | solution.py:13
  635.1 3.4 fusion.43
  638.6 25.1 %all-gather.26 = f32[8,1,512]{2,1,0:T(1,128)S(1)} all-gather(f32[1,1,512]{2,1,0:T(1,128)S(1)} %bitcast.288), channel_id=12, replica_groups=mesh['dp'=32,'orient'=8] {'orient'}, dimensions={0}, use_global_device_ids=true | all-gather | bytes 18432 | tf_op jit(solution)/shard_map/all_gather | solution.py:13
  663.7 25.1 %all-gather.27 = f32[8,1,512]{2,1,0:T(1,128)S(1)} all-gather(f32[1,1,512]{2,1,0:T(1,128)S(1)} %bitcast.295), channel_id=13, replica_groups=mesh['dp'=32,'orient'=8] {'orient'}, dimensions={0}, use_global_device_ids=true | all-gather | bytes 18432 | tf_op jit(solution)/shard_map/all_gather | solution.py:13
  688.8 3.4 fusion.44
  692.1 25.1 %all-gather.28 = f32[8,1,512]{2,1,0:T(1,128)S(1)} all-gather(f32[1,1,512]{2,1,0:T(1,128)S(1)} %bitcast.289), channel_id=14, replica_groups=mesh['dp'=32,'orient'=8] {'orient'}, dimensions={0}, use_global_device_ids=true | all-gather | bytes 18432 | tf_op jit(solution)/shard_map/all_gather | solution.py:13
  717.3 25.3 %all-gather.29 = f32[8,1,512]{2,1,0:T(1,128)S(1)} all-gather(f32[1,1,512]{2,1,0:T(1,128)S(1)} %bitcast.296), channel_id=15, replica_groups=mesh['dp'=32,'orient'=8] {'orient'}, dimensions={0}, use_global_device_ids=true | all-gather | bytes 18432 | tf_op jit(solution)/shard_map/all_gather | solution.py:13
  742.6 3.4 fusion.45
  746.1 25.1 %all-gather.30 = f32[8,1,512]{2,1,0:T(1,128)S(1)} all-gather(f32[1,1,512]{2,1,0:T(1,128)S(1)} %bitcast.282), channel_id=16, replica_groups=mesh['dp'=32,'orient'=8] {'orient'}, dimensions={0}, use_global_device_ids=true | all-gather | bytes 18432 | tf_op jit(solution)/shard_map/all_gather | solution.py:13
  771.2 25.1 %all-gather.31 = f32[8,1,512]{2,1,0:T(1,128)S(1)} all-gather(f32[1,1,512]{2,1,0:T(1,128)S(1)} %bitcast.297), channel_id=17, replica_groups=mesh['dp'=32,'orient'=8] {'orient'}, dimensions={0}, use_global_device_ids=true | all-gather | bytes 18432 | tf_op jit(solution)/shard_map/all_gather | solution.py:13
  796.4 5.5 while.136
  801.8 5.5 while.137
  807.3 5.5 while.138
  812.8 5.5 while.139
  818.3 5.4 while.140
  826.2 126.6 %psum.71 = f32[8,64]{1,0:T(8,128)S(1)} all-reduce(f32[8,64]{1,0:T(8,128)S(1)} %exponential_reduce_fusion), channel_id=1, replica_groups=mesh['dp'=32,'orient'=8] {'dp'}, use_global_device_ids=true, to_apply=%region_43.44 | all-reduce | flops 512 | bytes 4096 | tf_op jit(solution)/shard_map/psum | solution.py:91
  (293 shorter events, 44.8 us)
Async XLA Ops:
  8.0 328.5 %all-reduce.4.cloned.1.call-start = ((), (), s32[]{:S(2)}) async-start(), calls=%async_computation.1 | async-start | bytes 17301504 | tf_op jit(solution)/shard_map/psum | solution.py:9
  19.6 337.5 %all-gather.34.cloned.1.call-start = ((), (), s32[]{:S(2)}) async-start(), calls=%async_computation | async-start | bytes 9732096 | tf_op jit(solution)/shard_map/all_gather | solution.py:61
  22.7 13.3 %copy-start.41 = (f32[8]{0:T(128)S(1)}, f32[8]{0:T(128)}, u32[]{:S(2)}) copy-start(f32[8]{0:T(128)} %param.29) | copy-start | bytes 100
  344.9 2.3 copy-start.4
  344.9 2.3 copy-start.6
  349.8 2.3 copy-start.3
  357.2 59.0 %copy-start = (bf16[512,8448]{1,0:T(8,128)(2,1)S(1)}, bf16[512,8448]{1,0:T(8,128)(2,1)}, u32[]{:S(2)}) copy-start(bf16[512,8448]{1,0:T(8,128)(2,1)} %all-gather.34.cloned.1.call-done) | copy-start | bytes 25952260
  357.2 59.0 %copy-start.12 = (bf16[64,8448]{1,0:T(8,128)(2,1)S(1)}, bf16[64,8448]{1,0:T(8,128)(2,1)}, u32[]{:S(2)}) copy-start(bf16[64,8448]{1,0:T(8,128)(2,1)} %get-tuple-element.1164) | copy-start | bytes 3244036
  389.8 29.8 %copy-start.39 = (f32[8,1,512]{2,1,0:T(1,128)}, f32[8,1,512]{2,1,0:T(1,128)S(1)}, u32[]{:S(2)}) copy-start(f32[8,1,512]{2,1,0:T(1,128)S(1)} %all-gather.16) | copy-start | bytes 49156
  415.6 4.1 copy-start.40
  416.2 54.9 %copy-start.11 = (bf16[64,8448]{1,0:T(8,128)(2,1)S(1)}, bf16[64,8448]{1,0:T(8,128)(2,1)}, u32[]{:S(2)}) copy-start(bf16[64,8448]{1,0:T(8,128)(2,1)} %get-tuple-element.1165) | copy-start | bytes 3244036
  416.2 54.9 %copy-start.26 = (f32[64,512]{1,0:T(8,128)S(1)}, f32[64,512]{1,0:T(8,128)}, u32[]{:S(2)}) copy-start(f32[64,512]{1,0:T(8,128)} %convolution_multiply_fusion.6) | copy-start | bytes 393220
  444.7 26.3 %copy-start.37 = (f32[8,1,512]{2,1,0:T(1,128)}, f32[8,1,512]{2,1,0:T(1,128)S(1)}, u32[]{:S(2)}) copy-start(f32[8,1,512]{2,1,0:T(1,128)S(1)} %all-gather.18) | copy-start | bytes 49156
  471.1 54.9 %copy-start.9 = (bf16[64,8448]{1,0:T(8,128)(2,1)S(1)}, bf16[64,8448]{1,0:T(8,128)(2,1)}, u32[]{:S(2)}) copy-start(bf16[64,8448]{1,0:T(8,128)(2,1)} %get-tuple-element.1166) | copy-start | bytes 3244036
  471.1 54.9 %copy-start.25 = (f32[64,512]{1,0:T(8,128)S(1)}, f32[64,512]{1,0:T(8,128)}, u32[]{:S(2)}) copy-start(f32[64,512]{1,0:T(8,128)} %convolution_multiply_fusion.5) | copy-start | bytes 393220
  499.6 26.3 %copy-start.35 = (f32[8,1,512]{2,1,0:T(1,128)}, f32[8,1,512]{2,1,0:T(1,128)S(1)}, u32[]{:S(2)}) copy-start(f32[8,1,512]{2,1,0:T(1,128)S(1)} %all-gather.20) | copy-start | bytes 49156
  526.0 54.9 %copy-start.7 = (bf16[64,8448]{1,0:T(8,128)(2,1)S(1)}, bf16[64,8448]{1,0:T(8,128)(2,1)}, u32[]{:S(2)}) copy-start(bf16[64,8448]{1,0:T(8,128)(2,1)} %get-tuple-element.1167) | copy-start | bytes 3244036
  526.0 54.9 %copy-start.24 = (f32[64,512]{1,0:T(8,128)S(1)}, f32[64,512]{1,0:T(8,128)}, u32[]{:S(2)}) copy-start(f32[64,512]{1,0:T(8,128)} %convolution_multiply_fusion.4) | copy-start | bytes 393220
  529.4 54.8 %copy-start.14 = (f32[64,512]{1,0:T(8,128)}, f32[64,512]{1,0:T(8,128)S(1)}, u32[]{:S(2)}) copy-start(f32[64,512]{1,0:T(8,128)S(1)} %get-tuple-element.1236) | copy-start | bytes 393220
  554.5 29.7 %copy-start.33 = (f32[8,1,512]{2,1,0:T(1,128)}, f32[8,1,512]{2,1,0:T(1,128)S(1)}, u32[]{:S(2)}) copy-start(f32[8,1,512]{2,1,0:T(1,128)S(1)} %all-gather.22) | copy-start | bytes 49156
  580.2 4.0 copy-start.34
  580.9 54.2 %copy-start.5 = (bf16[64,8448]{1,0:T(8,128)(2,1)S(1)}, bf16[64,8448]{1,0:T(8,128)(2,1)}, u32[]{:S(2)}) copy-start(bf16[64,8448]{1,0:T(8,128)(2,1)} %get-tuple-element.1168) | copy-start | bytes 3244036
  580.9 54.2 %copy-start.23 = (f32[64,512]{1,0:T(8,128)S(1)}, f32[64,512]{1,0:T(8,128)}, u32[]{:S(2)}) copy-start(f32[64,512]{1,0:T(8,128)} %convolution_multiply_fusion.3) | copy-start | bytes 393220
  584.3 54.2 %copy-start.16 = (f32[64,512]{1,0:T(8,128)}, f32[64,512]{1,0:T(8,128)S(1)}, u32[]{:S(2)}) copy-start(f32[64,512]{1,0:T(8,128)S(1)} %get-tuple-element.1238) | copy-start | bytes 393220
  609.4 29.2 %copy-start.31 = (f32[8,1,512]{2,1,0:T(1,128)}, f32[8,1,512]{2,1,0:T(1,128)S(1)}, u32[]{:S(2)}) copy-start(f32[8,1,512]{2,1,0:T(1,128)S(1)} %all-gather.24) | copy-start | bytes 49156
  634.5 4.1 copy-start.32
  635.1 53.6 %copy-start.22 = (f32[64,512]{1,0:T(8,128)S(1)}, f32[64,512]{1,0:T(8,128)}, u32[]{:S(2)}) copy-start(f32[64,512]{1,0:T(8,128)} %convolution_multiply_fusion.2) | copy-start | bytes 393220
  638.5 53.6 %copy-start.18 = (f32[64,512]{1,0:T(8,128)}, f32[64,512]{1,0:T(8,128)S(1)}, u32[]{:S(2)}) copy-start(f32[64,512]{1,0:T(8,128)S(1)} %get-tuple-element.1240) | copy-start | bytes 393220
  663.6 28.5 %copy-start.29 = (f32[8,1,512]{2,1,0:T(1,128)}, f32[8,1,512]{2,1,0:T(1,128)S(1)}, u32[]{:S(2)}) copy-start(f32[8,1,512]{2,1,0:T(1,128)S(1)} %all-gather.26) | copy-start | bytes 49156
  688.7 3.4 copy-start.30
  688.7 53.9 %copy-start.21 = (f32[64,512]{1,0:T(8,128)S(1)}, f32[64,512]{1,0:T(8,128)}, u32[]{:S(2)}) copy-start(f32[64,512]{1,0:T(8,128)} %convolution_multiply_fusion.1) | copy-start | bytes 393220
  717.2 28.8 %copy-start.27 = (f32[8,1,512]{2,1,0:T(1,128)}, f32[8,1,512]{2,1,0:T(1,128)S(1)}, u32[]{:S(2)}) copy-start(f32[8,1,512]{2,1,0:T(1,128)S(1)} %all-gather.28) | copy-start | bytes 49156
  742.6 3.4 copy-start.28
  742.6 53.7 %slice-start.12 = ((f32[8,1,512]{2,1,0:T(1,128)}), f32[1,1,512]{2,1,0:T(1,128)S(1)}, s32[]{:S(2)}) async-start(f32[8,1,512]{2,1,0:T(1,128)} %copy-done.39), calls=%async_computation.14 | async-start | bytes 4096 | tf_op jit(solution)/shard_map/slice | solution.py:14
  742.6 53.7 %slice-start.13 = ((f32[8,1,512]{2,1,0:T(1,128)}), f32[1,1,512]{2,1,0:T(1,128)S(1)}, s32[]{:S(2)}) async-start(f32[8,1,512]{2,1,0:T(1,128)} %copy-done.40), calls=%async_computation.15 | async-start | bytes 4096 | tf_op jit(solution)/shard_map/slice | solution.py:14
  742.6 59.2 %slice-start.10 = ((f32[8,1,512]{2,1,0:T(1,128)}), f32[1,1,512]{2,1,0:T(1,128)S(1)}, s32[]{:S(2)}) async-start(f32[8,1,512]{2,1,0:T(1,128)} %copy-done.37), calls=%async_computation.12 | async-start | bytes 4096 | tf_op jit(solution)/shard_map/slice | solution.py:14
  742.6 59.2 %slice-start.11 = ((f32[8,1,512]{2,1,0:T(1,128)}), f32[1,1,512]{2,1,0:T(1,128)S(1)}, s32[]{:S(2)}) async-start(f32[8,1,512]{2,1,0:T(1,128)} %copy-done.38), calls=%async_computation.13 | async-start | bytes 4096 | tf_op jit(solution)/shard_map/slice | solution.py:14
  746.0 61.3 %slice-start.8 = ((f32[8,1,512]{2,1,0:T(1,128)}), f32[1,1,512]{2,1,0:T(1,128)S(1)}, s32[]{:S(2)}) async-start(f32[8,1,512]{2,1,0:T(1,128)} %copy-done.35), calls=%async_computation.10 | async-start | bytes 4096 | tf_op jit(solution)/shard_map/slice | solution.py:14
  746.0 61.3 %slice-start.9 = ((f32[8,1,512]{2,1,0:T(1,128)}), f32[1,1,512]{2,1,0:T(1,128)S(1)}, s32[]{:S(2)}) async-start(f32[8,1,512]{2,1,0:T(1,128)} %copy-done.36), calls=%async_computation.11 | async-start | bytes 4096 | tf_op jit(solution)/shard_map/slice | solution.py:14
  746.0 66.7 %slice-start.6 = ((f32[8,1,512]{2,1,0:T(1,128)}), f32[1,1,512]{2,1,0:T(1,128)S(1)}, s32[]{:S(2)}) async-start(f32[8,1,512]{2,1,0:T(1,128)} %copy-done.33), calls=%async_computation.8 | async-start | bytes 4096 | tf_op jit(solution)/shard_map/slice | solution.py:14
  746.1 66.7 %slice-start.7 = ((f32[8,1,512]{2,1,0:T(1,128)}), f32[1,1,512]{2,1,0:T(1,128)S(1)}, s32[]{:S(2)}) async-start(f32[8,1,512]{2,1,0:T(1,128)} %copy-done.34), calls=%async_computation.9 | async-start | bytes 4096 | tf_op jit(solution)/shard_map/slice | solution.py:14
  746.1 72.2 %slice-start.4 = ((f32[8,1,512]{2,1,0:T(1,128)}), f32[1,1,512]{2,1,0:T(1,128)S(1)}, s32[]{:S(2)}) async-start(f32[8,1,512]{2,1,0:T(1,128)} %copy-done.31), calls=%async_computation.6 | async-start | bytes 4096 | tf_op jit(solution)/shard_map/slice | solution.py:14
  746.1 72.2 %slice-start.5 = ((f32[8,1,512]{2,1,0:T(1,128)}), f32[1,1,512]{2,1,0:T(1,128)S(1)}, s32[]{:S(2)}) async-start(f32[8,1,512]{2,1,0:T(1,128)} %copy-done.32), calls=%async_computation.7 | async-start | bytes 4096 | tf_op jit(solution)/shard_map/slice | solution.py:14
  771.2 52.5 %slice-start.2 = ((f32[8,1,512]{2,1,0:T(1,128)}), f32[1,1,512]{2,1,0:T(1,128)S(1)}, s32[]{:S(2)}) async-start(f32[8,1,512]{2,1,0:T(1,128)} %copy-done.29), calls=%async_computation.4 | async-start | bytes 4096 | tf_op jit(solution)/shard_map/slice | solution.py:14
  771.2 52.5 %slice-start.3 = ((f32[8,1,512]{2,1,0:T(1,128)}), f32[1,1,512]{2,1,0:T(1,128)S(1)}, s32[]{:S(2)}) async-start(f32[8,1,512]{2,1,0:T(1,128)} %copy-done.30), calls=%async_computation.5 | async-start | bytes 4096 | tf_op jit(solution)/shard_map/slice | solution.py:14
  796.3 27.8 %slice-start = ((f32[8,1,512]{2,1,0:T(1,128)}), f32[1,1,512]{2,1,0:T(1,128)S(1)}, s32[]{:S(2)}) async-start(f32[8,1,512]{2,1,0:T(1,128)} %copy-done.27), calls=%async_computation.2 | async-start | bytes 4096 | tf_op jit(solution)/shard_map/slice | solution.py:14
  796.3 27.8 %slice-start.1 = ((f32[8,1,512]{2,1,0:T(1,128)}), f32[1,1,512]{2,1,0:T(1,128)S(1)}, s32[]{:S(2)}) async-start(f32[8,1,512]{2,1,0:T(1,128)} %copy-done.28), calls=%async_computation.3 | async-start | bytes 4096 | tf_op jit(solution)/shard_map/slice | solution.py:14
  818.3 7.6 copy-start.15
  (13 other events, 18.3 us)
Sparse Core Ops, SparseCore 0:
  19.8 316.6 all-reduce.3
Sparse Core Ops, SparseCore 1:
  22.8 127.2 all-gather.33
where the time goes:
time: 967 us; the launch traced here: 961 us
  blocking collectives  539 us (56%)
  waiting for transfers between devices  300 us (31%)
  matrix products  50 us (5%)
  local copies, waits for them, and re-layouts  37.2 us (4%)
  between operations  22 us (2%)
  other arithmetic  11.7 us (1%)
    all_gather x16, blocking collectives, combined_all(): everything = jax.tree.map(lambda part: lax.all_gather(part, axis), array)  401 us
    psum x1, waiting for transfers between devices, broadcast(): return lax.psum(block, axis)  300 us
    psum x1, blocking collectives, per_device(): orientation_mass = lax.psum(mass_local, 'dp') * normalise  127 us
    dot_general x8, matrix products, per_device(): lax.dot_general(panel, whole_images, (((1,), (1,)), ((), ())), preferred_...  31.4 us
    dynamic_slice x56, local copies, waits for them, and re-layouts, turn(): return combine(so_far, jax.tree.map(lambda part: part[k], everything))  26.3 us
  transfers between devices with their start and end apart: 2, of which 1 were waited for; matrix products, arithmetic and copies ran while one was open for 2% of the time, Pallas kernels for 0%

commit v1 on v0

v1 whole, which is shorter than its diff:
```python
import functools
import jax
import jax.numpy as jnp
from jax import lax
from jax.experimental import pallas as pl
from jax.experimental.pallas import tpu as pltpu
from jax.sharding import PartitionSpec as P

NZ, NYLO, NCORE = 8, 2, 2
NDP, NOR = 32, 8
CLS, PIX, GRP, ORI, ROWS = 8, 4224, 64, 64, 64
FEAT = 2 * PIX
EXT = 256
COLS = FEAT + EXT
HALF = COLS // 2
QUART = COLS // 4
GROUP_ROWS = NOR * ROWS
HIGH = lax.Precision.HIGHEST
NT = (((1,), (1,)), ((), ()))
MIB = 1024 * 1024


def permute(array, move):
    pairs = []
    for dp in range(NDP):
        z, ylo, core = dp // 4, (dp // 2) % 2, dp % 2
        nz, nylo, ncore = move(z, ylo, core)
        target = (nz % NZ) * 4 + nylo * 2 + ncore
        for orient in range(NOR):
            pairs.append((dp * NOR + orient, target * NOR + orient))
    return lax.ppermute(array, ("dp", "orient"), pairs)


def other_core(array):
    return permute(array, lambda z, ylo, core: (z, ylo, 1 - core))


def other_ylo(array):
    return permute(array, lambda z, ylo, core: (z, 1 - ylo, core))


def from_below(array):
    return permute(array, lambda z, ylo, core: (z + 1, ylo, core))


def from_above(array):
    return permute(array, lambda z, ylo, core: (z - 1, ylo, core))


def vmem():
    return pl.BlockSpec(memory_space=pltpu.VMEM)


def smem():
    return pl.BlockSpec(memory_space=pltpu.SMEM)


def params(mib, **more):
    return pltpu.CompilerParams(vmem_limit_bytes=mib * MIB, **more)


def weigh_kernel(core_ref, images_ref, groups_ref, contrast_ref, noise_ref, out_ref):
    core = core_ref[0]
    hot = (
        groups_ref[...] == lax.broadcasted_iota(jnp.int32, (ROWS, GRP), 1)
    ).astype(jnp.float32)
    rows = jnp.dot(hot, contrast_ref[...], precision=HIGH, preferred_element_type=jnp.float32)
    factor = rows * noise_ref[...]
    real = (images_ref[:, :PIX].astype(jnp.float32) * factor).astype(jnp.bfloat16)
    imag = (images_ref[:, PIX:].astype(jnp.float32) * factor).astype(jnp.bfloat16)
    out_ref[core, :, :PIX] = real
    out_ref[core, :, PIX:] = imag[:, : HALF - PIX]
    out_ref[1 - core, :, : FEAT - HALF] = imag[:, HALF - PIX :]
    ext = jnp.concatenate([hot, hot, hot, jnp.zeros_like(hot)], axis=1)
    out_ref[1 - core, :, FEAT - HALF :] = ext.astype(jnp.bfloat16)


def weigh(core, images, groups, contrast, noise):
    return pl.pallas_call(
        weigh_kernel,
        out_shape=jax.ShapeDtypeStruct((2, ROWS, HALF), jnp.bfloat16),
        in_specs=[smem(), vmem(), vmem(), vmem(), vmem()],
        out_specs=vmem(),
        compiler_params=params(24),
        name="weigh",
    )(core, images, groups, contrast, noise)


def panel_kernel(prior_ref, slot_ref, contrast_ref, noise_ref, out_ref):
    contrast = contrast_ref[...]
    power = contrast * contrast * noise_ref[...]
    real = slot_ref[:, :PIX].astype(jnp.float32)
    imag = slot_ref[:, PIX:].astype(jnp.float32)
    table = lax.dot_general(
        real * real + imag * imag, power, NT, precision=HIGH, preferred_element_type=jnp.float32
    )
    table = -0.5 * table + prior_ref[0]
    first = table.astype(jnp.bfloat16).astype(jnp.float32)
    rest = table - first
    second = rest.astype(jnp.bfloat16).astype(jnp.float32)
    third = rest - second
    ext = jnp.concatenate([first, second, third, jnp.zeros_like(first)], axis=1)
    for z in range(NZ):
        rows = slice(8 * z, 8 * z + 8)
        for ylo in range(NYLO):
            parts = []
            for core in range(NCORE):
                start = core * HALF + ylo * QUART
                stop = start + QUART
                if stop <= FEAT:
                    part = slot_ref[:, start:stop].astype(jnp.float32)[rows]
                else:
                    part = jnp.concatenate(
                        [slot_ref[:, start:FEAT].astype(jnp.float32)[rows], ext[rows]], axis=1
                    )
                parts.append(part)
            at = (z * 4 + ylo * 2) * 8
            out_ref[at : at + 16, :] = jnp.concatenate(parts, axis=0).astype(jnp.bfloat16)


def panel(prior, slot, contrast, noise):
    return pl.pallas_call(
        panel_kernel,
        out_shape=jax.ShapeDtypeStruct((NDP * 8, QUART), jnp.bfloat16),
        in_specs=[smem(), vmem(), vmem(), vmem()],
        out_specs=vmem(),
        compiler_params=params(24),
        name="panel",
    )(prior, slot, contrast, noise)


def scores_kernel(panel_ref, images_ref, out_ref):
    part = lax.dot_general(
        panel_ref[...].reshape(NZ * CLS * 8, QUART),
        images_ref[...].reshape(GROUP_ROWS, QUART),
        NT,
        preferred_element_type=jnp.float32,
    )

    @pl.when(pl.program_id(0) == 0)
    def _():
        out_ref[...] = part

    @pl.when(pl.program_id(0) != 0)
    def _():
        out_ref[...] += part


def scores_of(panels, images, which):
    rows = NZ * CLS * 8
    return pl.pallas_call(
        scores_kernel,
        grid=(NYLO,),
        out_shape=jax.ShapeDtypeStruct((rows, GROUP_ROWS), jnp.float32),
        in_specs=[
            pl.BlockSpec((NZ, 1, CLS * 8, QUART), lambda y: (0, y, 0, 0)),
            pl.BlockSpec((NOR, 1, ROWS, QUART), lambda y: (0, which, 0, y)),
        ],
        out_specs=pl.BlockSpec((rows, GROUP_ROWS), lambda y: (0, 0)),
        compiler_params=params(32),
        cost_estimate=pl.CostEstimate(
            flops=2 * rows * GROUP_ROWS * HALF, bytes_accessed=10 * MIB, transcendentals=0
        ),
        name="scores",
    )(panels, images)


def norms_kernel(mine_ref, other_ref, scores_ref, lse_ref):
    scores = mine_ref[...] + other_ref[...]
    scores_ref[...] = scores
    scores = scores.reshape(NZ, CLS, 8, GROUP_ROWS)
    maximum = jnp.max(jnp.max(scores, axis=0), axis=1, keepdims=True)
    totals = jnp.sum(jnp.sum(jnp.exp(scores - maximum[None]), axis=0), axis=1)
    lse_ref[...] = maximum[:, 0, :] + jnp.log(totals)


def norms(mine, other):
    return pl.pallas_call(
        norms_kernel,
        out_shape=(
            jax.ShapeDtypeStruct(mine.shape, jnp.float32),
            jax.ShapeDtypeStruct((CLS, GROUP_ROWS), jnp.float32),
        ),
        in_specs=[vmem(), vmem()],
        out_specs=(vmem(), vmem()),
        compiler_params=params(24),
        name="norms",
    )(mine, other)


def finish_kernel(shift_ref, parts_ref, scores_ref, evidence_ref, posterior_ref, mass_ref):
    parts = parts_ref[...]
    maximum = jnp.max(parts, axis=0)
    class_lse = maximum + jnp.log(jnp.sum(jnp.exp(parts - maximum[None]), axis=0))
    top = jnp.max(class_lse, axis=0, keepdims=True)
    evidence = top + jnp.log(jnp.sum(jnp.exp(class_lse - top), axis=0, keepdims=True))
    evidence_ref[...] = evidence
    posterior_ref[...] = jnp.exp(class_lse - evidence)
    terms = jnp.exp(scores_ref[...] - evidence)
    ones = jnp.ones((8, GROUP_ROWS), jnp.float32)
    mass = lax.dot_general(ones, terms, NT, precision=HIGH, preferred_element_type=jnp.float32)
    mass_ref[...] = pltpu.roll(mass, shift_ref[0], 1)


def finish(shift, parts, scores):
    return pl.pallas_call(
        finish_kernel,
        out_shape=(
            jax.ShapeDtypeStruct((1, GROUP_ROWS), jnp.float32),
            jax.ShapeDtypeStruct((CLS, GROUP_ROWS), jnp.float32),
            jax.ShapeDtypeStruct((8, scores.shape[0]), jnp.float32),
        ),
        in_specs=[smem(), vmem(), vmem()],
        out_specs=(vmem(), vmem(), vmem()),
        compiler_params=params(24),
        name="finish",
    )(shift, parts, scores)


def per_device(images, groups, panel_slots, owners, contrast, noise_weight, class_prior):
    dp = lax.axis_index("dp")
    orient = lax.axis_index("orient")
    core = dp % 2
    ylo = (dp // 2) % 2
    z = dp // 4
    noise = noise_weight.reshape(1, PIX)
    weighted = weigh(core.reshape(1), images, groups.reshape(ROWS, 1), contrast, noise)
    group = jnp.concatenate([weighted[0], other_core(weighted[1])], axis=0)
    whole = lax.all_gather(group, "orient", axis=0).reshape(NOR, 2, ROWS, HALF)

    prior = jnp.sum(jnp.where(owners == dp, class_prior, 0.0)).reshape(1)
    sent = panel(prior, panel_slots[0], contrast, noise).reshape(NDP, 8, QUART)
    got = lax.all_to_all(sent, "dp", 0, 0)
    mine = jnp.concatenate(
        [lax.dynamic_slice_in_dim(got, owners[k], 1, 0) for k in range(CLS)], axis=0
    )
    theirs = other_ylo(mine)
    first = jnp.where(ylo == 0, mine, theirs)
    second = jnp.where(ylo == 0, theirs, mine)
    block = jnp.stack([first, second]).reshape(NYLO, CLS * 8, QUART)
    up = down = block
    blocks = {0: block}
    for step in (1, 2, 3):
        up, down = from_below(up), from_above(down)
        blocks[NZ - step], blocks[step] = up, down
    blocks[NZ // 2] = jnp.concatenate([from_below(up[:1]), from_above(down[1:])], axis=0)
    panels = jnp.stack([blocks[k] for k in range(NZ)])

    received = other_core(scores_of(panels, whole, 1))
    scores, partial = norms(scores_of(panels, whole, 0), received)
    parts = lax.all_to_all(
        jnp.broadcast_to(partial[None], (NOR, CLS, GROUP_ROWS)), "orient", 0, 0
    )
    evidence, posterior, mass = finish((z * (CLS * 8)).reshape(1), parts, scores)
    masses = lax.all_to_all(jnp.broadcast_to(mass[:1], (NDP, NZ * CLS * 8)), "dp", 0, 0)
    normalise = CLS * ORI * NOR / (ROWS * NOR * NDP)
    total = jnp.sum(masses, axis=0) * normalise
    orientation_mass = total.reshape(NZ, CLS, 8).transpose(1, 0, 2).reshape(CLS, ORI)
    log_evidence = lax.dynamic_slice_in_dim(evidence[0], orient * ROWS, ROWS, 0)
    class_posterior = lax.dynamic_slice_in_dim(posterior, orient * ROWS, ROWS, 1)
    return (log_evidence, class_posterior, orientation_mass)


def solution(mesh):
    return jax.shard_map(
        per_device,
        mesh=mesh,
        in_specs=(
            P(("dp", "orient"), None),
            P(("dp", "orient")),
            P("dp", "orient", None),
            P(),
            P(),
            P(),
            P(),
        ),
        out_specs=(P(("dp", "orient")), P(None, ("dp", "orient")), P(None, "orient")),
        check_vma=False,
    )
```

time: 967 us -> 200 us (0.21)
  blocking collectives: 539 us -> 0 us
  waiting for transfers between devices: 300 us -> 99.8 us
  matrix products: 50 us -> 0 us
  starting transfers between devices: 0.08 us -> 38.9 us
  local copies, waits for them, and re-layouts: 37.2 us -> 16.6 us
  Pallas kernels: 0 us -> 12.7 us
  other arithmetic: 11.7 us -> 1.97 us
    all_gather x16 -> x0, blocking collectives: 401 us -> none  [combined_all(): everything = jax.tree.map(lambda part: lax.all_gather(part, axis), array)]
    psum x1 -> x0, waiting for transfers between devices: 300 us -> none  [broadcast(): return lax.psum(block, axis)]
    psum x1 -> x0, blocking collectives: 127 us -> none  [per_device(): orientation_mass = lax.psum(mass_local, 'dp') * normalise]
    dot_general x25 -> x0, matrix products: 50 us -> none  [the longest x8 31.4 us: per_device(): lax.dot_general(panel, whole_images, (((1,), (1,)), ((), ())), preferred_...]
    ppermute x0 -> x11, waiting for transfers between devices: none -> 44.3 us  [permute(): return lax.ppermute(array, ('dp', 'orient'), pairs)]
    all_gather x1, waiting for transfers between devices: 0.01 us -> 27.7 us  [per_device(): whole = lax.all_gather(group, 'orient', axis=0).reshape(NOR, 2, ROWS, HALF)]
    all_to_all x0 -> x3, waiting for transfers between devices: none -> 27.7 us  [the longest x1 14 us: per_device(): got = lax.all_to_all(sent, 'dp', 0, 0)]
    dynamic_slice x57 -> x2, local copies, waits for them, and re-layouts: 26.3 us -> 1.25 us  [the longest x1 0.66 us: per_device(): lax.dynamic_slice_in_dim(posterior, orient * ROWS, ROWS, 1)]
  transfers between devices with their start and end apart: 2 -> 15, of which waited for: 1 -> 11; matrix products, arithmetic and copies ran while one was open for 2% -> 2% of each run, Pallas kernels for 0% -> 3%
where the time goes in v1:
time: 200 us; the launch traced here: 199 us
  waiting for transfers between devices  99.8 us (50%)
  starting transfers between devices  38.9 us (19%)
  between operations  29.2 us (15%)
  local copies, waits for them, and re-layouts  16.6 us (8%)
  Pallas kernels  12.7 us (6%)
    ppermute x11, waiting for transfers between devices, permute(): return lax.ppermute(array, ('dp', 'orient'), pairs)  44.3 us
    all_gather x1, waiting for transfers between devices, per_device(): whole = lax.all_gather(group, 'orient', axis=0).reshape(NOR, 2, ROWS, HALF)  27.7 us
    ppermute x11, starting transfers between devices, permute(): return lax.ppermute(array, ('dp', 'orient'), pairs)  18.4 us
    all_to_all x1, waiting for transfers between devices, per_device(): got = lax.all_to_all(sent, 'dp', 0, 0)  14 us
    unnamed x30, local copies, waits for them, and re-layouts  10.8 us
    all_to_all x1, starting transfers between devices, per_device(): lax.all_to_all(jnp.broadcast_to(mass[:1], (NDP, NZ * CLS * 8)), 'dp', 0, 0)  8.87 us
    all_to_all x1, starting transfers between devices, per_device(): got = lax.all_to_all(sent, 'dp', 0, 0)  8.26 us
    pallas_call x2, Pallas kernels, scores_of(): pl.pallas_call(scores_kernel, grid=(NYLO,), out_shape=jax.ShapeDtypeStruc...  7.29 us
  transfers between devices with their start and end apart: 15, of which 11 were waited for; matrix products, arithmetic and copies ran while one was open for 2% of the time, Pallas kernels for 3%

profile of v1, /device:TPU:1, one launch (start us, length us, event | category | flops | bytes accessed | tf_op | source)
XLA Modules:
  0.0 199.1 jit_solution(314418571054325996)
XLA Ops:
  7.2 0.7 reshape.53.noise_ref
  8.0 0.7 copy.16.groups_ref
  8.7 1.2 copy-done.3
  9.9 1.2 copy-done.5
  11.2 1.1 weigh.1
  12.3 0.1 slice_bitcast_fusion.1
  12.5 3.3 %collective-permute-start.9 = (bf16[64,4352]{1,0:T(8,128)(2,1)S(1)}, bf16[64,4352]{1,0:T(8,128)(2,1)S(1)}, u32[]{:S(2)}, u32[]{:S(2)}) collective-permute-start(bf16[64,4352]{1,0:T(8,128)(2,1)S(1)} %get-tuple-element.14), channel_id=1, source_target_pairs={{0,8},{1,9},{2,10},{3,11},{4,12},{5,13},{6,14},{7,15},{8,0},{9,1},... | collective-permute-start | bytes 1671176 | tf_op jit(solution)/shard_map/ppermute | solution.py:31
  15.8 1.6 collective-permute-done.9
  17.4 1.1 pad_maximum_fusion
  18.5 0.6 fusion.5
  19.1 2.8 %panel.1 = bf16[256,2176]{1,0:T(8,128)(2,1)} custom-call(f32[1]{0:T(128)} %bitcast.1.prior_ref, bf16[64,8448]{1,0:T(8,128)(2,1)S(1)} %bitcast.49, f32[64,4224]{1,0:T(8,128)S(1)} %copy-done.4, f32[1,4224]{1,0:T(1,128)S(1)} %reshape.53.noise_ref), custom_call_target="tpu_custom_call" | custom-call | tf_op jit(solution)/shard_map/panel/pallas_call | solution.py:122
  21.9 8.3 %all-to-all-start = ((bf16[32,8,2176]{2,1,0:T(8,128)(2,1)}), bf16[32,8,2176]{2,1,0:T(8,128)(2,1)S(1)}, u32[]{:S(2)}, u32[]{:S(2)}) async-start(bf16[32,8,2176]{2,1,0:T(8,128)(2,1)} %bitcast.3), calls=%async_computation | async-start | bytes 2228224 | tf_op jit(solution)/shard_map/all_to_all | solution.py:233
  30.2 0.7 fusion.7
  45.7 14.0 %all-to-all-done = bf16[32,8,2176]{2,1,0:T(8,128)(2,1)S(1)} async-done(((bf16[32,8,2176]{2,1,0:T(8,128)(2,1)}), bf16[32,8,2176]{2,1,0:T(8,128)(2,1)S(1)}, u32[]{:S(2)}, u32[]{:S(2)}) %all-to-all-start) | async-done | bytes 1114144 | tf_op jit(solution)/shard_map/all_to_all | solution.py:233
  59.8 1.5 collective-permute-start
  61.4 5.6 %collective-permute-done = bf16[8,8,2176]{2,1,0:T(8,128)(2,1)S(1)} collective-permute-done((bf16[8,8,2176]{2,1,0:T(8,128)(2,1)S(1)}, bf16[8,8,2176]{2,1,0:T(8,128)(2,1)S(1)}, u32[]{:S(2)}, u32[]{:S(2)}) %collective-permute-start) | collective-permute-done | bytes 278560 | tf_op jit(solution)/shard_map/ppermute | solution.py:31
  67.0 0.1 fusion.1
  67.1 1.1 collective-permute-start.1
  68.2 0.5 collective-permute-start.4
  68.7 10.6 %collective-permute-done.1 = bf16[2,64,2176]{2,1,0:T(8,128)(2,1)S(1)} collective-permute-done((bf16[2,64,2176]{2,1,0:T(8,128)(2,1)S(1)}, bf16[2,64,2176]{2,1,0:T(8,128)(2,1)S(1)}, u32[]{:S(2)}, u32[]{:S(2)}) %collective-permute-start.1) | collective-permute-done | bytes 557088 | tf_op jit(solution)/shard_map/ppermute | solution.py:31
  79.4 3.4 %collective-permute-start.2 = (bf16[2,64,2176]{2,1,0:T(8,128)(2,1)S(1)}, bf16[2,64,2176]{2,1,0:T(8,128)(2,1)S(1)}, u32[]{:S(2)}, u32[]{:S(2)}) collective-permute-start(bf16[2,64,2176]{2,1,0:T(8,128)(2,1)S(1)} %collective-permute-done.1), channel_id=1, source_target_pairs={{0,224},{1,225},{2,226},{3,227},{4,228},{5,229},{6,230},{7,231},{8... | collective-permute-start | bytes 1671176 | tf_op jit(solution)/shard_map/ppermute | solution.py:31
  82.8 10.2 %collective-permute-done.2 = bf16[2,64,2176]{2,1,0:T(8,128)(2,1)S(1)} collective-permute-done((bf16[2,64,2176]{2,1,0:T(8,128)(2,1)S(1)}, bf16[2,64,2176]{2,1,0:T(8,128)(2,1)S(1)}, u32[]{:S(2)}, u32[]{:S(2)}) %collective-permute-start.2) | collective-permute-done | bytes 557088 | tf_op jit(solution)/shard_map/ppermute | solution.py:31
  93.0 3.5 %collective-permute-start.3 = (bf16[2,64,2176]{2,1,0:T(8,128)(2,1)S(1)}, bf16[2,64,2176]{2,1,0:T(8,128)(2,1)S(1)}, u32[]{:S(2)}, u32[]{:S(2)}) collective-permute-start(bf16[2,64,2176]{2,1,0:T(8,128)(2,1)S(1)} %collective-permute-done.2), channel_id=1, source_target_pairs={{0,224},{1,225},{2,226},{3,227},{4,228},{5,229},{6,230},{7,231},{8... | collective-permute-start | bytes 1671176 | tf_op jit(solution)/shard_map/ppermute | solution.py:31
  96.6 9.4 %collective-permute-done.3 = bf16[2,64,2176]{2,1,0:T(8,128)(2,1)S(1)} collective-permute-done((bf16[2,64,2176]{2,1,0:T(8,128)(2,1)S(1)}, bf16[2,64,2176]{2,1,0:T(8,128)(2,1)S(1)}, u32[]{:S(2)}, u32[]{:S(2)}) %collective-permute-start.3) | collective-permute-done | bytes 557088 | tf_op jit(solution)/shard_map/ppermute | solution.py:31
  106.0 3.6 %collective-permute-start.8 = (bf16[1,64,2176]{2,1,0:T(8,128)(2,1)S(1)}, bf16[1,64,2176]{2,1,0:T(8,128)(2,1)S(1)}, u32[]{:S(2)}, u32[]{:S(2)}) collective-permute-start(bf16[1,64,2176]{2,1,0:T(8,128)(2,1)S(1)} %slice.56), channel_id=1, source_target_pairs={{0,224},{1,225},{2,226},{3,227},{4,228},{5,229},{6,230},{7,231},{8... | collective-permute-start | bytes 835592 | tf_op jit(solution)/shard_map/ppermute | solution.py:31
  109.6 0.3 collective-permute-start.7
  109.9 3.1 %collective-permute-done.8 = bf16[1,64,2176]{2,1,0:T(8,128)(2,1)S(1)} collective-permute-done((bf16[1,64,2176]{2,1,0:T(8,128)(2,1)S(1)}, bf16[1,64,2176]{2,1,0:T(8,128)(2,1)S(1)}, u32[]{:S(2)}, u32[]{:S(2)}) %collective-permute-start.8) | collective-permute-done | bytes 278560 | tf_op jit(solution)/shard_map/ppermute | solution.py:31
  113.1 3.8 %collective-permute-done.7 = bf16[1,64,2176]{2,1,0:T(8,128)(2,1)S(1)} collective-permute-done((bf16[1,64,2176]{2,1,0:T(8,128)(2,1)S(1)}, bf16[1,64,2176]{2,1,0:T(8,128)(2,1)S(1)}, u32[]{:S(2)}, u32[]{:S(2)}) %collective-permute-start.7) | collective-permute-done | bytes 278560 | tf_op jit(solution)/shard_map/ppermute | solution.py:31
  117.1 2.2 %copy-done.1 = bf16[8,2,64,2176]{3,2,1,0:T(8,128)(2,1)} copy-done((bf16[8,2,64,2176]{3,2,1,0:T(8,128)(2,1)}, bf16[8,2,64,2176]{3,2,1,0:T(8,128)(2,1)S(1)}, u32[]{:S(2)}) %copy-start.1) | copy-done | bytes 4456472
  119.3 27.7 %all-gather.3.cloned.1.call-done = bf16[1024,4352]{1,0:T(8,128)(2,1)} async-done(((bf16[128,4352]{1,0:T(8,128)(2,1)}), bf16[1024,4352]{1,0:T(8,128)(2,1)}) %all-gather.3.cloned.1.call-update) | async-done | bytes 8912912 | tf_op jit(solution)/shard_map/all_gather | solution.py:229
  147.1 3.5 %copy-done = bf16[1024,4352]{1,0:T(8,128)(2,1)S(1)} copy-done((bf16[1024,4352]{1,0:T(8,128)(2,1)S(1)}, bf16[1024,4352]{1,0:T(8,128)(2,1)}, u32[]{:S(2)}) %copy-start) | copy-done | bytes 8912920
  150.6 2.3 %copy-done.2 = bf16[8,2,64,2176]{3,2,1,0:T(8,128)(2,1)S(1)} copy-done((bf16[8,2,64,2176]{3,2,1,0:T(8,128)(2,1)S(1)}, bf16[8,2,64,2176]{3,2,1,0:T(8,128)(2,1)}, u32[]{:S(2)}) %copy-start.2) | copy-done | bytes 4456472
  152.8 3.6 %scores.3 = f32[512,512]{1,0:T(8,128)S(1)} custom-call(bf16[8,2,64,2176]{3,2,1,0:T(8,128)(2,1)S(1)} %copy-done.2, bf16[8,2,64,4352]{3,2,1,0:T(8,128)(2,1)S(1)} %bitcast.47), custom_call_target="tpu_custom_call" | custom-call | flops 2281701376 | bytes 10485760 | tf_op jit(solution)/shard_map/scores/pallas_call | solution.py:151
  156.5 1.2 collective-permute-start.10
  157.7 3.6 %scores.2.mine_ref = f32[512,512]{1,0:T(8,128)S(1)} custom-call(bf16[8,2,64,2176]{3,2,1,0:T(8,128)(2,1)S(1)} %copy-done.2, bf16[8,2,64,4352]{3,2,1,0:T(8,128)(2,1)S(1)} %bitcast.48), custom_call_target="tpu_custom_call" | custom-call | flops 2281701376 | bytes 10485760 | tf_op jit(solution)/shard_map/scores/pallas_call | solution.py:151
  161.3 0.4 norms.1
  161.7 0.7 broadcast_in_dim.16
  162.4 3.4 %all-to-all-start.1 = ((f32[8,8,512]{2,1,0:T(8,128)}), f32[8,8,512]{2,1,0:T(8,128)S(1)}, u32[]{:S(2)}, u32[]{:S(2)}) async-start(f32[8,8,512]{2,1,0:T(8,128)} %broadcast_in_dim.16), calls=%async_computation.1 | async-start | bytes 262144 | tf_op jit(solution)/shard_map/all_to_all | solution.py:251
  165.8 6.7 %all-to-all-done.1.parts_ref = f32[8,8,512]{2,1,0:T(8,128)S(1)} async-done(((f32[8,8,512]{2,1,0:T(8,128)}), f32[8,8,512]{2,1,0:T(8,128)S(1)}, u32[]{:S(2)}, u32[]{:S(2)}) %all-to-all-start.1) | async-done | bytes 131104 | tf_op jit(solution)/shard_map/all_to_all | solution.py:251
  172.4 1.1 finish.1
  173.5 0.7 broadcast_in_dim.17
  174.2 8.9 %all-to-all-start.2 = ((f32[32,1,512]{2,1,0:T(1,128)}), f32[32,1,512]{2,1,0:T(1,128)S(1)}, u32[]{:S(2)}, u32[]{:S(2)}) async-start(f32[32,1,512]{2,1,0:T(1,128)} %broadcast_in_dim.17), calls=%async_computation.2 | async-start | bytes 131072 | tf_op jit(solution)/shard_map/all_to_all | solution.py:255
  183.1 0.6 fusion.6
  183.7 0.7 constant_dynamic-slice_fusion
  184.3 7.1 %all-to-all-done.2 = f32[32,1,512]{2,1,0:T(1,128)S(1)} async-done(((f32[32,1,512]{2,1,0:T(1,128)}), f32[32,1,512]{2,1,0:T(1,128)S(1)}, u32[]{:S(2)}, u32[]{:S(2)}) %all-to-all-start.2) | async-done | bytes 65568 | tf_op jit(solution)/shard_map/all_to_all | solution.py:255
  191.4 0.1 reduce_sum.19
  191.5 0.1 mul.21
  191.6 0.7 reshape.58
  (43 shorter events, 0.8 us)
Async XLA Ops:
  7.2 139.9 %all-gather.3.cloned.1.call-start = ((), (), s32[]{:S(2)}) async-start(), calls=%async_computation.3 | async-start | bytes 10027008 | tf_op jit(solution)/shard_map/all_gather | solution.py:229
  8.7 1.2 copy-start.3
  9.9 1.2 copy-start.5
  12.4 6.1 %copy-start.7 = (s32[8]{0:T(128)S(1)}, s32[8]{0:T(128)}, u32[]{:S(2)}) copy-start(s32[8]{0:T(128)} %param.10) | copy-start | bytes 100
  12.4 6.0 %copy-start.8 = (f32[8]{0:T(128)S(1)}, f32[8]{0:T(128)}, u32[]{:S(2)}) copy-start(f32[8]{0:T(128)} %param.13) | copy-start | bytes 100
  12.4 6.6 %copy-start.4 = (f32[64,4224]{1,0:T(8,128)S(1)}, f32[64,4224]{1,0:T(8,128)}, u32[]{:S(2)}) copy-start(f32[64,4224]{1,0:T(8,128)} %contrast_ref.3) | copy-start | bytes 3244036
  12.5 6.6 %copy-start.6 = (bf16[1,64,8448]{2,1,0:T(8,128)(2,1)S(1)}, bf16[1,64,8448]{2,1,0:T(8,128)(2,1)}, u32[]{:S(2)}) copy-start(bf16[1,64,8448]{2,1,0:T(8,128)(2,1)} %param.9) | copy-start | bytes 3244036
  12.5 4.9 %collective-permute-start.9 = (bf16[64,4352]{1,0:T(8,128)(2,1)S(1)}, bf16[64,4352]{1,0:T(8,128)(2,1)S(1)}, u32[]{:S(2)}, u32[]{:S(2)}) collective-permute-start(bf16[64,4352]{1,0:T(8,128)(2,1)S(1)} %get-tuple-element.14), channel_id=1, source_target_pairs={{0,8},{1,9},{2,10},{3,11},{4,12},{5,13},{6,14},{7,15},{8,0},{9,1},... | collective-permute-start | bytes 1671176 | tf_op jit(solution)/shard_map/ppermute | solution.py:31
  21.9 37.8 %all-to-all-start = ((bf16[32,8,2176]{2,1,0:T(8,128)(2,1)}), bf16[32,8,2176]{2,1,0:T(8,128)(2,1)S(1)}, u32[]{:S(2)}, u32[]{:S(2)}) async-start(bf16[32,8,2176]{2,1,0:T(8,128)(2,1)} %bitcast.3), calls=%async_computation | async-start | bytes 2228224 | tf_op jit(solution)/shard_map/all_to_all | solution.py:233
  59.8 7.1 %collective-permute-start = (bf16[8,8,2176]{2,1,0:T(8,128)(2,1)S(1)}, bf16[8,8,2176]{2,1,0:T(8,128)(2,1)S(1)}, u32[]{:S(2)}, u32[]{:S(2)}) collective-permute-start(bf16[8,8,2176]{2,1,0:T(8,128)(2,1)S(1)} %constant_dynamic-update-slice_fusion), channel_id=1, source_target_pairs={{0,16},{1,17},{2,18},{3,19},{4,20},{5,21},{6,22},{7,23},{8,24},{9,... | collective-permute-start | bytes 835592 | tf_op jit(solution)/shard_map/ppermute | solution.py:31
  67.1 12.2 %collective-permute-start.1 = (bf16[2,64,2176]{2,1,0:T(8,128)(2,1)S(1)}, bf16[2,64,2176]{2,1,0:T(8,128)(2,1)S(1)}, u32[]{:S(2)}, u32[]{:S(2)}) collective-permute-start(bf16[2,64,2176]{2,1,0:T(8,128)(2,1)S(1)} %pad_maximum_fusion.1), channel_id=1, source_target_pairs={{0,224},{1,225},{2,226},{3,227},{4,228},{5,229},{6,230},{7,231},{8... | collective-permute-start | bytes 1671176 | tf_op jit(solution)/shard_map/ppermute | solution.py:31
  68.2 14.6 %collective-permute-start.4 = (bf16[2,64,2176]{2,1,0:T(8,128)(2,1)S(1)}, bf16[2,64,2176]{2,1,0:T(8,128)(2,1)S(1)}, u32[]{:S(2)}, u32[]{:S(2)}) collective-permute-start(bf16[2,64,2176]{2,1,0:T(8,128)(2,1)S(1)} %pad_maximum_fusion.1), channel_id=1, source_target_pairs={{0,32},{1,33},{2,34},{3,35},{4,36},{5,37},{6,38},{7,39},{8,40},{9,... | collective-permute-start | bytes 1671176 | tf_op jit(solution)/shard_map/ppermute | solution.py:31
  79.4 13.7 %collective-permute-start.2 = (bf16[2,64,2176]{2,1,0:T(8,128)(2,1)S(1)}, bf16[2,64,2176]{2,1,0:T(8,128)(2,1)S(1)}, u32[]{:S(2)}, u32[]{:S(2)}) collective-permute-start(bf16[2,64,2176]{2,1,0:T(8,128)(2,1)S(1)} %collective-permute-done.1), channel_id=1, source_target_pairs={{0,224},{1,225},{2,226},{3,227},{4,228},{5,229},{6,230},{7,231},{8... | collective-permute-start | bytes 1671176 | tf_op jit(solution)/shard_map/ppermute | solution.py:31
  82.8 13.8 %collective-permute-start.5 = (bf16[2,64,2176]{2,1,0:T(8,128)(2,1)S(1)}, bf16[2,64,2176]{2,1,0:T(8,128)(2,1)S(1)}, u32[]{:S(2)}, u32[]{:S(2)}) collective-permute-start(bf16[2,64,2176]{2,1,0:T(8,128)(2,1)S(1)} %collective-permute-done.4), channel_id=1, source_target_pairs={{0,32},{1,33},{2,34},{3,35},{4,36},{5,37},{6,38},{7,39},{8,40},{9,... | collective-permute-start | bytes 1671176 | tf_op jit(solution)/shard_map/ppermute | solution.py:31
  93.0 12.9 %collective-permute-start.3 = (bf16[2,64,2176]{2,1,0:T(8,128)(2,1)S(1)}, bf16[2,64,2176]{2,1,0:T(8,128)(2,1)S(1)}, u32[]{:S(2)}, u32[]{:S(2)}) collective-permute-start(bf16[2,64,2176]{2,1,0:T(8,128)(2,1)S(1)} %collective-permute-done.2), channel_id=1, source_target_pairs={{0,224},{1,225},{2,226},{3,227},{4,228},{5,229},{6,230},{7,231},{8... | collective-permute-start | bytes 1671176 | tf_op jit(solution)/shard_map/ppermute | solution.py:31
  96.5 13.1 %collective-permute-start.6 = (bf16[2,64,2176]{2,1,0:T(8,128)(2,1)S(1)}, bf16[2,64,2176]{2,1,0:T(8,128)(2,1)S(1)}, u32[]{:S(2)}, u32[]{:S(2)}) collective-permute-start(bf16[2,64,2176]{2,1,0:T(8,128)(2,1)S(1)} %collective-permute-done.5), channel_id=1, source_target_pairs={{0,32},{1,33},{2,34},{3,35},{4,36},{5,37},{6,38},{7,39},{8,40},{9,... | collective-permute-start | bytes 1671176 | tf_op jit(solution)/shard_map/ppermute | solution.py:31
  106.0 7.1 %collective-permute-start.8 = (bf16[1,64,2176]{2,1,0:T(8,128)(2,1)S(1)}, bf16[1,64,2176]{2,1,0:T(8,128)(2,1)S(1)}, u32[]{:S(2)}, u32[]{:S(2)}) collective-permute-start(bf16[1,64,2176]{2,1,0:T(8,128)(2,1)S(1)} %slice.56), channel_id=1, source_target_pairs={{0,224},{1,225},{2,226},{3,227},{4,228},{5,229},{6,230},{7,231},{8... | collective-permute-start | bytes 835592 | tf_op jit(solution)/shard_map/ppermute | solution.py:31
  109.6 7.3 %collective-permute-start.7 = (bf16[1,64,2176]{2,1,0:T(8,128)(2,1)S(1)}, bf16[1,64,2176]{2,1,0:T(8,128)(2,1)S(1)}, u32[]{:S(2)}, u32[]{:S(2)}) collective-permute-start(bf16[1,64,2176]{2,1,0:T(8,128)(2,1)S(1)} %slice.55), channel_id=1, source_target_pairs={{0,32},{1,33},{2,34},{3,35},{4,36},{5,37},{6,38},{7,39},{8,40},{9,... | collective-permute-start | bytes 835592 | tf_op jit(solution)/shard_map/ppermute | solution.py:31
  117.1 2.2 %copy-start.1 = (bf16[8,2,64,2176]{3,2,1,0:T(8,128)(2,1)}, bf16[8,2,64,2176]{3,2,1,0:T(8,128)(2,1)S(1)}, u32[]{:S(2)}) copy-start(bf16[8,2,64,2176]{3,2,1,0:T(8,128)(2,1)S(1)} %bitcast_dynamic-update-slice_fusion.panel_ref) | copy-start | bytes 13369348
  147.1 3.5 %copy-start = (bf16[1024,4352]{1,0:T(8,128)(2,1)S(1)}, bf16[1024,4352]{1,0:T(8,128)(2,1)}, u32[]{:S(2)}) copy-start(bf16[1024,4352]{1,0:T(8,128)(2,1)} %all-gather.3.cloned.1.call-done) | copy-start | bytes 26738692
  150.6 2.3 %copy-start.2 = (bf16[8,2,64,2176]{3,2,1,0:T(8,128)(2,1)S(1)}, bf16[8,2,64,2176]{3,2,1,0:T(8,128)(2,1)}, u32[]{:S(2)}) copy-start(bf16[8,2,64,2176]{3,2,1,0:T(8,128)(2,1)} %copy-done.1) | copy-start | bytes 13369348
  156.5 4.8 %collective-permute-start.10 = (f32[512,512]{1,0:T(8,128)S(1)}, f32[512,512]{1,0:T(8,128)S(1)}, u32[]{:S(2)}, u32[]{:S(2)}) collective-permute-start(f32[512,512]{1,0:T(8,128)S(1)} %scores.3), channel_id=1, source_target_pairs={{0,8},{1,9},{2,10},{3,11},{4,12},{5,13},{6,14},{7,15},{8,0},{9,1},... | collective-permute-start | bytes 3145736 | tf_op jit(solution)/shard_map/ppermute | solution.py:31
  162.4 10.1 %all-to-all-start.1 = ((f32[8,8,512]{2,1,0:T(8,128)}), f32[8,8,512]{2,1,0:T(8,128)S(1)}, u32[]{:S(2)}, u32[]{:S(2)}) async-start(f32[8,8,512]{2,1,0:T(8,128)} %broadcast_in_dim.16), calls=%async_computation.1 | async-start | bytes 262144 | tf_op jit(solution)/shard_map/all_to_all | solution.py:251
  174.2 17.2 %all-to-all-start.2 = ((f32[32,1,512]{2,1,0:T(1,128)}), f32[32,1,512]{2,1,0:T(1,128)S(1)}, u32[]{:S(2)}, u32[]{:S(2)}) async-start(f32[32,1,512]{2,1,0:T(1,128)} %broadcast_in_dim.17), calls=%async_computation.2 | async-start | bytes 131072 | tf_op jit(solution)/shard_map/all_to_all | solution.py:255
Sparse Core Ops, SparseCore 0:
  18.6 128.4 all-gather.2

commit v2 on v1

v2 whole, which is shorter than its diff:
```python
import functools
import jax
import jax.numpy as jnp
from jax import lax
from jax.experimental import pallas as pl
from jax.experimental.pallas import tpu as pltpu
from jax.sharding import PartitionSpec as P

NX, NZ = 4, 8
NDP, NOR = 32, 8
CLS, PIX, GRP, ORI, ROWS = 8, 4224, 64, 64, 64
FEAT = 2 * PIX
EXT = 256
COLS = FEAT + EXT
HALF = COLS // 2
QUART = COLS // 4
GROUP_ROWS = NOR * ROWS
HIGH = lax.Precision.HIGHEST
NT = (((1,), (1,)), ((), ()))
MIB = 1024 * 1024


def permute(array, move):
    pairs = []
    for dp in range(NDP):
        for orient in range(NOR):
            place = (dp // 4, (dp // 2) % 2, dp % 2, orient // 2, orient % 2)
            z, ylo, core, x, yhi = move(*place)
            target = ((z % NZ) * 4 + ylo * 2 + core) * NOR + (x % NX) * 2 + yhi
            pairs.append((dp * NOR + orient, target))
    return lax.ppermute(array, ("dp", "orient"), pairs)


def other_core(array):
    return permute(array, lambda z, ylo, core, x, yhi: (z, ylo, 1 - core, x, yhi))


def other_ylo(array):
    return permute(array, lambda z, ylo, core, x, yhi: (z, 1 - ylo, core, x, yhi))


def other_yhi(array):
    return permute(array, lambda z, ylo, core, x, yhi: (z, ylo, core, x, 1 - yhi))


def from_below(array):
    return permute(array, lambda z, ylo, core, x, yhi: (z + 1, ylo, core, x, yhi))


def from_above(array):
    return permute(array, lambda z, ylo, core, x, yhi: (z - 1, ylo, core, x, yhi))


def from_left(array):
    return permute(array, lambda z, ylo, core, x, yhi: (z, ylo, core, x + 1, yhi))


def from_right(array):
    return permute(array, lambda z, ylo, core, x, yhi: (z, ylo, core, x - 1, yhi))


def vmem():
    return pl.BlockSpec(memory_space=pltpu.VMEM)


def anywhere():
    return pl.BlockSpec(memory_space=pl.ANY)


def smem():
    return pl.BlockSpec(memory_space=pltpu.SMEM)


def params(mib, **more):
    return pltpu.CompilerParams(vmem_limit_bytes=mib * MIB, **more)


def place():
    dp, orient = lax.axis_index("dp"), lax.axis_index("orient")
    return dp // 4, (dp // 2) % 2, dp % 2, orient // 2, orient % 2


def weigh_kernel(images_ref, groups_ref, contrast_ref, noise_ref, out_ref):
    _, ylo, core, _, _ = place()
    hot = (
        groups_ref[...] == lax.broadcasted_iota(jnp.int32, (ROWS, GRP), 1)
    ).astype(jnp.float32)
    rows = jnp.dot(hot, contrast_ref[...], precision=HIGH, preferred_element_type=jnp.float32)
    factor = rows * noise_ref[...]
    real = (images_ref[:, :PIX].astype(jnp.float32) * factor).astype(jnp.bfloat16)
    imag = (images_ref[:, PIX:].astype(jnp.float32) * factor).astype(jnp.bfloat16)
    ext = jnp.concatenate([hot, hot, hot, jnp.zeros_like(hot)], axis=1).astype(jnp.bfloat16)
    out_ref[core, ylo] = real[:, :QUART]
    out_ref[core, 1 - ylo] = jnp.concatenate([real[:, QUART:], imag[:, : HALF - PIX]], axis=1)
    out_ref[1 - core, ylo] = imag[:, HALF - PIX : 3 * QUART - PIX]
    out_ref[1 - core, 1 - ylo] = jnp.concatenate([imag[:, 3 * QUART - PIX :], ext], axis=1)


def weigh(images, groups, contrast, noise):
    return pl.pallas_call(
        weigh_kernel,
        out_shape=jax.ShapeDtypeStruct((2, 2, ROWS, QUART), jnp.bfloat16),
        in_specs=[vmem(), vmem(), vmem(), vmem()],
        out_specs=vmem(),
        compiler_params=params(24),
        name="weigh",
    )(images, groups, contrast, noise)


def panel_kernel(owners_ref, priors_ref, slot_ref, contrast_ref, noise_ref, out_ref):
    dp = lax.axis_index("dp")
    prior = jnp.float32(0)
    for k in range(CLS):
        prior += jnp.where(owners_ref[k] == dp, priors_ref[k], jnp.float32(0))
    contrast = contrast_ref[...]
    power = contrast * contrast * noise_ref[...]
    real = slot_ref[:, :PIX].astype(jnp.float32)
    imag = slot_ref[:, PIX:].astype(jnp.float32)
    table = lax.dot_general(
        real * real + imag * imag, power, NT, precision=HIGH, preferred_element_type=jnp.float32
    )
    table = -0.5 * table + prior
    first = table.astype(jnp.bfloat16).astype(jnp.float32)
    rest = table - first
    second = rest.astype(jnp.bfloat16).astype(jnp.float32)
    third = rest - second
    ext = jnp.concatenate([first, second, third, jnp.zeros_like(first)], axis=1)
    for z in range(NZ):
        rows = slice(8 * z, 8 * z + 8)
        for ylo in range(2):
            parts = []
            for core in range(2):
                start = core * HALF + ylo * QUART
                stop = start + QUART
                if stop <= FEAT:
                    part = slot_ref[:, start:stop].astype(jnp.float32)[rows]
                else:
                    part = jnp.concatenate(
                        [slot_ref[:, start:FEAT].astype(jnp.float32)[rows], ext[rows]], axis=1
                    )
                parts.append(part)
            at = (z * 4 + ylo * 2) * 8
            out_ref[at : at + 16, :] = jnp.concatenate(parts, axis=0).astype(jnp.bfloat16)


def panel(owners, priors, slot, contrast, noise):
    return pl.pallas_call(
        panel_kernel,
        out_shape=jax.ShapeDtypeStruct((NDP * 8, QUART), jnp.bfloat16),
        in_specs=[smem(), smem(), vmem(), vmem(), vmem()],
        out_specs=vmem(),
        compiler_params=params(24),
        name="panel",
    )(owners, priors, slot, contrast, noise)


def pick_kernel(owners_ref, got_ref, out_ref, sems):
    copies = [
        pltpu.make_async_copy(got_ref.at[owners_ref[k]], out_ref.at[k], sems.at[k])
        for k in range(CLS)
    ]
    for copy in copies:
        copy.start()
    for copy in copies:
        copy.wait()


def pick(owners, got):
    return pl.pallas_call(
        pick_kernel,
        out_shape=jax.ShapeDtypeStruct((CLS, 8, QUART), jnp.bfloat16),
        in_specs=[smem(), anywhere()],
        out_specs=vmem(),
        scratch_shapes=[pltpu.SemaphoreType.DMA((CLS,))],
        compiler_params=params(16),
        name="pick",
    )(owners, got)


def scores_kernel(owners, n_panels, n_images, *refs):
    panels, refs = refs[:n_panels], refs[n_panels:]
    images, refs = refs[:n_images], refs[n_images:]
    outs, (panel_buf, image_buf, panel_sems, image_sems) = refs[: len(owners)], refs[len(owners) :]

    def panel_copies(chain):
        at = 0
        for ref in panels:
            if ref.shape[0] == 1:
                source = ref.at[0] if ref is panels[n_panels - 2 + chain] else None
            else:
                source = ref.at[chain]
            if source is not None:
                target = panel_buf.at[chain, CLS * 8 * at : CLS * 8 * (at + 1)]
                yield pltpu.make_async_copy(source, target, panel_sems.at[chain, at])
                at += 1

    def image_copies(owner, slot, chain):
        for at, ref in enumerate(images):
            target = image_buf.at[slot, chain, ROWS * at : ROWS * (at + 1)]
            yield pltpu.make_async_copy(
                ref.at[owner, chain], target, image_sems.at[slot, chain, at]
            )

    def all_copies(slot, chain):
        copies = list(image_copies(owners[slot], slot, chain))
        return (list(panel_copies(chain)) if slot == 0 else []) + copies

    order = [(slot, chain) for slot in range(len(owners)) for chain in range(2)]
    for slot, chain in order:
        for copy in all_copies(slot, chain):
            copy.start()
    for slot, chain in order:
        for copy in all_copies(slot, chain):
            copy.wait()
        part = lax.dot_general(
            panel_buf[chain], image_buf[slot, chain], NT, preferred_element_type=jnp.float32
        )
        if chain == 0:
            outs[slot][...] = part
        else:
            outs[slot][...] += part


def scores_of(panels, images, owners, blocks):
    rows = blocks * CLS * 8
    outs = len(owners)
    return pl.pallas_call(
        functools.partial(scores_kernel, owners, len(panels), len(images)),
        out_shape=[jax.ShapeDtypeStruct((rows, GROUP_ROWS), jnp.float32)] * outs,
        in_specs=[anywhere()] * (len(panels) + len(images)),
        out_specs=[vmem()] * outs,
        scratch_shapes=[
            pltpu.VMEM((2, rows, QUART), jnp.bfloat16),
            pltpu.VMEM((outs, 2, GROUP_ROWS, QUART), jnp.bfloat16),
            pltpu.SemaphoreType.DMA((2, blocks)),
            pltpu.SemaphoreType.DMA((outs, 2, NOR)),
        ],
        compiler_params=params(20),
        cost_estimate=pl.CostEstimate(
            flops=2 * rows * GROUP_ROWS * HALF * outs, bytes_accessed=8 * MIB, transcendentals=0
        ),
        name="scores",
    )(*panels, *images)


def swap_halves(lanes, yhi):
    pieces = [
        pltpu.roll(lanes[:, k : k + 2 * ROWS], yhi * ROWS, 1)
        for k in range(0, GROUP_ROWS, 2 * ROWS)
    ]
    return jnp.concatenate(pieces, axis=1)


def norms_kernel(near_ref, near_other_ref, far_ref, far_other_ref, scores_ref, parts_ref):
    _, _, _, x, yhi = place()
    near = near_ref[...] + near_other_ref[...]
    far = far_ref[...] + far_other_ref[...]
    middle = 4 * CLS * 8
    scores = jnp.concatenate([near[:middle], far, near[middle:]], axis=0)
    scores_ref[...] = scores
    scores = scores.reshape(NZ, CLS, 8, GROUP_ROWS)
    maximum = jnp.max(jnp.max(scores, axis=0), axis=1, keepdims=True)
    totals = jnp.sum(jnp.sum(jnp.exp(scores - maximum[None]), axis=0), axis=1)
    lse = swap_halves(maximum[:, 0, :] + jnp.log(totals), yhi)
    lse = pltpu.roll(lse, x * 2 * ROWS, 1)
    parts_ref[...] = jnp.broadcast_to(lse[None], parts_ref.shape)


def norms(*scores):
    return pl.pallas_call(
        norms_kernel,
        out_shape=(
            jax.ShapeDtypeStruct((NZ * CLS * 8, GROUP_ROWS), jnp.float32),
            jax.ShapeDtypeStruct((NOR, CLS, GROUP_ROWS), jnp.float32),
        ),
        in_specs=[vmem()] * 4,
        out_specs=(vmem(), vmem()),
        compiler_params=params(24),
        name="norms",
    )(*scores)


def finish_kernel(parts_ref, scores_ref, evidence_ref, posterior_ref, mass_ref):
    z, _, _, x, yhi = place()
    parts = parts_ref[...]
    maximum = jnp.max(parts, axis=0)
    class_lse = maximum + jnp.log(jnp.sum(jnp.exp(parts - maximum[None]), axis=0))
    top = jnp.max(class_lse, axis=0, keepdims=True)
    evidence = top + jnp.log(jnp.sum(jnp.exp(class_lse - top), axis=0, keepdims=True))
    evidence_ref[...] = evidence
    posterior_ref[...] = jnp.exp(class_lse - evidence)
    here = swap_halves(pltpu.roll(evidence, ((NX - x) % NX) * 2 * ROWS, 1), yhi)
    terms = jnp.exp(scores_ref[...] - here)
    ones = jnp.ones((NDP, GROUP_ROWS), jnp.float32)
    mass = lax.dot_general(ones, terms, NT, precision=HIGH, preferred_element_type=jnp.float32)
    mass_ref[...] = pltpu.roll(mass, z * CLS * 8, 1)


def finish(parts, scores):
    return pl.pallas_call(
        finish_kernel,
        out_shape=(
            jax.ShapeDtypeStruct((1, GROUP_ROWS), jnp.float32),
            jax.ShapeDtypeStruct((CLS, GROUP_ROWS), jnp.float32),
            jax.ShapeDtypeStruct((NDP, NZ * CLS * 8), jnp.float32),
        ),
        in_specs=[vmem(), vmem()],
        out_specs=(vmem(), vmem(), vmem()),
        compiler_params=params(24),
        name="finish",
    )(parts, scores)


def together(*arrays):
    return lax.optimization_barrier(arrays)


def per_device(images, groups, panel_slots, owners, contrast, noise_weight, class_prior):
    orient = lax.axis_index("orient")
    noise = noise_weight.reshape(1, PIX)

    sent = panel(owners, class_prior, panel_slots[0], contrast, noise).reshape(NDP, 8, QUART)
    got = lax.all_to_all(sent, "dp", 0, 0)

    weighted = weigh(images, groups.reshape(ROWS, 1), contrast, noise)
    own = jnp.stack([weighted[0], other_core(weighted[1])])
    across, left, right = other_yhi(own), from_left(own), from_right(own)

    got, left, right, across = together(got, left, right, across)
    mine = pick(owners, got)
    far = [from_left(left[:1]), from_right(right[1:])]
    block = jnp.stack([mine, other_ylo(mine)]).reshape(2, CLS * 8, QUART)
    up1, down1 = from_below(block), from_above(block)
    up1, down1, across, *far = together(up1, down1, across, *far)
    far = jnp.concatenate(far, axis=0)
    left_across, right_across, far_across = from_left(across), from_right(across), other_yhi(far)
    up2, down2 = from_below(up1), from_above(down1)
    up3, down3 = from_below(up2), from_above(down2)
    up3, down3, left_across, right_across, far_across = together(
        up3, down3, left_across, right_across, far_across
    )
    last = [from_below(up3[:1]), from_above(down3[1:])]
    whole = [own, across, right, right_across, far, far_across, left, left_across]

    near = [block, down1, down2, down3, up3, up2, up1]
    (near_theirs,) = scores_of(near, whole, (1,), 7)
    near_other = other_core(near_theirs)
    (near_mine,) = scores_of(near, whole, (0,), 7)
    near_mine, *last = together(near_mine, *last)
    far_theirs, far_mine = scores_of(last, whole, (1, 0), 1)
    scores, partial = norms(near_mine, near_other, far_mine, other_core(far_theirs))
    parts = lax.all_to_all(partial, "orient", 0, 0)
    evidence, posterior, mass = finish(parts, scores)
    masses = lax.all_to_all(mass, "dp", 0, 0)
    normalise = CLS * ORI * NOR / (ROWS * NOR * NDP)
    total = jnp.sum(masses, axis=0) * normalise
    orientation_mass = total.reshape(NZ, CLS, 8).transpose(1, 0, 2).reshape(CLS, ORI)
    log_evidence = lax.dynamic_slice_in_dim(evidence[0], orient * ROWS, ROWS, 0)
    class_posterior = lax.dynamic_slice_in_dim(posterior, orient * ROWS, ROWS, 1)
    return (log_evidence, class_posterior, orientation_mass)


def solution(mesh):
    return jax.shard_map(
        per_device,
        mesh=mesh,
        in_specs=(
            P(("dp", "orient"), None),
            P(("dp", "orient")),
            P("dp", "orient", None),
            P(),
            P(),
            P(),
            P(),
        ),
        out_specs=(P(("dp", "orient")), P(None, ("dp", "orient")), P(None, "orient")),
        check_vma=False,
    )
```

time: 200 us -> 170 us (0.85)
  between operations: 29.2 us -> 0.82 us
  starting transfers between devices: 38.9 us -> 54.3 us
  waiting for transfers between devices: 99.8 us -> 86.1 us
  local copies, waits for them, and re-layouts: 16.6 us -> 7.64 us
  Pallas kernels: 12.7 us -> 20.4 us
    ppermute x11 -> x20, waiting for transfers between devices: 44.3 us -> 72.1 us  [permute(): return lax.ppermute(array, ('dp', 'orient'), pairs)]
    all_gather x1 -> x0, waiting for transfers between devices: 27.7 us -> none  [per_device(): whole = lax.all_gather(group, 'orient', axis=0).reshape(NOR, 2, ROWS, HALF)]
    all_to_all x1, waiting for transfers between devices: 14 us -> 0.01 us  [per_device(): got = lax.all_to_all(sent, 'dp', 0, 0)]
    ppermute x11 -> x20, starting transfers between devices: 18.4 us -> 32.2 us  [permute(): return lax.ppermute(array, ('dp', 'orient'), pairs)]
    pallas_call x4 -> x6, Pallas kernels: 8.78 us -> 16.3 us  [the longest x3 12.4 us: scores_of(): pl.pallas_call(functools.partial(scores_kernel, owners, len(panels), len(...]
    unnamed x30 -> x17, local copies, waits for them, and re-layouts: 10.8 us -> 3.83 us
    all_to_all x1, starting transfers between devices: 8.26 us -> 11.3 us  [per_device(): got = lax.all_to_all(sent, 'dp', 0, 0)]
  transfers between devices with their start and end apart: 15 -> 23, of which waited for: 11 -> 14; matrix products, arithmetic and copies ran while one was open for 2% -> 1% of each run, Pallas kernels for 3% -> 6%
where the time goes in v2:
time: 170 us; the launch traced here: 169 us
  waiting for transfers between devices  86.1 us (51%)
  starting transfers between devices  54.3 us (32%)
  Pallas kernels  20.4 us (12%)
  local copies, waits for them, and re-layouts  7.64 us (4%)
    ppermute x20, waiting for transfers between devices, permute(): return lax.ppermute(array, ('dp', 'orient'), pairs)  72.1 us
    ppermute x20, starting transfers between devices, permute(): return lax.ppermute(array, ('dp', 'orient'), pairs)  32.2 us
    pallas_call x3, Pallas kernels, scores_of(): pl.pallas_call(functools.partial(scores_kernel, owners, len(panels), len(...  12.4 us
    all_to_all x1, starting transfers between devices, per_device(): got = lax.all_to_all(sent, 'dp', 0, 0)  11.3 us
    all_to_all x1, waiting for transfers between devices, per_device(): masses = lax.all_to_all(mass, 'dp', 0, 0)  7.07 us
    all_to_all x1, waiting for transfers between devices, per_device(): parts = lax.all_to_all(partial, 'orient', 0, 0)  6.94 us
    all_to_all x1, starting transfers between devices, per_device(): masses = lax.all_to_all(mass, 'dp', 0, 0)  6.83 us
    all_to_all x1, starting transfers between devices, per_device(): parts = lax.all_to_all(partial, 'orient', 0, 0)  3.95 us
  transfers between devices with their start and end apart: 23, of which 14 were waited for; matrix products, arithmetic and copies ran while one was open for 1% of the time, Pallas kernels for 6%

profile of v2, /device:TPU:1, one launch (start us, length us, event | category | flops | bytes accessed | tf_op | source)
XLA Modules:
  0.0 169.5 jit_solution(12658748619817477518)
XLA Ops:
  0.6 0.7 reshape.30.noise_ref
  1.4 1.2 copy-done
  2.6 1.2 copy-done.2
  3.9 0.7 copy-done.4
  4.5 0.7 copy-done.6
  5.2 2.8 %panel.1 = bf16[256,2176]{1,0:T(8,128)(2,1)} custom-call(s32[8]{0:T(128)S(1)} %copy-done.4, f32[8]{0:T(128)S(1)} %copy-done.6, bf16[64,8448]{1,0:T(8,128)(2,1)S(1)} %bitcast.13, f32[64,4224]{1,0:T(8,128)S(1)} %copy-done, f32[1,4224]{1,0:T(1,128)S(1)} %reshape.30.noise_ref), custom_call_target="tpu_custom_call" | custom-call | tf_op jit(solution)/shard_map/panel/pallas_call | solution.py:147
  7.9 11.3 %all-to-all-start = ((bf16[32,8,2176]{2,1,0:T(8,128)(2,1)}), bf16[32,8,2176]{2,1,0:T(8,128)(2,1)}, u32[]{:S(2)}, u32[]{:S(2)}) async-start(bf16[32,8,2176]{2,1,0:T(8,128)(2,1)} %bitcast.1), calls=%async_computation | async-start | bytes 2228224 | tf_op jit(solution)/shard_map/all_to_all | solution.py:323
  19.4 1.1 weigh.1
  21.0 1.7 collective-permute-done
  22.8 1.3 collective-permute-start.1
  24.1 1.5 collective-permute-start.2
  25.5 2.6 %collective-permute-start.3 = (bf16[2,2,64,2176]{3,2,1,0:T(8,128)(2,1)S(1)}, bf16[2,2,64,2176]{3,2,1,0:T(8,128)(2,1)}, u32[]{:S(2)}, u32[]{:S(2)}) collective-permute-start(bf16[2,2,64,2176]{3,2,1,0:T(8,128)(2,1)S(1)} %pad_maximum_fusion.refs_7_.refs_2_), channel_id=1, source_target_pairs={{0,1},{1,0},{2,3},{3,2},{4,5},{5,4},{6,7},{7,6},{8,9},{9,8},{10,11... | collective-permute-start | bytes 3342344 | tf_op jit(solution)/shard_map/ppermute | solution.py:31
  28.1 21.9 %collective-permute-done.1.refs_13_.refs_8_ = bf16[2,2,64,2176]{3,2,1,0:T(8,128)(2,1)S(1)} collective-permute-done((bf16[2,2,64,2176]{3,2,1,0:T(8,128)(2,1)S(1)}, bf16[2,2,64,2176]{3,2,1,0:T(8,128)(2,1)S(1)}, u32[]{:S(2)}, u32[]{:S(2)}) %collective-permute-start.1) | collective-permute-done | bytes 1114144 | tf_op jit(solution)/shard_map/ppermute | solution.py:31
  50.0 11.3 %collective-permute-done.3.refs_8_.refs_3_ = bf16[2,2,64,2176]{3,2,1,0:T(8,128)(2,1)} collective-permute-done((bf16[2,2,64,2176]{3,2,1,0:T(8,128)(2,1)S(1)}, bf16[2,2,64,2176]{3,2,1,0:T(8,128)(2,1)}, u32[]{:S(2)}, u32[]{:S(2)}) %collective-permute-start.3) | collective-permute-done | bytes 1114144 | tf_op jit(solution)/shard_map/ppermute | solution.py:31
  61.3 1.5 pick.1
  62.8 1.5 collective-permute-start.4
  64.9 2.3 %collective-permute-start.8 = (bf16[1,2,64,2176]{3,2,1,0:T(8,128)(2,1)S(1)}, bf16[1,2,64,2176]{3,2,1,0:T(8,128)(2,1)S(1)}, u32[]{:S(2)}, u32[]{:S(2)}) collective-permute-start(bf16[1,2,64,2176]{3,2,1,0:T(8,128)(2,1)S(1)} %slice.21), channel_id=1, source_target_pairs={{0,6},{1,7},{2,0},{3,1},{4,2},{5,3},{6,4},{7,5},{8,14},{9,15},{10,... | collective-permute-start | bytes 1671176 | tf_op jit(solution)/shard_map/ppermute | solution.py:31
  67.2 3.1 %collective-permute-done.4 = bf16[8,8,2176]{2,1,0:T(8,128)(2,1)S(1)} collective-permute-done((bf16[8,8,2176]{2,1,0:T(8,128)(2,1)S(1)}, bf16[8,8,2176]{2,1,0:T(8,128)(2,1)S(1)}, u32[]{:S(2)}, u32[]{:S(2)}) %collective-permute-start.4) | collective-permute-done | bytes 278560 | tf_op jit(solution)/shard_map/ppermute | solution.py:31
  70.4 1.5 collective-permute-start.5
  71.9 1.3 collective-permute-start.6
  73.1 5.3 %collective-permute-done.7 = bf16[1,2,64,2176]{3,2,1,0:T(8,128)(2,1)S(1)} collective-permute-done((bf16[1,2,64,2176]{3,2,1,0:T(8,128)(2,1)S(1)}, bf16[1,2,64,2176]{3,2,1,0:T(8,128)(2,1)S(1)}, u32[]{:S(2)}, u32[]{:S(2)}) %collective-permute-start.7) | collective-permute-done | bytes 557088 | tf_op jit(solution)/shard_map/ppermute | solution.py:31
  78.5 5.6 %collective-permute-done.5.refs_6_ = bf16[2,64,2176]{2,1,0:T(8,128)(2,1)S(1)} collective-permute-done((bf16[2,64,2176]{2,1,0:T(8,128)(2,1)S(1)}, bf16[2,64,2176]{2,1,0:T(8,128)(2,1)S(1)}, u32[]{:S(2)}, u32[]{:S(2)}) %collective-permute-start.5) | collective-permute-done | bytes 557088 | tf_op jit(solution)/shard_map/ppermute | solution.py:31
  84.2 3.9 %collective-permute-start.15 = (bf16[2,2,64,2176]{3,2,1,0:T(8,128)(2,1)S(1)}, bf16[2,2,64,2176]{3,2,1,0:T(8,128)(2,1)S(1)}, u32[]{:S(2)}, u32[]{:S(2)}) collective-permute-start(bf16[2,2,64,2176]{3,2,1,0:T(8,128)(2,1)S(1)} %constant_dynamic-update-slice_fusion.refs_11_.refs_6_), channel_id=1, source_target_pairs={{0,1},{1,0},{2,3},{3,2},{4,5},{5,4},{6,7},{7,6},{8,9},{9,8},{10,11... | collective-permute-start | bytes 3342344 | tf_op jit(solution)/shard_map/ppermute | solution.py:31
  88.1 2.7 %collective-permute-start.9 = (bf16[2,64,2176]{2,1,0:T(8,128)(2,1)S(1)}, bf16[2,64,2176]{2,1,0:T(8,128)(2,1)S(1)}, u32[]{:S(2)}, u32[]{:S(2)}) collective-permute-start(bf16[2,64,2176]{2,1,0:T(8,128)(2,1)S(1)} %collective-permute-done.6.refs_1_), channel_id=1, source_target_pairs={{0,224},{1,225},{2,226},{3,227},{4,228},{5,229},{6,230},{7,231},{8... | collective-permute-start | bytes 1671176 | tf_op jit(solution)/shard_map/ppermute | solution.py:31
  90.8 2.7 %collective-permute-start.14 = (bf16[2,2,64,2176]{3,2,1,0:T(8,128)(2,1)}, bf16[2,2,64,2176]{3,2,1,0:T(8,128)(2,1)S(1)}, u32[]{:S(2)}, u32[]{:S(2)}) collective-permute-start(bf16[2,2,64,2176]{3,2,1,0:T(8,128)(2,1)} %collective-permute-done.3.refs_8_.refs_3_), channel_id=1, source_target_pairs={{0,6},{1,7},{2,0},{3,1},{4,2},{5,3},{6,4},{7,5},{8,14},{9,15},{10,... | collective-permute-start | bytes 3342344 | tf_op jit(solution)/shard_map/ppermute | solution.py:31
  93.5 7.8 %collective-permute-done.10.refs_5_ = bf16[2,64,2176]{2,1,0:T(8,128)(2,1)S(1)} collective-permute-done((bf16[2,64,2176]{2,1,0:T(8,128)(2,1)S(1)}, bf16[2,64,2176]{2,1,0:T(8,128)(2,1)S(1)}, u32[]{:S(2)}, u32[]{:S(2)}) %collective-permute-start.10) | collective-permute-done | bytes 557088 | tf_op jit(solution)/shard_map/ppermute | solution.py:31
  101.2 2.7 %collective-permute-start.12 = (bf16[2,64,2176]{2,1,0:T(8,128)(2,1)S(1)}, bf16[2,64,2176]{2,1,0:T(8,128)(2,1)S(1)}, u32[]{:S(2)}, u32[]{:S(2)}) collective-permute-start(bf16[2,64,2176]{2,1,0:T(8,128)(2,1)S(1)} %collective-permute-done.9.refs_2_), channel_id=1, source_target_pairs={{0,224},{1,225},{2,226},{3,227},{4,228},{5,229},{6,230},{7,231},{8... | collective-permute-start | bytes 1671176 | tf_op jit(solution)/shard_map/ppermute | solution.py:31
  103.9 6.9 %collective-permute-done.15.refs_12_.refs_7_ = bf16[2,2,64,2176]{3,2,1,0:T(8,128)(2,1)S(1)} collective-permute-done((bf16[2,2,64,2176]{3,2,1,0:T(8,128)(2,1)S(1)}, bf16[2,2,64,2176]{3,2,1,0:T(8,128)(2,1)S(1)}, u32[]{:S(2)}, u32[]{:S(2)}) %collective-permute-start.15) | collective-permute-done | bytes 1114144 | tf_op jit(solution)/shard_map/ppermute | solution.py:31
  110.8 2.6 %collective-permute-done.11.refs_4_ = bf16[2,64,2176]{2,1,0:T(8,128)(2,1)S(1)} collective-permute-done((bf16[2,64,2176]{2,1,0:T(8,128)(2,1)S(1)}, bf16[2,64,2176]{2,1,0:T(8,128)(2,1)S(1)}, u32[]{:S(2)}, u32[]{:S(2)}) %collective-permute-start.11) | collective-permute-done | bytes 557088 | tf_op jit(solution)/shard_map/ppermute | solution.py:31
  113.4 2.1 %collective-permute-done.13.refs_14_.refs_9_ = bf16[2,2,64,2176]{3,2,1,0:T(8,128)(2,1)S(1)} collective-permute-done((bf16[2,2,64,2176]{3,2,1,0:T(8,128)(2,1)}, bf16[2,2,64,2176]{3,2,1,0:T(8,128)(2,1)S(1)}, u32[]{:S(2)}, u32[]{:S(2)}) %collective-permute-start.13) | collective-permute-done | bytes 1114144 | tf_op jit(solution)/shard_map/ppermute | solution.py:31
  115.5 4.0 %scores.4 = f32[448,512]{1,0:T(8,128)S(1)} custom-call(bf16[2,64,2176]{2,1,0:T(8,128)(2,1)S(1)} %pad_maximum_fusion.1.refs_0_, bf16[2,64,2176]{2,1,0:T(8,128)(2,1)S(1)} %collective-permute-done.6.refs_1_, bf16[2,64,2176]{2,1,0:T(8,128)(2,1)S(1)} %collective-permute-done.9.refs_2_, bf16[2,64,2176]{2,1,0:T(8,128)(2,1)S(1)} %collective-permute-done.12.refs_3_, ...), custom_call_target="tpu_custom_call" | custom-call | flops 1996488704 | bytes 8388608 | tf_op jit(solution)/shard_map/scores/pallas_call | solution.py:227
  119.5 3.8 %collective-permute-start.18 = (f32[448,512]{1,0:T(8,128)S(1)}, f32[448,512]{1,0:T(8,128)S(1)}, u32[]{:S(2)}, u32[]{:S(2)}) collective-permute-start(f32[448,512]{1,0:T(8,128)S(1)} %scores.4), channel_id=1, source_target_pairs={{0,8},{1,9},{2,10},{3,11},{4,12},{5,13},{6,14},{7,15},{8,0},{9,1},... | collective-permute-start | bytes 2752520 | tf_op jit(solution)/shard_map/ppermute | solution.py:31
  123.4 2.7 %collective-permute-start.17 = (bf16[1,64,2176]{2,1,0:T(8,128)(2,1)S(1)}, bf16[1,64,2176]{2,1,0:T(8,128)(2,1)S(1)}, u32[]{:S(2)}, u32[]{:S(2)}) collective-permute-start(bf16[1,64,2176]{2,1,0:T(8,128)(2,1)S(1)} %slice.23), channel_id=1, source_target_pairs={{0,224},{1,225},{2,226},{3,227},{4,228},{5,229},{6,230},{7,231},{8... | collective-permute-start | bytes 835592 | tf_op jit(solution)/shard_map/ppermute | solution.py:31
  126.1 4.0 %scores.3.near_ref = f32[448,512]{1,0:T(8,128)S(1)} custom-call(bf16[2,64,2176]{2,1,0:T(8,128)(2,1)S(1)} %pad_maximum_fusion.1.refs_0_, bf16[2,64,2176]{2,1,0:T(8,128)(2,1)S(1)} %collective-permute-done.6.refs_1_, bf16[2,64,2176]{2,1,0:T(8,128)(2,1)S(1)} %collective-permute-done.9.refs_2_, bf16[2,64,2176]{2,1,0:T(8,128)(2,1)S(1)} %collective-permute-done.12.refs_3_, ...), custom_call_target="tpu_custom_call" | custom-call | flops 1996488704 | bytes 8388608 | tf_op jit(solution)/shard_map/scores/pallas_call | solution.py:227
  130.1 2.8 %collective-permute-done.16.refs_0_ = bf16[1,64,2176]{2,1,0:T(8,128)(2,1)S(1)} collective-permute-done((bf16[1,64,2176]{2,1,0:T(8,128)(2,1)S(1)}, bf16[1,64,2176]{2,1,0:T(8,128)(2,1)S(1)}, u32[]{:S(2)}, u32[]{:S(2)}) %collective-permute-start.16) | collective-permute-done | bytes 278560 | tf_op jit(solution)/shard_map/ppermute | solution.py:31
  132.9 4.5 %scores.5 = (f32[64,512]{1,0:T(8,128)S(1)}, f32[64,512]{1,0:T(8,128)S(1)}) custom-call(bf16[1,64,2176]{2,1,0:T(8,128)(2,1)S(1)} %collective-permute-done.16.refs_0_, bf16[1,64,2176]{2,1,0:T(8,128)(2,1)S(1)} %collective-permute-done.17.refs_1_, bf16[2,2,64,2176]{3,2,1,0:T(8,128)(2,1)S(1)} %pad_maximum_fusion.refs_7_.refs_2_, ...), custom_call_target="tpu_custom_call" | custom-call | flops 570425344 | bytes 8388608 | tf_op jit(solution)/shard_map/scores/pallas_call | solution.py:227
  137.4 0.9 collective-permute-start.19
  138.3 1.0 collective-permute-done.19.far_other_ref
  139.3 1.3 norms.1
  140.5 3.9 %all-to-all-start.1 = ((f32[8,8,512]{2,1,0:T(8,128)}), f32[8,8,512]{2,1,0:T(8,128)S(1)}, u32[]{:S(2)}, u32[]{:S(2)}) async-start(f32[8,8,512]{2,1,0:T(8,128)} %get-tuple-element.46), calls=%async_computation.1 | async-start | bytes 262144 | tf_op jit(solution)/shard_map/all_to_all | solution.py:352
  144.5 6.9 %all-to-all-done.1.parts_ref = f32[8,8,512]{2,1,0:T(8,128)S(1)} async-done(((f32[8,8,512]{2,1,0:T(8,128)}), f32[8,8,512]{2,1,0:T(8,128)S(1)}, u32[]{:S(2)}, u32[]{:S(2)}) %all-to-all-start.1) | async-done | bytes 131104 | tf_op jit(solution)/shard_map/all_to_all | solution.py:352
  151.4 1.4 finish.1
  152.8 0.7 copy.15
  153.5 6.8 %all-to-all-start.2 = ((f32[32,1,512]{2,1,0:T(1,128)}), f32[32,1,512]{2,1,0:T(1,128)S(1)}, u32[]{:S(2)}, u32[]{:S(2)}) async-start(f32[32,1,512]{2,1,0:T(1,128)} %copy.15), calls=%async_computation.2 | async-start | bytes 131072 | tf_op jit(solution)/shard_map/all_to_all | solution.py:354
  160.3 0.6 dynamic-slice_bitcast_fusion
  160.9 0.7 constant_dynamic-slice_fusion
  161.6 7.1 %all-to-all-done.2 = f32[32,1,512]{2,1,0:T(1,128)S(1)} async-done(((f32[32,1,512]{2,1,0:T(1,128)}), f32[32,1,512]{2,1,0:T(1,128)S(1)}, u32[]{:S(2)}, u32[]{:S(2)}) %all-to-all-start.2) | async-done | bytes 65568 | tf_op jit(solution)/shard_map/all_to_all | solution.py:354
  168.8 0.7 reshape.33
  (41 shorter events, 1.8 us)
Async XLA Ops:
  1.4 1.2 copy-start
  2.6 1.2 copy-start.2
  3.9 0.7 copy-start.4
  4.5 0.7 copy-start.6
  7.9 11.3 %copy-start.7 = (s32[64]{0:T(128)S(1)}, s32[64]{0:T(128)}, u32[]{:S(2)}) copy-start(s32[64]{0:T(128)} %param.8) | copy-start | bytes 772
  7.9 11.4 %copy-start.1 = (f32[64,4224]{1,0:T(8,128)S(1)}, f32[64,4224]{1,0:T(8,128)}, u32[]{:S(2)}) copy-start(f32[64,4224]{1,0:T(8,128)} %contrast_ref.3) | copy-start | bytes 3244036
  7.9 11.4 %copy-start.3 = (bf16[64,8448]{1,0:T(8,128)(2,1)S(1)}, bf16[64,8448]{1,0:T(8,128)(2,1)}, u32[]{:S(2)}) copy-start(bf16[64,8448]{1,0:T(8,128)(2,1)} %images_ref.1) | copy-start | bytes 3244036
  7.9 53.4 %all-to-all-start = ((bf16[32,8,2176]{2,1,0:T(8,128)(2,1)}), bf16[32,8,2176]{2,1,0:T(8,128)(2,1)}, u32[]{:S(2)}, u32[]{:S(2)}) async-start(bf16[32,8,2176]{2,1,0:T(8,128)(2,1)} %bitcast.1), calls=%async_computation | async-start | bytes 2228224 | tf_op jit(solution)/shard_map/all_to_all | solution.py:323
  20.6 2.0 %collective-permute-start = (bf16[2,64,2176]{2,1,0:T(8,128)(2,1)S(1)}, bf16[2,64,2176]{2,1,0:T(8,128)(2,1)S(1)}, u32[]{:S(2)}, u32[]{:S(2)}) collective-permute-start(bf16[2,64,2176]{2,1,0:T(8,128)(2,1)S(1)} %get-tuple-element.52), channel_id=1, source_target_pairs={{0,8},{1,9},{2,10},{3,11},{4,12},{5,13},{6,14},{7,15},{8,0},{9,1},... | collective-permute-start | bytes 1671176 | tf_op jit(solution)/shard_map/ppermute | solution.py:31
  22.6 38.7 %copy-start.5 = (s32[8]{0:T(128)S(1)}, s32[8]{0:T(128)}, u32[]{:S(2)}) copy-start(s32[8]{0:T(128)} %owners_ref.3) | copy-start | bytes 100
  22.8 27.3 %collective-permute-start.1 = (bf16[2,2,64,2176]{3,2,1,0:T(8,128)(2,1)S(1)}, bf16[2,2,64,2176]{3,2,1,0:T(8,128)(2,1)S(1)}, u32[]{:S(2)}, u32[]{:S(2)}) collective-permute-start(bf16[2,2,64,2176]{3,2,1,0:T(8,128)(2,1)S(1)} %pad_maximum_fusion.refs_7_.refs_2_), channel_id=1, source_target_pairs={{0,2},{1,3},{2,4},{3,5},{4,6},{5,7},{6,0},{7,1},{8,10},{9,11},{10,... | collective-permute-start | bytes 3342344 | tf_op jit(solution)/shard_map/ppermute | solution.py:31
  24.1 26.0 %collective-permute-start.2 = (bf16[2,2,64,2176]{3,2,1,0:T(8,128)(2,1)S(1)}, bf16[2,2,64,2176]{3,2,1,0:T(8,128)(2,1)S(1)}, u32[]{:S(2)}, u32[]{:S(2)}) collective-permute-start(bf16[2,2,64,2176]{3,2,1,0:T(8,128)(2,1)S(1)} %pad_maximum_fusion.refs_7_.refs_2_), channel_id=1, source_target_pairs={{0,6},{1,7},{2,0},{3,1},{4,2},{5,3},{6,4},{7,5},{8,14},{9,15},{10,... | collective-permute-start | bytes 3342344 | tf_op jit(solution)/shard_map/ppermute | solution.py:31
  25.5 35.8 %collective-permute-start.3 = (bf16[2,2,64,2176]{3,2,1,0:T(8,128)(2,1)S(1)}, bf16[2,2,64,2176]{3,2,1,0:T(8,128)(2,1)}, u32[]{:S(2)}, u32[]{:S(2)}) collective-permute-start(bf16[2,2,64,2176]{3,2,1,0:T(8,128)(2,1)S(1)} %pad_maximum_fusion.refs_7_.refs_2_), channel_id=1, source_target_pairs={{0,1},{1,0},{2,3},{3,2},{4,5},{5,4},{6,7},{7,6},{8,9},{9,8},{10,11... | collective-permute-start | bytes 3342344 | tf_op jit(solution)/shard_map/ppermute | solution.py:31
  62.8 7.5 %collective-permute-start.4 = (bf16[8,8,2176]{2,1,0:T(8,128)(2,1)S(1)}, bf16[8,8,2176]{2,1,0:T(8,128)(2,1)S(1)}, u32[]{:S(2)}, u32[]{:S(2)}) collective-permute-start(bf16[8,8,2176]{2,1,0:T(8,128)(2,1)S(1)} %pick.1), channel_id=1, source_target_pairs={{0,16},{1,17},{2,18},{3,19},{4,20},{5,21},{6,22},{7,23},{8,24},{9,... | collective-permute-start | bytes 835592 | tf_op jit(solution)/shard_map/ppermute | solution.py:31
  64.3 14.1 %collective-permute-start.7 = (bf16[1,2,64,2176]{3,2,1,0:T(8,128)(2,1)S(1)}, bf16[1,2,64,2176]{3,2,1,0:T(8,128)(2,1)S(1)}, u32[]{:S(2)}, u32[]{:S(2)}) collective-permute-start(bf16[1,2,64,2176]{3,2,1,0:T(8,128)(2,1)S(1)} %slice.20), channel_id=1, source_target_pairs={{0,2},{1,3},{2,4},{3,5},{4,6},{5,7},{6,0},{7,1},{8,10},{9,11},{10,... | collective-permute-start | bytes 1671176 | tf_op jit(solution)/shard_map/ppermute | solution.py:31
  64.9 13.6 %collective-permute-start.8 = (bf16[1,2,64,2176]{3,2,1,0:T(8,128)(2,1)S(1)}, bf16[1,2,64,2176]{3,2,1,0:T(8,128)(2,1)S(1)}, u32[]{:S(2)}, u32[]{:S(2)}) collective-permute-start(bf16[1,2,64,2176]{3,2,1,0:T(8,128)(2,1)S(1)} %slice.21), channel_id=1, source_target_pairs={{0,6},{1,7},{2,0},{3,1},{4,2},{5,3},{6,4},{7,5},{8,14},{9,15},{10,... | collective-permute-start | bytes 1671176 | tf_op jit(solution)/shard_map/ppermute | solution.py:31
  70.4 13.7 %collective-permute-start.5 = (bf16[2,64,2176]{2,1,0:T(8,128)(2,1)S(1)}, bf16[2,64,2176]{2,1,0:T(8,128)(2,1)S(1)}, u32[]{:S(2)}, u32[]{:S(2)}) collective-permute-start(bf16[2,64,2176]{2,1,0:T(8,128)(2,1)S(1)} %pad_maximum_fusion.1.refs_0_), channel_id=1, source_target_pairs={{0,32},{1,33},{2,34},{3,35},{4,36},{5,37},{6,38},{7,39},{8,40},{9,... | collective-permute-start | bytes 1671176 | tf_op jit(solution)/shard_map/ppermute | solution.py:31
  71.9 12.2 %collective-permute-start.6 = (bf16[2,64,2176]{2,1,0:T(8,128)(2,1)S(1)}, bf16[2,64,2176]{2,1,0:T(8,128)(2,1)S(1)}, u32[]{:S(2)}, u32[]{:S(2)}) collective-permute-start(bf16[2,64,2176]{2,1,0:T(8,128)(2,1)S(1)} %pad_maximum_fusion.1.refs_0_), channel_id=1, source_target_pairs={{0,224},{1,225},{2,226},{3,227},{4,228},{5,229},{6,230},{7,231},{8... | collective-permute-start | bytes 1671176 | tf_op jit(solution)/shard_map/ppermute | solution.py:31
  84.2 26.6 %collective-permute-start.15 = (bf16[2,2,64,2176]{3,2,1,0:T(8,128)(2,1)S(1)}, bf16[2,2,64,2176]{3,2,1,0:T(8,128)(2,1)S(1)}, u32[]{:S(2)}, u32[]{:S(2)}) collective-permute-start(bf16[2,2,64,2176]{3,2,1,0:T(8,128)(2,1)S(1)} %constant_dynamic-update-slice_fusion.refs_11_.refs_6_), channel_id=1, source_target_pairs={{0,1},{1,0},{2,3},{3,2},{4,5},{5,4},{6,7},{7,6},{8,9},{9,8},{10,11... | collective-permute-start | bytes 3342344 | tf_op jit(solution)/shard_map/ppermute | solution.py:31
  88.1 13.1 %collective-permute-start.10 = (bf16[2,64,2176]{2,1,0:T(8,128)(2,1)S(1)}, bf16[2,64,2176]{2,1,0:T(8,128)(2,1)S(1)}, u32[]{:S(2)}, u32[]{:S(2)}) collective-permute-start(bf16[2,64,2176]{2,1,0:T(8,128)(2,1)S(1)} %collective-permute-done.5.refs_6_), channel_id=1, source_target_pairs={{0,32},{1,33},{2,34},{3,35},{4,36},{5,37},{6,38},{7,39},{8,40},{9,... | collective-permute-start | bytes 1671176 | tf_op jit(solution)/shard_map/ppermute | solution.py:31
  88.1 13.1 %collective-permute-start.9 = (bf16[2,64,2176]{2,1,0:T(8,128)(2,1)S(1)}, bf16[2,64,2176]{2,1,0:T(8,128)(2,1)S(1)}, u32[]{:S(2)}, u32[]{:S(2)}) collective-permute-start(bf16[2,64,2176]{2,1,0:T(8,128)(2,1)S(1)} %collective-permute-done.6.refs_1_), channel_id=1, source_target_pairs={{0,224},{1,225},{2,226},{3,227},{4,228},{5,229},{6,230},{7,231},{8... | collective-permute-start | bytes 1671176 | tf_op jit(solution)/shard_map/ppermute | solution.py:31
  90.8 24.7 %collective-permute-start.13 = (bf16[2,2,64,2176]{3,2,1,0:T(8,128)(2,1)}, bf16[2,2,64,2176]{3,2,1,0:T(8,128)(2,1)S(1)}, u32[]{:S(2)}, u32[]{:S(2)}) collective-permute-start(bf16[2,2,64,2176]{3,2,1,0:T(8,128)(2,1)} %collective-permute-done.3.refs_8_.refs_3_), channel_id=1, source_target_pairs={{0,2},{1,3},{2,4},{3,5},{4,6},{5,7},{6,0},{7,1},{8,10},{9,11},{10,... | collective-permute-start | bytes 3342344 | tf_op jit(solution)/shard_map/ppermute | solution.py:31
  90.8 24.7 %collective-permute-start.14 = (bf16[2,2,64,2176]{3,2,1,0:T(8,128)(2,1)}, bf16[2,2,64,2176]{3,2,1,0:T(8,128)(2,1)S(1)}, u32[]{:S(2)}, u32[]{:S(2)}) collective-permute-start(bf16[2,2,64,2176]{3,2,1,0:T(8,128)(2,1)} %collective-permute-done.3.refs_8_.refs_3_), channel_id=1, source_target_pairs={{0,6},{1,7},{2,0},{3,1},{4,2},{5,3},{6,4},{7,5},{8,14},{9,15},{10,... | collective-permute-start | bytes 3342344 | tf_op jit(solution)/shard_map/ppermute | solution.py:31
  101.2 12.2 %collective-permute-start.11 = (bf16[2,64,2176]{2,1,0:T(8,128)(2,1)S(1)}, bf16[2,64,2176]{2,1,0:T(8,128)(2,1)S(1)}, u32[]{:S(2)}, u32[]{:S(2)}) collective-permute-start(bf16[2,64,2176]{2,1,0:T(8,128)(2,1)S(1)} %collective-permute-done.10.refs_5_), channel_id=1, source_target_pairs={{0,32},{1,33},{2,34},{3,35},{4,36},{5,37},{6,38},{7,39},{8,40},{9,... | collective-permute-start | bytes 1671176 | tf_op jit(solution)/shard_map/ppermute | solution.py:31
  101.2 12.2 %collective-permute-start.12 = (bf16[2,64,2176]{2,1,0:T(8,128)(2,1)S(1)}, bf16[2,64,2176]{2,1,0:T(8,128)(2,1)S(1)}, u32[]{:S(2)}, u32[]{:S(2)}) collective-permute-start(bf16[2,64,2176]{2,1,0:T(8,128)(2,1)S(1)} %collective-permute-done.9.refs_2_), channel_id=1, source_target_pairs={{0,224},{1,225},{2,226},{3,227},{4,228},{5,229},{6,230},{7,231},{8... | collective-permute-start | bytes 1671176 | tf_op jit(solution)/shard_map/ppermute | solution.py:31
  119.5 19.8 %collective-permute-start.18 = (f32[448,512]{1,0:T(8,128)S(1)}, f32[448,512]{1,0:T(8,128)S(1)}, u32[]{:S(2)}, u32[]{:S(2)}) collective-permute-start(f32[448,512]{1,0:T(8,128)S(1)} %scores.4), channel_id=1, source_target_pairs={{0,8},{1,9},{2,10},{3,11},{4,12},{5,13},{6,14},{7,15},{8,0},{9,1},... | collective-permute-start | bytes 2752520 | tf_op jit(solution)/shard_map/ppermute | solution.py:31
  123.3 9.6 %collective-permute-start.16 = (bf16[1,64,2176]{2,1,0:T(8,128)(2,1)S(1)}, bf16[1,64,2176]{2,1,0:T(8,128)(2,1)S(1)}, u32[]{:S(2)}, u32[]{:S(2)}) collective-permute-start(bf16[1,64,2176]{2,1,0:T(8,128)(2,1)S(1)} %slice.22), channel_id=1, source_target_pairs={{0,32},{1,33},{2,34},{3,35},{4,36},{5,37},{6,38},{7,39},{8,40},{9,... | collective-permute-start | bytes 835592 | tf_op jit(solution)/shard_map/ppermute | solution.py:31
  123.4 9.5 %collective-permute-start.17 = (bf16[1,64,2176]{2,1,0:T(8,128)(2,1)S(1)}, bf16[1,64,2176]{2,1,0:T(8,128)(2,1)S(1)}, u32[]{:S(2)}, u32[]{:S(2)}) collective-permute-start(bf16[1,64,2176]{2,1,0:T(8,128)(2,1)S(1)} %slice.23), channel_id=1, source_target_pairs={{0,224},{1,225},{2,226},{3,227},{4,228},{5,229},{6,230},{7,231},{8... | collective-permute-start | bytes 835592 | tf_op jit(solution)/shard_map/ppermute | solution.py:31
  137.4 1.9 %collective-permute-start.19 = (f32[64,512]{1,0:T(8,128)S(1)}, f32[64,512]{1,0:T(8,128)S(1)}, u32[]{:S(2)}, u32[]{:S(2)}) collective-permute-start(f32[64,512]{1,0:T(8,128)S(1)} %get-tuple-element.45), channel_id=1, source_target_pairs={{0,8},{1,9},{2,10},{3,11},{4,12},{5,13},{6,14},{7,15},{8,0},{9,1},... | collective-permute-start | bytes 393224 | tf_op jit(solution)/shard_map/ppermute | solution.py:31
  140.5 10.9 %all-to-all-start.1 = ((f32[8,8,512]{2,1,0:T(8,128)}), f32[8,8,512]{2,1,0:T(8,128)S(1)}, u32[]{:S(2)}, u32[]{:S(2)}) async-start(f32[8,8,512]{2,1,0:T(8,128)} %get-tuple-element.46), calls=%async_computation.1 | async-start | bytes 262144 | tf_op jit(solution)/shard_map/all_to_all | solution.py:352
  153.5 15.2 %all-to-all-start.2 = ((f32[32,1,512]{2,1,0:T(1,128)}), f32[32,1,512]{2,1,0:T(1,128)S(1)}, u32[]{:S(2)}, u32[]{:S(2)}) async-start(f32[32,1,512]{2,1,0:T(1,128)} %copy.15), calls=%async_computation.2 | async-start | bytes 131072 | tf_op jit(solution)/shard_map/all_to_all | solution.py:354

commit v3 on v2

--- a/solution.py
+++ b/solution.py
@@ -107,13 +107,45 @@
     )(images, groups, contrast, noise)
 
 
-def panel_kernel(owners_ref, priors_ref, slot_ref, contrast_ref, noise_ref, out_ref):
+def panel_kernel(
+    owners_hbm, priors_hbm, slot_hbm, contrast_hbm, noise_hbm, out_ref,
+    owners_ref, priors_ref, slot_ref, contrast_ref, noise_ref, sems,
+):
+    pairs = [
+        (slot_hbm.at[0], slot_ref),
+        (contrast_hbm, contrast_ref),
+        (noise_hbm, noise_ref),
+        (owners_hbm, owners_ref),
+        (priors_hbm, priors_ref),
+    ]
+    copies = [pltpu.make_async_copy(a, b, sems.at[k]) for k, (a, b) in enumerate(pairs)]
+    for copy in copies:
+        copy.start()
+
+    def chunks(ylo, ext):
+        for z in range(NZ):
+            rows = slice(8 * z, 8 * z + 8)
+            parts = []
+            for core in range(2):
+                start = core * HALF + ylo * QUART
+                stop = min(start + QUART, FEAT)
+                part = slot_ref[:, start:stop].astype(jnp.float32)[rows]
+                if stop < start + QUART:
+                    part = jnp.concatenate([part, ext[rows]], axis=1)
+                parts.append(part)
+            at = (z * 4 + ylo * 2) * 8
+            out_ref[at : at + 16, :] = jnp.concatenate(parts, axis=0).astype(jnp.bfloat16)
+
+    copies[0].wait()
+    chunks(0, None)
+    for copy in copies[1:]:
+        copy.wait()
     dp = lax.axis_index("dp")
     prior = jnp.float32(0)
     for k in range(CLS):
         prior += jnp.where(owners_ref[k] == dp, priors_ref[k], jnp.float32(0))
     contrast = contrast_ref[...]
-    power = contrast * contrast * noise_ref[...]
+    power = contrast * contrast * noise_ref[...].reshape(1, PIX)
     real = slot_ref[:, :PIX].astype(jnp.float32)
     imag = slot_ref[:, PIX:].astype(jnp.float32)
     table = lax.dot_general(
@@ -124,34 +156,26 @@
     rest = table - first
     second = rest.astype(jnp.bfloat16).astype(jnp.float32)
     third = rest - second
-    ext = jnp.concatenate([first, second, third, jnp.zeros_like(first)], axis=1)
-    for z in range(NZ):
-        rows = slice(8 * z, 8 * z + 8)
-        for ylo in range(2):
-            parts = []
-            for core in range(2):
-                start = core * HALF + ylo * QUART
-                stop = start + QUART
-                if stop <= FEAT:
-                    part = slot_ref[:, start:stop].astype(jnp.float32)[rows]
-                else:
-                    part = jnp.concatenate(
-                        [slot_ref[:, start:FEAT].astype(jnp.float32)[rows], ext[rows]], axis=1
-                    )
-                parts.append(part)
-            at = (z * 4 + ylo * 2) * 8
-            out_ref[at : at + 16, :] = jnp.concatenate(parts, axis=0).astype(jnp.bfloat16)
-
-
-def panel(owners, priors, slot, contrast, noise):
+    chunks(1, jnp.concatenate([first, second, third, jnp.zeros_like(first)], axis=1))
+
+
+def panel(owners, priors, slots, contrast, noise):
     return pl.pallas_call(
         panel_kernel,
         out_shape=jax.ShapeDtypeStruct((NDP * 8, QUART), jnp.bfloat16),
-        in_specs=[smem(), smem(), vmem(), vmem(), vmem()],
+        in_specs=[anywhere()] * 5,
         out_specs=vmem(),
-        compiler_params=params(24),
+        scratch_shapes=[
+            pltpu.SMEM((CLS,), jnp.int32),
+            pltpu.SMEM((CLS,), jnp.float32),
+            pltpu.VMEM((ROWS, FEAT), jnp.bfloat16),
+            pltpu.VMEM((GRP, PIX), jnp.float32),
+            pltpu.VMEM((PIX,), jnp.float32),
+            pltpu.SemaphoreType.DMA((5,)),
+        ],
+        compiler_params=params(60),
         name="panel",
-    )(owners, priors, slot, contrast, noise)
+    )(owners, priors, slots, contrast, noise)
 
 
 def pick_kernel(owners_ref, got_ref, out_ref, sems):
@@ -177,67 +201,35 @@
     )(owners, got)
 
 
-def scores_kernel(owners, n_panels, n_images, *refs):
-    panels, refs = refs[:n_panels], refs[n_panels:]
-    images, refs = refs[:n_images], refs[n_images:]
-    outs, (panel_buf, image_buf, panel_sems, image_sems) = refs[: len(owners)], refs[len(owners) :]
-
-    def panel_copies(chain):
-        at = 0
-        for ref in panels:
-            if ref.shape[0] == 1:
-                source = ref.at[0] if ref is panels[n_panels - 2 + chain] else None
+def scores_kernel(owners, plan, *refs):
+    n_panels = sum(count for _, count, _ in plan)
+    panels, images, outs = refs[:n_panels], refs[n_panels : n_panels + NOR], refs[n_panels + NOR :]
+    at = 0
+    for chain, count, first in plan:
+        panel = jnp.concatenate([ref[...] for ref in panels[at : at + count]], axis=0)
+        for owner, out in zip(owners, outs):
+            image = jnp.concatenate([ref[owner, chain] for ref in images], axis=0)
+            part = lax.dot_general(panel, image, NT, preferred_element_type=jnp.float32)
+            if at == 0:
+                out[...] = part
             else:
-                source = ref.at[chain]
-            if source is not None:
-                target = panel_buf.at[chain, CLS * 8 * at : CLS * 8 * (at + 1)]
-                yield pltpu.make_async_copy(source, target, panel_sems.at[chain, at])
-                at += 1
-
-    def image_copies(owner, slot, chain):
-        for at, ref in enumerate(images):
-            target = image_buf.at[slot, chain, ROWS * at : ROWS * (at + 1)]
-            yield pltpu.make_async_copy(
-                ref.at[owner, chain], target, image_sems.at[slot, chain, at]
-            )
-
-    def all_copies(slot, chain):
-        copies = list(image_copies(owners[slot], slot, chain))
-        return (list(panel_copies(chain)) if slot == 0 else []) + copies
-
-    order = [(slot, chain) for slot in range(len(owners)) for chain in range(2)]
-    for slot, chain in order:
-        for copy in all_copies(slot, chain):
-            copy.start()
-    for slot, chain in order:
-        for copy in all_copies(slot, chain):
-            copy.wait()
-        part = lax.dot_general(
-            panel_buf[chain], image_buf[slot, chain], NT, preferred_element_type=jnp.float32
-        )
-        if chain == 0:
-            outs[slot][...] = part
-        else:
-            outs[slot][...] += part
-
-
-def scores_of(panels, images, owners, blocks):
-    rows = blocks * CLS * 8
+                out[first : first + panel.shape[0]] += part
+        at += count
+
+
+def scores_of(panels, images, owners, plan):
+    rows = plan[0][1] * CLS * 8
     outs = len(owners)
     return pl.pallas_call(
-        functools.partial(scores_kernel, owners, len(panels), len(images)),
+        functools.partial(scores_kernel, owners, plan),
         out_shape=[jax.ShapeDtypeStruct((rows, GROUP_ROWS), jnp.float32)] * outs,
-        in_specs=[anywhere()] * (len(panels) + len(images)),
+        in_specs=[vmem()] * (len(panels) + NOR),
         out_specs=[vmem()] * outs,
-        scratch_shapes=[
-            pltpu.VMEM((2, rows, QUART), jnp.bfloat16),
-            pltpu.VMEM((outs, 2, GROUP_ROWS, QUART), jnp.bfloat16),
-            pltpu.SemaphoreType.DMA((2, blocks)),
-            pltpu.SemaphoreType.DMA((outs, 2, NOR)),
-        ],
-        compiler_params=params(20),
+        compiler_params=params(16),
         cost_estimate=pl.CostEstimate(
-            flops=2 * rows * GROUP_ROWS * HALF * outs, bytes_accessed=8 * MIB, transcendentals=0
+            flops=2 * len(panels) * CLS * 8 * GROUP_ROWS * QUART * outs,
+            bytes_accessed=8 * MIB,
+            transcendentals=0,
         ),
         name="scores",
     )(*panels, *images)
@@ -255,8 +247,13 @@
     _, _, _, x, yhi = place()
     near = near_ref[...] + near_other_ref[...]
     far = far_ref[...] + far_other_ref[...]
-    middle = 4 * CLS * 8
-    scores = jnp.concatenate([near[:middle], far, near[middle:]], axis=0)
+    step = CLS * 8
+    full, part = 5 * step, 7 * step
+    third = near[full : full + step] + far[:step]
+    fifth = near[full + step : part] + far[step : 2 * step]
+    scores = jnp.concatenate(
+        [near[: 3 * step], third, far[2 * step :], fifth, near[3 * step : full]], axis=0
+    )
     scores_ref[...] = scores
     scores = scores.reshape(NZ, CLS, 8, GROUP_ROWS)
     maximum = jnp.max(jnp.max(scores, axis=0), axis=1, keepdims=True)
@@ -293,7 +290,7 @@
     terms = jnp.exp(scores_ref[...] - here)
     ones = jnp.ones((NDP, GROUP_ROWS), jnp.float32)
     mass = lax.dot_general(ones, terms, NT, precision=HIGH, preferred_element_type=jnp.float32)
-    mass_ref[...] = pltpu.roll(mass, z * CLS * 8, 1)
+    mass_ref[...] = pltpu.roll(mass, z * CLS * 8, 1).reshape(mass_ref.shape)
 
 
 def finish(parts, scores):
@@ -302,7 +299,7 @@
         out_shape=(
             jax.ShapeDtypeStruct((1, GROUP_ROWS), jnp.float32),
             jax.ShapeDtypeStruct((CLS, GROUP_ROWS), jnp.float32),
-            jax.ShapeDtypeStruct((NDP, NZ * CLS * 8), jnp.float32),
+            jax.ShapeDtypeStruct((NDP, 1, NZ * CLS * 8), jnp.float32),
         ),
         in_specs=[vmem(), vmem()],
         out_specs=(vmem(), vmem(), vmem()),
@@ -319,41 +316,57 @@
     orient = lax.axis_index("orient")
     noise = noise_weight.reshape(1, PIX)
 
-    sent = panel(owners, class_prior, panel_slots[0], contrast, noise).reshape(NDP, 8, QUART)
+    sent = panel(owners, class_prior, panel_slots, contrast, noise_weight).reshape(NDP, 8, QUART)
     got = lax.all_to_all(sent, "dp", 0, 0)
 
     weighted = weigh(images, groups.reshape(ROWS, 1), contrast, noise)
     own = jnp.stack([weighted[0], other_core(weighted[1])])
-    across, left, right = other_yhi(own), from_left(own), from_right(own)
-
-    got, left, right, across = together(got, left, right, across)
-    mine = pick(owners, got)
+    left, right, across = from_left(own), from_right(own), other_yhi(own)
+
+    got, left, right = together(got, left, right)
     far = [from_left(left[:1]), from_right(right[1:])]
-    block = jnp.stack([mine, other_ylo(mine)]).reshape(2, CLS * 8, QUART)
-    up1, down1 = from_below(block), from_above(block)
-    up1, down1, across, *far = together(up1, down1, across, *far)
+    mine0 = pick(owners, got).reshape(CLS * 8, QUART)
+    mine1, mine7 = from_above(mine0), from_below(mine0)
+    theirs0 = other_ylo(mine0)
+
+    mine1, mine7, theirs0, across, *far = together(mine1, mine7, theirs0, across, *far)
+    pair1 = from_above(jnp.stack([mine1, theirs0]))
+    pair7 = from_below(jnp.stack([mine7, theirs0]))
     far = jnp.concatenate(far, axis=0)
     left_across, right_across, far_across = from_left(across), from_right(across), other_yhi(far)
-    up2, down2 = from_below(up1), from_above(down1)
-    up3, down3 = from_below(up2), from_above(down2)
-    up3, down3, left_across, right_across, far_across = together(
-        up3, down3, left_across, right_across, far_across
-    )
-    last = [from_below(up3[:1]), from_above(down3[1:])]
+    mine2, theirs1 = pair1
+    mine6, theirs7 = pair7
+    pair2, pair6 = from_above(pair1), from_below(pair7)
+
+    pair2, pair6, left_across, right_across, far_across = together(
+        pair2, pair6, left_across, right_across, far_across
+    )
+    mine3, theirs2 = pair2
+    mine5, theirs6 = pair6
+    half = CLS * 4
+    next3 = from_above(jnp.concatenate([mine3[half:], theirs2], axis=0))
+    next5 = from_below(jnp.concatenate([mine5[:half], theirs6], axis=0))
     whole = [own, across, right, right_across, far, far_across, left, left_across]
-
-    near = [block, down1, down2, down3, up3, up2, up1]
-    (near_theirs,) = scores_of(near, whole, (1,), 7)
+    near = [mine0, mine1, mine2, mine6, mine7, mine3, mine5]
+    near += [theirs0, theirs1, theirs2, theirs6, theirs7]
+    near_plan = ((0, 7, 0), (1, 5, 0))
+    (near_theirs,) = scores_of(near, whole, (1,), near_plan)
     near_other = other_core(near_theirs)
-    (near_mine,) = scores_of(near, whole, (0,), 7)
+    (near_mine,) = scores_of(near, whole, (0,), near_plan)
+    theirs3, theirs5 = next3[half:], next5[half:]
+    last = [from_below(theirs5[:half]), from_above(theirs3[half:])]
     near_mine, *last = together(near_mine, *last)
-    far_theirs, far_mine = scores_of(last, whole, (1, 0), 1)
+    mine4 = jnp.concatenate([next5[:half], next3[:half]], axis=0)
+    theirs4 = jnp.concatenate(last, axis=0)
+    far_theirs, far_mine = scores_of(
+        [theirs3, theirs5, theirs4, mine4], whole, (1, 0), ((1, 3, 0), (0, 1, 2 * CLS * 8))
+    )
     scores, partial = norms(near_mine, near_other, far_mine, other_core(far_theirs))
     parts = lax.all_to_all(partial, "orient", 0, 0)
     evidence, posterior, mass = finish(parts, scores)
     masses = lax.all_to_all(mass, "dp", 0, 0)
     normalise = CLS * ORI * NOR / (ROWS * NOR * NDP)
-    total = jnp.sum(masses, axis=0) * normalise
+    total = jnp.sum(masses, axis=(0, 1)) * normalise
     orientation_mass = total.reshape(NZ, CLS, 8).transpose(1, 0, 2).reshape(CLS, ORI)
     log_evidence = lax.dynamic_slice_in_dim(evidence[0], orient * ROWS, ROWS, 0)
     class_posterior = lax.dynamic_slice_in_dim(posterior, orient * ROWS, ROWS, 1)

time: 170 us -> 156 us (0.918)
  waiting for transfers between devices: 86.1 us -> 74.9 us
  local copies, waits for them, and re-layouts: 7.64 us -> 2.69 us
    ppermute x20 -> x22, waiting for transfers between devices: 72.1 us -> 61.1 us  [permute(): return lax.ppermute(array, ('dp', 'orient'), pairs)]
    unnamed x17 -> x11, local copies, waits for them, and re-layouts: 3.83 us -> 0.07 us
    pallas_call x3, Pallas kernels: 12.4 us -> 10.7 us  [scores_of(): pl.pallas_call(functools.partial(scores_kernel, owners, plan), out_shape=...]
    ppermute x20 -> x22, starting transfers between devices: 32.2 us -> 33.9 us  [permute(): return lax.ppermute(array, ('dp', 'orient'), pairs)]
  transfers between devices with their start and end apart: 23 -> 25, of which waited for: 14 -> 13; matrix products, arithmetic and copies ran while one was open for 1% -> 1% of each run, Pallas kernels for 6% -> 9%
where the time goes in v3:
time: 156 us; the launch traced here: 155 us
  waiting for transfers between devices  74.9 us (48%)
  starting transfers between devices  55.6 us (36%)
  Pallas kernels  20.5 us (13%)
  local copies, waits for them, and re-layouts  2.69 us (2%)
    ppermute x22, waiting for transfers between devices, permute(): return lax.ppermute(array, ('dp', 'orient'), pairs)  61.1 us
    ppermute x22, starting transfers between devices, permute(): return lax.ppermute(array, ('dp', 'orient'), pairs)  33.9 us
    all_to_all x1, starting transfers between devices, per_device(): got = lax.all_to_all(sent, 'dp', 0, 0)  11.3 us
    pallas_call x3, Pallas kernels, scores_of(): pl.pallas_call(functools.partial(scores_kernel, owners, plan), out_shape=...  10.7 us
    all_to_all x1, waiting for transfers between devices, per_device(): masses = lax.all_to_all(mass, 'dp', 0, 0)  7.07 us
    all_to_all x1, starting transfers between devices, per_device(): masses = lax.all_to_all(mass, 'dp', 0, 0)  7.06 us
    all_to_all x1, waiting for transfers between devices, per_device(): parts = lax.all_to_all(partial, 'orient', 0, 0)  6.74 us
    pallas_call x1, Pallas kernels, panel(): pl.pallas_call(panel_kernel, out_shape=jax.ShapeDtypeStruct((NDP * 8, QUA...  3.81 us
  transfers between devices with their start and end apart: 25, of which 13 were waited for; matrix products, arithmetic and copies ran while one was open for 1% of the time, Pallas kernels for 9%

profile of v3, /device:TPU:1, one launch (start us, length us, event | category | flops | bytes accessed | tf_op | source)
XLA Modules:
  0.0 155.0 jit_solution(547488042756633096)
XLA Ops:
  0.6 3.8 %panel.1 = bf16[256,2176]{1,0:T(8,128)(2,1)} custom-call(s32[8]{0:T(128)} %owners_ref.1, f32[8]{0:T(128)} %priors_hbm.1, bf16[1,64,8448]{2,1,0:T(8,128)(2,1)} %slot_hbm.1, f32[64,4224]{1,0:T(8,128)} %contrast_ref.1, f32[4224]{0:T(1024)} %noise_hbm.1), custom_call_target="tpu_custom_call" | custom-call | tf_op jit(solution)/shard_map/panel/pallas_call | solution.py:163
  4.5 11.3 %all-to-all-start = ((bf16[32,8,2176]{2,1,0:T(8,128)(2,1)}), bf16[32,8,2176]{2,1,0:T(8,128)(2,1)}, u32[]{:S(2)}, u32[]{:S(2)}) async-start(bf16[32,8,2176]{2,1,0:T(8,128)(2,1)} %bitcast.40), calls=%async_computation | async-start | bytes 2228224 | tf_op jit(solution)/shard_map/all_to_all | solution.py:320
  15.9 0.1 copy.12.groups_ref
  16.0 1.1 weigh.1
  17.2 0.4 collective-permute-start
  17.6 1.7 %collective-permute-done = bf16[2,64,2176]{2,1,0:T(8,128)(2,1)S(1)} collective-permute-done((bf16[2,64,2176]{2,1,0:T(8,128)(2,1)S(1)}, bf16[2,64,2176]{2,1,0:T(8,128)(2,1)S(1)}, u32[]{:S(2)}, u32[]{:S(2)}) %collective-permute-start) | collective-permute-done | bytes 557088 | tf_op jit(solution)/shard_map/ppermute | solution.py:31
  19.3 0.1 pad_maximum_fusion.refs_12_.refs_4_
  19.4 1.3 collective-permute-start.1
  20.7 1.5 collective-permute-start.2
  22.1 2.6 %collective-permute-start.6 = (bf16[2,2,64,2176]{3,2,1,0:T(8,128)(2,1)S(1)}, bf16[2,2,64,2176]{3,2,1,0:T(8,128)(2,1)}, u32[]{:S(2)}, u32[]{:S(2)}) collective-permute-start(bf16[2,2,64,2176]{3,2,1,0:T(8,128)(2,1)S(1)} %pad_maximum_fusion.refs_12_.refs_4_), channel_id=1, source_target_pairs={{0,1},{1,0},{2,3},{3,2},{4,5},{5,4},{6,7},{7,6},{8,9},{9,8},{10,11... | collective-permute-start | bytes 3342344 | tf_op jit(solution)/shard_map/ppermute | solution.py:31
  24.8 21.9 %collective-permute-done.1.refs_18_.refs_10_ = bf16[2,2,64,2176]{3,2,1,0:T(8,128)(2,1)S(1)} collective-permute-done((bf16[2,2,64,2176]{3,2,1,0:T(8,128)(2,1)S(1)}, bf16[2,2,64,2176]{3,2,1,0:T(8,128)(2,1)S(1)}, u32[]{:S(2)}, u32[]{:S(2)}) %collective-permute-start.1) | collective-permute-done | bytes 1114144 | tf_op jit(solution)/shard_map/ppermute | solution.py:31
  46.7 1.0 collective-permute-start.7
  47.7 1.9 %collective-permute-start.8 = (bf16[1,2,64,2176]{3,2,1,0:T(8,128)(2,1)S(1)}, bf16[1,2,64,2176]{3,2,1,0:T(8,128)(2,1)S(1)}, u32[]{:S(2)}, u32[]{:S(2)}) collective-permute-start(bf16[1,2,64,2176]{3,2,1,0:T(8,128)(2,1)S(1)} %slice.49), channel_id=1, source_target_pairs={{0,6},{1,7},{2,0},{3,1},{4,2},{5,3},{6,4},{7,5},{8,14},{9,15},{10,... | collective-permute-start | bytes 1671176 | tf_op jit(solution)/shard_map/ppermute | solution.py:31
  49.6 1.5 pick.1
  51.1 2.7 %collective-permute-start.3 = (bf16[64,2176]{1,0:T(8,128)(2,1)S(1)}, bf16[64,2176]{1,0:T(8,128)(2,1)S(1)}, u32[]{:S(2)}, u32[]{:S(2)}) collective-permute-start(bf16[64,2176]{1,0:T(8,128)(2,1)S(1)} %bitcast.32), channel_id=1, source_target_pairs={{0,224},{1,225},{2,226},{3,227},{4,228},{5,229},{6,230},{7,231},{8... | collective-permute-start | bytes 835592 | tf_op jit(solution)/shard_map/ppermute | solution.py:31
  53.7 4.2 %collective-permute-done.6.refs_13_.refs_5_ = bf16[2,2,64,2176]{3,2,1,0:T(8,128)(2,1)} collective-permute-done((bf16[2,2,64,2176]{3,2,1,0:T(8,128)(2,1)S(1)}, bf16[2,2,64,2176]{3,2,1,0:T(8,128)(2,1)}, u32[]{:S(2)}, u32[]{:S(2)}) %collective-permute-start.6) | collective-permute-done | bytes 1114144 | tf_op jit(solution)/shard_map/ppermute | solution.py:31
  57.9 1.4 collective-permute-start.5
  59.3 1.9 %collective-permute-done.4.refs_4_ = bf16[64,2176]{1,0:T(8,128)(2,1)S(1)} collective-permute-done((bf16[64,2176]{1,0:T(8,128)(2,1)S(1)}, bf16[64,2176]{1,0:T(8,128)(2,1)S(1)}, u32[]{:S(2)}, u32[]{:S(2)}) %collective-permute-start.4) | collective-permute-done | bytes 278560 | tf_op jit(solution)/shard_map/ppermute | solution.py:31
  61.2 4.1 %collective-permute-done.5.refs_7_ = bf16[64,2176]{1,0:T(8,128)(2,1)S(1)} collective-permute-done((bf16[64,2176]{1,0:T(8,128)(2,1)S(1)}, bf16[64,2176]{1,0:T(8,128)(2,1)S(1)}, u32[]{:S(2)}, u32[]{:S(2)}) %collective-permute-start.5) | collective-permute-done | bytes 278560 | tf_op jit(solution)/shard_map/ppermute | solution.py:31
  65.3 1.5 collective-permute-start.13
  66.8 1.4 collective-permute-start.14
  68.2 0.1 pad_maximum_fusion.1
  68.3 2.2 %collective-permute-start.9 = (bf16[2,64,2176]{2,1,0:T(8,128)(2,1)S(1)}, bf16[2,64,2176]{2,1,0:T(8,128)(2,1)S(1)}, u32[]{:S(2)}, u32[]{:S(2)}) collective-permute-start(bf16[2,64,2176]{2,1,0:T(8,128)(2,1)S(1)} %get-tuple-element.66), channel_id=1, source_target_pairs={{0,224},{1,225},{2,226},{3,227},{4,228},{5,229},{6,230},{7,231},{8... | collective-permute-start | bytes 1671176 | tf_op jit(solution)/shard_map/ppermute | solution.py:31
  70.7 2.3 %collective-permute-start.15 = (bf16[2,2,64,2176]{3,2,1,0:T(8,128)(2,1)S(1)}, bf16[2,2,64,2176]{3,2,1,0:T(8,128)(2,1)S(1)}, u32[]{:S(2)}, u32[]{:S(2)}) collective-permute-start(bf16[2,2,64,2176]{3,2,1,0:T(8,128)(2,1)S(1)} %constant_dynamic-update-slice_fusion.refs_16_.refs_8_), channel_id=1, source_target_pairs={{0,1},{1,0},{2,3},{3,2},{4,5},{5,4},{6,7},{7,6},{8,9},{9,8},{10,11... | collective-permute-start | bytes 3342344 | tf_op jit(solution)/shard_map/ppermute | solution.py:31
  73.0 7.7 %collective-permute-done.9 = bf16[2,64,2176]{2,1,0:T(8,128)(2,1)S(1)} collective-permute-done((bf16[2,64,2176]{2,1,0:T(8,128)(2,1)S(1)}, bf16[2,64,2176]{2,1,0:T(8,128)(2,1)S(1)}, u32[]{:S(2)}, u32[]{:S(2)}) %collective-permute-start.9) | collective-permute-done | bytes 557088 | tf_op jit(solution)/shard_map/ppermute | solution.py:31
  80.7 3.4 %collective-permute-start.11 = (bf16[2,64,2176]{2,1,0:T(8,128)(2,1)S(1)}, bf16[2,64,2176]{2,1,0:T(8,128)(2,1)S(1)}, u32[]{:S(2)}, u32[]{:S(2)}) collective-permute-start(bf16[2,64,2176]{2,1,0:T(8,128)(2,1)S(1)} %collective-permute-done.9), channel_id=1, source_target_pairs={{0,224},{1,225},{2,226},{3,227},{4,228},{5,229},{6,230},{7,231},{8... | collective-permute-start | bytes 1671176 | tf_op jit(solution)/shard_map/ppermute | solution.py:31
  84.2 12.0 %collective-permute-done.15.refs_17_.refs_9_ = bf16[2,2,64,2176]{3,2,1,0:T(8,128)(2,1)S(1)} collective-permute-done((bf16[2,2,64,2176]{3,2,1,0:T(8,128)(2,1)S(1)}, bf16[2,2,64,2176]{3,2,1,0:T(8,128)(2,1)S(1)}, u32[]{:S(2)}, u32[]{:S(2)}) %collective-permute-start.15) | collective-permute-done | bytes 1114144 | tf_op jit(solution)/shard_map/ppermute | solution.py:31
  96.2 0.2 collective-permute-done.12
  96.6 2.3 %collective-permute-start.18 = (bf16[96,2176]{1,0:T(8,128)(2,1)S(1)}, bf16[96,2176]{1,0:T(8,128)(2,1)S(1)}, u32[]{:S(2)}, u32[]{:S(2)}) collective-permute-start(bf16[96,2176]{1,0:T(8,128)(2,1)S(1)} %pad_maximum_fusion.4), channel_id=1, source_target_pairs={{0,224},{1,225},{2,226},{3,227},{4,228},{5,229},{6,230},{7,231},{8... | collective-permute-start | bytes 1253384 | tf_op jit(solution)/shard_map/ppermute | solution.py:31
  99.0 3.3 %scores.4 = f32[448,512]{1,0:T(8,128)S(1)} custom-call(bf16[64,2176]{1,0:T(8,128)(2,1)S(1)} %bitcast.35, bf16[64,2176]{1,0:T(8,128)(2,1)S(1)} %collective-permute-done.3.refs_1_, bf16[64,2176]{1,0:T(8,128)(2,1)S(1)} %get-tuple-element.60.refs_2_, bf16[64,2176]{1,0:T(8,128)(2,1)S(1)} %get-tuple-element.54.refs_3_, ...), custom_call_target="tpu_custom_call" | custom-call | flops 1711276032 | bytes 8388608 | tf_op jit(solution)/shard_map/scores/pallas_call | solution.py:223
  102.3 3.8 %collective-permute-start.20 = (f32[448,512]{1,0:T(8,128)S(1)}, f32[448,512]{1,0:T(8,128)S(1)}, u32[]{:S(2)}, u32[]{:S(2)}) collective-permute-start(f32[448,512]{1,0:T(8,128)S(1)} %scores.4), channel_id=1, source_target_pairs={{0,8},{1,9},{2,10},{3,11},{4,12},{5,13},{6,14},{7,15},{8,0},{9,1},... | collective-permute-start | bytes 2752520 | tf_op jit(solution)/shard_map/ppermute | solution.py:31
  106.1 3.3 %scores.3.near_ref = f32[448,512]{1,0:T(8,128)S(1)} custom-call(bf16[64,2176]{1,0:T(8,128)(2,1)S(1)} %bitcast.36, bf16[64,2176]{1,0:T(8,128)(2,1)S(1)} %collective-permute-done.3.refs_1_, bf16[64,2176]{1,0:T(8,128)(2,1)S(1)} %get-tuple-element.60.refs_2_, bf16[64,2176]{1,0:T(8,128)(2,1)S(1)} %get-tuple-element.54.refs_3_, ...), custom_call_target="tpu_custom_call" | custom-call | flops 1711276032 | bytes 8388608 | tf_op jit(solution)/shard_map/scores/pallas_call | solution.py:223
  109.4 2.9 %collective-permute-start.19 = (bf16[32,2176]{1,0:T(8,128)(2,1)S(1)}, bf16[32,2176]{1,0:T(8,128)(2,1)S(1)}, u32[]{:S(2)}, u32[]{:S(2)}) collective-permute-start(bf16[32,2176]{1,0:T(8,128)(2,1)S(1)} %get-tuple-element.64), channel_id=1, source_target_pairs={{0,224},{1,225},{2,226},{3,227},{4,228},{5,229},{6,230},{7,231},{8... | collective-permute-start | bytes 417800 | tf_op jit(solution)/shard_map/ppermute | solution.py:31
  112.5 2.9 %collective-permute-done.19 = bf16[32,2176]{1,0:T(8,128)(2,1)S(1)} collective-permute-done((bf16[32,2176]{1,0:T(8,128)(2,1)S(1)}, bf16[32,2176]{1,0:T(8,128)(2,1)S(1)}, u32[]{:S(2)}, u32[]{:S(2)}) %collective-permute-start.19) | collective-permute-done | bytes 139296 | tf_op jit(solution)/shard_map/ppermute | solution.py:31
  115.4 3.2 %collective-permute-done.17 = bf16[32,2176]{1,0:T(8,128)(2,1)S(1)} collective-permute-done((bf16[32,2176]{1,0:T(8,128)(2,1)S(1)}, bf16[32,2176]{1,0:T(8,128)(2,1)S(1)}, u32[]{:S(2)}, u32[]{:S(2)}) %collective-permute-start.17) | collective-permute-done | bytes 139296 | tf_op jit(solution)/shard_map/ppermute | solution.py:31
  118.6 4.1 %scores.5 = (f32[192,512]{1,0:T(8,128)S(1)}, f32[192,512]{1,0:T(8,128)S(1)}) custom-call(bf16[64,2176]{1,0:T(8,128)(2,1)S(1)} %slice.64.refs_0_, bf16[64,2176]{1,0:T(8,128)(2,1)S(1)} %slice.65.refs_1_, bf16[64,2176]{1,0:T(8,128)(2,1)S(1)} %pad_maximum_fusion.5.refs_2_, bf16[64,2176]{1,0:T(8,128)(2,1)S(1)} %pad_maximum_fusion.6.refs_3_, ...), custom_call_target="tpu_custom_call" | custom-call | flops 1140850688 | bytes 8388608 | tf_op jit(solution)/shard_map/scores/pallas_call | solution.py:223
  122.7 1.2 collective-permute-start.21
  123.9 1.3 collective-permute-done.21.far_other_ref
  125.3 1.4 norms.1
  126.7 3.4 %all-to-all-start.1 = ((f32[8,8,512]{2,1,0:T(8,128)}), f32[8,8,512]{2,1,0:T(8,128)S(1)}, u32[]{:S(2)}, u32[]{:S(2)}) async-start(f32[8,8,512]{2,1,0:T(8,128)} %get-tuple-element.46), calls=%async_computation.1 | async-start | bytes 262144 | tf_op jit(solution)/shard_map/all_to_all | solution.py:365
  130.1 6.7 %all-to-all-done.1.parts_ref = f32[8,8,512]{2,1,0:T(8,128)S(1)} async-done(((f32[8,8,512]{2,1,0:T(8,128)}), f32[8,8,512]{2,1,0:T(8,128)S(1)}, u32[]{:S(2)}, u32[]{:S(2)}) %all-to-all-start.1) | async-done | bytes 131104 | tf_op jit(solution)/shard_map/all_to_all | solution.py:365
  136.8 2.0 %finish.1 = (f32[1,512]{1,0:T(1,128)S(1)}, f32[8,512]{1,0:T(8,128)S(1)}, f32[32,1,512]{2,1,0:T(1,128)}) custom-call(f32[8,8,512]{2,1,0:T(8,128)S(1)} %all-to-all-done.1.parts_ref, f32[512,512]{1,0:T(8,128)S(1)} %get-tuple-element.47.scores_ref), custom_call_target="tpu_custom_call" | custom-call | tf_op jit(solution)/shard_map/finish/pallas_call | solution.py:297
  138.8 7.1 %all-to-all-start.2 = ((f32[32,1,512]{2,1,0:T(1,128)}), f32[32,1,512]{2,1,0:T(1,128)S(1)}, u32[]{:S(2)}, u32[]{:S(2)}) async-start(f32[32,1,512]{2,1,0:T(1,128)} %get-tuple-element.50), calls=%async_computation.2 | async-start | bytes 131072 | tf_op jit(solution)/shard_map/all_to_all | solution.py:367
  145.9 0.6 dynamic-slice_bitcast_fusion
  146.5 0.7 constant_dynamic-slice_fusion
  147.1 7.1 %all-to-all-done.2 = f32[32,1,512]{2,1,0:T(1,128)S(1)} async-done(((f32[32,1,512]{2,1,0:T(1,128)}), f32[32,1,512]{2,1,0:T(1,128)S(1)}, u32[]{:S(2)}, u32[]{:S(2)}) %all-to-all-start.2) | async-done | bytes 65568 | tf_op jit(solution)/shard_map/all_to_all | solution.py:367
  154.3 0.1 mul.17
  154.4 0.7 reshape.32
  (50 shorter events, 1.0 us)
Async XLA Ops:
  4.4 11.4 %copy-start.3 = (f32[4224]{0:T(1024)S(1)}, f32[4224]{0:T(1024)}, u32[]{:S(2)}) copy-start(f32[4224]{0:T(1024)} %noise_hbm.1) | copy-start | bytes 50692
  4.5 11.4 %copy-start.4 = (s32[64]{0:T(128)S(1)}, s32[64]{0:T(128)}, u32[]{:S(2)}) copy-start(s32[64]{0:T(128)} %param.8) | copy-start | bytes 772
  4.5 11.5 %copy-start = (f32[64,4224]{1,0:T(8,128)S(1)}, f32[64,4224]{1,0:T(8,128)}, u32[]{:S(2)}) copy-start(f32[64,4224]{1,0:T(8,128)} %contrast_ref.1) | copy-start | bytes 3244036
  4.5 11.5 %copy-start.1 = (bf16[64,8448]{1,0:T(8,128)(2,1)S(1)}, bf16[64,8448]{1,0:T(8,128)(2,1)}, u32[]{:S(2)}) copy-start(bf16[64,8448]{1,0:T(8,128)(2,1)} %images_ref.1) | copy-start | bytes 3244036
  4.5 42.1 %all-to-all-start = ((bf16[32,8,2176]{2,1,0:T(8,128)(2,1)}), bf16[32,8,2176]{2,1,0:T(8,128)(2,1)}, u32[]{:S(2)}, u32[]{:S(2)}) async-start(bf16[32,8,2176]{2,1,0:T(8,128)(2,1)} %bitcast.40), calls=%async_computation | async-start | bytes 2228224 | tf_op jit(solution)/shard_map/all_to_all | solution.py:320
  17.2 2.0 %collective-permute-start = (bf16[2,64,2176]{2,1,0:T(8,128)(2,1)S(1)}, bf16[2,64,2176]{2,1,0:T(8,128)(2,1)S(1)}, u32[]{:S(2)}, u32[]{:S(2)}) collective-permute-start(bf16[2,64,2176]{2,1,0:T(8,128)(2,1)S(1)} %get-tuple-element.52), channel_id=1, source_target_pairs={{0,8},{1,9},{2,10},{3,11},{4,12},{5,13},{6,14},{7,15},{8,0},{9,1},... | collective-permute-start | bytes 1671176 | tf_op jit(solution)/shard_map/ppermute | solution.py:31
  19.4 30.2 %copy-start.2 = (s32[8]{0:T(128)S(1)}, s32[8]{0:T(128)}, u32[]{:S(2)}) copy-start(s32[8]{0:T(128)} %owners_ref.1) | copy-start | bytes 100
  19.4 27.3 %collective-permute-start.1 = (bf16[2,2,64,2176]{3,2,1,0:T(8,128)(2,1)S(1)}, bf16[2,2,64,2176]{3,2,1,0:T(8,128)(2,1)S(1)}, u32[]{:S(2)}, u32[]{:S(2)}) collective-permute-start(bf16[2,2,64,2176]{3,2,1,0:T(8,128)(2,1)S(1)} %pad_maximum_fusion.refs_12_.refs_4_), channel_id=1, source_target_pairs={{0,2},{1,3},{2,4},{3,5},{4,6},{5,7},{6,0},{7,1},{8,10},{9,11},{10,... | collective-permute-start | bytes 3342344 | tf_op jit(solution)/shard_map/ppermute | solution.py:31
  20.7 26.0 %collective-permute-start.2 = (bf16[2,2,64,2176]{3,2,1,0:T(8,128)(2,1)S(1)}, bf16[2,2,64,2176]{3,2,1,0:T(8,128)(2,1)S(1)}, u32[]{:S(2)}, u32[]{:S(2)}) collective-permute-start(bf16[2,2,64,2176]{3,2,1,0:T(8,128)(2,1)S(1)} %pad_maximum_fusion.refs_12_.refs_4_), channel_id=1, source_target_pairs={{0,6},{1,7},{2,0},{3,1},{4,2},{5,3},{6,4},{7,5},{8,14},{9,15},{10,... | collective-permute-start | bytes 3342344 | tf_op jit(solution)/shard_map/ppermute | solution.py:31
  22.1 35.8 %collective-permute-start.6 = (bf16[2,2,64,2176]{3,2,1,0:T(8,128)(2,1)S(1)}, bf16[2,2,64,2176]{3,2,1,0:T(8,128)(2,1)}, u32[]{:S(2)}, u32[]{:S(2)}) collective-permute-start(bf16[2,2,64,2176]{3,2,1,0:T(8,128)(2,1)S(1)} %pad_maximum_fusion.refs_12_.refs_4_), channel_id=1, source_target_pairs={{0,1},{1,0},{2,3},{3,2},{4,5},{5,4},{6,7},{7,6},{8,9},{9,8},{10,11... | collective-permute-start | bytes 3342344 | tf_op jit(solution)/shard_map/ppermute | solution.py:31
  46.7 18.6 %collective-permute-start.7 = (bf16[1,2,64,2176]{3,2,1,0:T(8,128)(2,1)S(1)}, bf16[1,2,64,2176]{3,2,1,0:T(8,128)(2,1)S(1)}, u32[]{:S(2)}, u32[]{:S(2)}) collective-permute-start(bf16[1,2,64,2176]{3,2,1,0:T(8,128)(2,1)S(1)} %slice.48), channel_id=1, source_target_pairs={{0,2},{1,3},{2,4},{3,5},{4,6},{5,7},{6,0},{7,1},{8,10},{9,11},{10,... | collective-permute-start | bytes 1671176 | tf_op jit(solution)/shard_map/ppermute | solution.py:31
  47.7 17.6 %collective-permute-start.8 = (bf16[1,2,64,2176]{3,2,1,0:T(8,128)(2,1)S(1)}, bf16[1,2,64,2176]{3,2,1,0:T(8,128)(2,1)S(1)}, u32[]{:S(2)}, u32[]{:S(2)}) collective-permute-start(bf16[1,2,64,2176]{3,2,1,0:T(8,128)(2,1)S(1)} %slice.49), channel_id=1, source_target_pairs={{0,6},{1,7},{2,0},{3,1},{4,2},{5,3},{6,4},{7,5},{8,14},{9,15},{10,... | collective-permute-start | bytes 1671176 | tf_op jit(solution)/shard_map/ppermute | solution.py:31
  51.1 8.2 %collective-permute-start.3 = (bf16[64,2176]{1,0:T(8,128)(2,1)S(1)}, bf16[64,2176]{1,0:T(8,128)(2,1)S(1)}, u32[]{:S(2)}, u32[]{:S(2)}) collective-permute-start(bf16[64,2176]{1,0:T(8,128)(2,1)S(1)} %bitcast.32), channel_id=1, source_target_pairs={{0,224},{1,225},{2,226},{3,227},{4,228},{5,229},{6,230},{7,231},{8... | collective-permute-start | bytes 835592 | tf_op jit(solution)/shard_map/ppermute | solution.py:31
  53.7 7.4 %collective-permute-start.4 = (bf16[64,2176]{1,0:T(8,128)(2,1)S(1)}, bf16[64,2176]{1,0:T(8,128)(2,1)S(1)}, u32[]{:S(2)}, u32[]{:S(2)}) collective-permute-start(bf16[64,2176]{1,0:T(8,128)(2,1)S(1)} %bitcast.33), channel_id=1, source_target_pairs={{0,32},{1,33},{2,34},{3,35},{4,36},{5,37},{6,38},{7,39},{8,40},{9,... | collective-permute-start | bytes 835592 | tf_op jit(solution)/shard_map/ppermute | solution.py:31
  57.9 7.4 %collective-permute-start.5 = (bf16[64,2176]{1,0:T(8,128)(2,1)S(1)}, bf16[64,2176]{1,0:T(8,128)(2,1)S(1)}, u32[]{:S(2)}, u32[]{:S(2)}) collective-permute-start(bf16[64,2176]{1,0:T(8,128)(2,1)S(1)} %bitcast.34), channel_id=1, source_target_pairs={{0,16},{1,17},{2,18},{3,19},{4,20},{5,21},{6,22},{7,23},{8,24},{9,... | collective-permute-start | bytes 835592 | tf_op jit(solution)/shard_map/ppermute | solution.py:31
  65.3 31.1 %collective-permute-start.13 = (bf16[2,2,64,2176]{3,2,1,0:T(8,128)(2,1)}, bf16[2,2,64,2176]{3,2,1,0:T(8,128)(2,1)S(1)}, u32[]{:S(2)}, u32[]{:S(2)}) collective-permute-start(bf16[2,2,64,2176]{3,2,1,0:T(8,128)(2,1)} %collective-permute-done.6.refs_13_.refs_5_), channel_id=1, source_target_pairs={{0,2},{1,3},{2,4},{3,5},{4,6},{5,7},{6,0},{7,1},{8,10},{9,11},{10,... | collective-permute-start | bytes 3342344 | tf_op jit(solution)/shard_map/ppermute | solution.py:31
  66.8 29.6 %collective-permute-start.14 = (bf16[2,2,64,2176]{3,2,1,0:T(8,128)(2,1)}, bf16[2,2,64,2176]{3,2,1,0:T(8,128)(2,1)S(1)}, u32[]{:S(2)}, u32[]{:S(2)}) collective-permute-start(bf16[2,2,64,2176]{3,2,1,0:T(8,128)(2,1)} %collective-permute-done.6.refs_13_.refs_5_), channel_id=1, source_target_pairs={{0,6},{1,7},{2,0},{3,1},{4,2},{5,3},{6,4},{7,5},{8,14},{9,15},{10,... | collective-permute-start | bytes 3342344 | tf_op jit(solution)/shard_map/ppermute | solution.py:31
  68.3 12.4 %collective-permute-start.9 = (bf16[2,64,2176]{2,1,0:T(8,128)(2,1)S(1)}, bf16[2,64,2176]{2,1,0:T(8,128)(2,1)S(1)}, u32[]{:S(2)}, u32[]{:S(2)}) collective-permute-start(bf16[2,64,2176]{2,1,0:T(8,128)(2,1)S(1)} %get-tuple-element.66), channel_id=1, source_target_pairs={{0,224},{1,225},{2,226},{3,227},{4,228},{5,229},{6,230},{7,231},{8... | collective-permute-start | bytes 1671176 | tf_op jit(solution)/shard_map/ppermute | solution.py:31
  70.5 13.5 %collective-permute-start.10 = (bf16[2,64,2176]{2,1,0:T(8,128)(2,1)S(1)}, bf16[2,64,2176]{2,1,0:T(8,128)(2,1)S(1)}, u32[]{:S(2)}, u32[]{:S(2)}) collective-permute-start(bf16[2,64,2176]{2,1,0:T(8,128)(2,1)S(1)} %get-tuple-element.65), channel_id=1, source_target_pairs={{0,32},{1,33},{2,34},{3,35},{4,36},{5,37},{6,38},{7,39},{8,40},{9,... | collective-permute-start | bytes 1671176 | tf_op jit(solution)/shard_map/ppermute | solution.py:31
  70.7 25.6 %collective-permute-start.15 = (bf16[2,2,64,2176]{3,2,1,0:T(8,128)(2,1)S(1)}, bf16[2,2,64,2176]{3,2,1,0:T(8,128)(2,1)S(1)}, u32[]{:S(2)}, u32[]{:S(2)}) collective-permute-start(bf16[2,2,64,2176]{3,2,1,0:T(8,128)(2,1)S(1)} %constant_dynamic-update-slice_fusion.refs_16_.refs_8_), channel_id=1, source_target_pairs={{0,1},{1,0},{2,3},{3,2},{4,5},{5,4},{6,7},{7,6},{8,9},{9,8},{10,11... | collective-permute-start | bytes 3342344 | tf_op jit(solution)/shard_map/ppermute | solution.py:31
  80.7 15.6 %collective-permute-start.11 = (bf16[2,64,2176]{2,1,0:T(8,128)(2,1)S(1)}, bf16[2,64,2176]{2,1,0:T(8,128)(2,1)S(1)}, u32[]{:S(2)}, u32[]{:S(2)}) collective-permute-start(bf16[2,64,2176]{2,1,0:T(8,128)(2,1)S(1)} %collective-permute-done.9), channel_id=1, source_target_pairs={{0,224},{1,225},{2,226},{3,227},{4,228},{5,229},{6,230},{7,231},{8... | collective-permute-start | bytes 1671176 | tf_op jit(solution)/shard_map/ppermute | solution.py:31
  84.1 12.3 %collective-permute-start.12 = (bf16[2,64,2176]{2,1,0:T(8,128)(2,1)S(1)}, bf16[2,64,2176]{2,1,0:T(8,128)(2,1)S(1)}, u32[]{:S(2)}, u32[]{:S(2)}) collective-permute-start(bf16[2,64,2176]{2,1,0:T(8,128)(2,1)S(1)} %collective-permute-done.10), channel_id=1, source_target_pairs={{0,32},{1,33},{2,34},{3,35},{4,36},{5,37},{6,38},{7,39},{8,40},{9,... | collective-permute-start | bytes 1671176 | tf_op jit(solution)/shard_map/ppermute | solution.py:31
  96.6 12.8 %collective-permute-start.18 = (bf16[96,2176]{1,0:T(8,128)(2,1)S(1)}, bf16[96,2176]{1,0:T(8,128)(2,1)S(1)}, u32[]{:S(2)}, u32[]{:S(2)}) collective-permute-start(bf16[96,2176]{1,0:T(8,128)(2,1)S(1)} %pad_maximum_fusion.4), channel_id=1, source_target_pairs={{0,224},{1,225},{2,226},{3,227},{4,228},{5,229},{6,230},{7,231},{8... | collective-permute-start | bytes 1253384 | tf_op jit(solution)/shard_map/ppermute | solution.py:31
  98.9 13.3 %collective-permute-start.16 = (bf16[96,2176]{1,0:T(8,128)(2,1)S(1)}, bf16[96,2176]{1,0:T(8,128)(2,1)S(1)}, u32[]{:S(2)}, u32[]{:S(2)}) collective-permute-start(bf16[96,2176]{1,0:T(8,128)(2,1)S(1)} %pad_maximum_fusion.3), channel_id=1, source_target_pairs={{0,32},{1,33},{2,34},{3,35},{4,36},{5,37},{6,38},{7,39},{8,40},{9,... | collective-permute-start | bytes 1253384 | tf_op jit(solution)/shard_map/ppermute | solution.py:31
  102.3 21.6 %collective-permute-start.20 = (f32[448,512]{1,0:T(8,128)S(1)}, f32[448,512]{1,0:T(8,128)S(1)}, u32[]{:S(2)}, u32[]{:S(2)}) collective-permute-start(f32[448,512]{1,0:T(8,128)S(1)} %scores.4), channel_id=1, source_target_pairs={{0,8},{1,9},{2,10},{3,11},{4,12},{5,13},{6,14},{7,15},{8,0},{9,1},... | collective-permute-start | bytes 2752520 | tf_op jit(solution)/shard_map/ppermute | solution.py:31
  109.4 5.9 %collective-permute-start.19 = (bf16[32,2176]{1,0:T(8,128)(2,1)S(1)}, bf16[32,2176]{1,0:T(8,128)(2,1)S(1)}, u32[]{:S(2)}, u32[]{:S(2)}) collective-permute-start(bf16[32,2176]{1,0:T(8,128)(2,1)S(1)} %get-tuple-element.64), channel_id=1, source_target_pairs={{0,224},{1,225},{2,226},{3,227},{4,228},{5,229},{6,230},{7,231},{8... | collective-permute-start | bytes 417800 | tf_op jit(solution)/shard_map/ppermute | solution.py:31
  112.3 6.2 %collective-permute-start.17 = (bf16[32,2176]{1,0:T(8,128)(2,1)S(1)}, bf16[32,2176]{1,0:T(8,128)(2,1)S(1)}, u32[]{:S(2)}, u32[]{:S(2)}) collective-permute-start(bf16[32,2176]{1,0:T(8,128)(2,1)S(1)} %get-tuple-element.62), channel_id=1, source_target_pairs={{0,32},{1,33},{2,34},{3,35},{4,36},{5,37},{6,38},{7,39},{8,40},{9,... | collective-permute-start | bytes 417800 | tf_op jit(solution)/shard_map/ppermute | solution.py:31
  122.7 2.6 %collective-permute-start.21 = (f32[192,512]{1,0:T(8,128)S(1)}, f32[192,512]{1,0:T(8,128)S(1)}, u32[]{:S(2)}, u32[]{:S(2)}) collective-permute-start(f32[192,512]{1,0:T(8,128)S(1)} %get-tuple-element.45), channel_id=1, source_target_pairs={{0,8},{1,9},{2,10},{3,11},{4,12},{5,13},{6,14},{7,15},{8,0},{9,1},... | collective-permute-start | bytes 1179656 | tf_op jit(solution)/shard_map/ppermute | solution.py:31
  126.7 10.1 %all-to-all-start.1 = ((f32[8,8,512]{2,1,0:T(8,128)}), f32[8,8,512]{2,1,0:T(8,128)S(1)}, u32[]{:S(2)}, u32[]{:S(2)}) async-start(f32[8,8,512]{2,1,0:T(8,128)} %get-tuple-element.46), calls=%async_computation.1 | async-start | bytes 262144 | tf_op jit(solution)/shard_map/all_to_all | solution.py:365
  138.8 15.4 %all-to-all-start.2 = ((f32[32,1,512]{2,1,0:T(1,128)}), f32[32,1,512]{2,1,0:T(1,128)S(1)}, u32[]{:S(2)}, u32[]{:S(2)}) async-start(f32[32,1,512]{2,1,0:T(1,128)} %get-tuple-element.50), calls=%async_computation.2 | async-start | bytes 131072 | tf_op jit(solution)/shard_map/all_to_all | solution.py:367

commit v4 on v3

--- a/solution.py
+++ b/solution.py
@@ -201,6 +201,24 @@
     )(owners, got)
 
 
+def settle_kernel(in_ref, out_ref, sem):
+    copy = pltpu.make_async_copy(in_ref, out_ref, sem)
+    copy.start()
+    copy.wait()
+
+
+def settle(array):
+    return pl.pallas_call(
+        settle_kernel,
+        out_shape=jax.ShapeDtypeStruct(array.shape, array.dtype),
+        in_specs=[anywhere()],
+        out_specs=vmem(),
+        scratch_shapes=[pltpu.SemaphoreType.DMA],
+        compiler_params=params(16),
+        name="settle",
+    )(array)
+
+
 def scores_kernel(owners, plan, *refs):
     n_panels = sum(count for _, count, _ in plan)
     panels, images, outs = refs[:n_panels], refs[n_panels : n_panels + NOR], refs[n_panels + NOR :]
@@ -248,12 +266,10 @@
     near = near_ref[...] + near_other_ref[...]
     far = far_ref[...] + far_other_ref[...]
     step = CLS * 8
-    full, part = 5 * step, 7 * step
-    third = near[full : full + step] + far[:step]
-    fifth = near[full + step : part] + far[step : 2 * step]
-    scores = jnp.concatenate(
-        [near[: 3 * step], third, far[2 * step :], fifth, near[3 * step : full]], axis=0
-    )
+    rows = [near[k : k + step] for k in range(0, NZ * step, step)]
+    for k in range(3):
+        rows[5 + k] += far[k * step : (k + 1) * step]
+    scores = jnp.concatenate([rows[k] for k in (0, 1, 2, 5, 7, 6, 3, 4)], axis=0)
     scores_ref[...] = scores
     scores = scores.reshape(NZ, CLS, 8, GROUP_ROWS)
     maximum = jnp.max(jnp.max(scores, axis=0), axis=1, keepdims=True)
@@ -288,9 +304,11 @@
     posterior_ref[...] = jnp.exp(class_lse - evidence)
     here = swap_halves(pltpu.roll(evidence, ((NX - x) % NX) * 2 * ROWS, 1), yhi)
     terms = jnp.exp(scores_ref[...] - here)
-    ones = jnp.ones((NDP, GROUP_ROWS), jnp.float32)
+    ones = jnp.ones((8, GROUP_ROWS), jnp.float32)
     mass = lax.dot_general(ones, terms, NT, precision=HIGH, preferred_element_type=jnp.float32)
-    mass_ref[...] = pltpu.roll(mass, z * CLS * 8, 1).reshape(mass_ref.shape)
+    mass = pltpu.roll(mass, z * CLS * 8, 1)[:1]
+    for k in range(NDP):
+        mass_ref[k] = mass
 
 
 def finish(parts, scores):
@@ -317,51 +335,53 @@
     noise = noise_weight.reshape(1, PIX)
 
     sent = panel(owners, class_prior, panel_slots, contrast, noise_weight).reshape(NDP, 8, QUART)
+    sent, images = together(sent, images)
     got = lax.all_to_all(sent, "dp", 0, 0)
 
     weighted = weigh(images, groups.reshape(ROWS, 1), contrast, noise)
     own = jnp.stack([weighted[0], other_core(weighted[1])])
-    left, right, across = from_left(own), from_right(own), other_yhi(own)
+    across, left, right = other_yhi(own), from_left(own), from_right(own)
 
     got, left, right = together(got, left, right)
-    far = [from_left(left[:1]), from_right(right[1:])]
+    half = CLS * 4
     mine0 = pick(owners, got).reshape(CLS * 8, QUART)
     mine1, mine7 = from_above(mine0), from_below(mine0)
     theirs0 = other_ylo(mine0)
-
-    mine1, mine7, theirs0, across, *far = together(mine1, mine7, theirs0, across, *far)
-    pair1 = from_above(jnp.stack([mine1, theirs0]))
-    pair7 = from_below(jnp.stack([mine7, theirs0]))
-    far = jnp.concatenate(far, axis=0)
+    left, _ = together(left, mine0)
+    far0 = from_left(left[:1])
+    mine1, mine7, across, right = together(mine1, mine7, across, right)
+    far1 = from_right(right[1:])
+    mine2, mine6 = from_above(mine1), from_below(mine7)
+    mine2, mine6, theirs0 = together(mine2, mine6, theirs0)
+    pair3 = from_above(jnp.stack([mine2, theirs0]))
+    pair5 = from_below(jnp.stack([mine6, theirs0]))
+    far0, far1, across = together(far0, far1, across)
+    far = jnp.concatenate([far0, far1], axis=0)
     left_across, right_across, far_across = from_left(across), from_right(across), other_yhi(far)
-    mine2, theirs1 = pair1
-    mine6, theirs7 = pair7
-    pair2, pair6 = from_above(pair1), from_below(pair7)
-
-    pair2, pair6, left_across, right_across, far_across = together(
-        pair2, pair6, left_across, right_across, far_across
-    )
-    mine3, theirs2 = pair2
-    mine5, theirs6 = pair6
-    half = CLS * 4
-    next3 = from_above(jnp.concatenate([mine3[half:], theirs2], axis=0))
-    next5 = from_below(jnp.concatenate([mine5[:half], theirs6], axis=0))
+    pair3, pair5 = together(pair3, pair5)
+    mine3, theirs1 = pair3
+    mine5, theirs7 = pair5
+    next4 = from_above(jnp.concatenate([mine3[half:], theirs1], axis=0))
+    next6 = from_below(jnp.concatenate([mine5[:half], theirs7], axis=0))
+    next4, next6 = together(next4, next6)
+    theirs2, theirs6 = next4[half:], next6[half:]
+    mine4 = jnp.concatenate([next6[:half], next4[:half]], axis=0)
+    theirs3, theirs5 = from_above(theirs2), from_below(theirs6)
+    across = settle(across)
     whole = [own, across, right, right_across, far, far_across, left, left_across]
-    near = [mine0, mine1, mine2, mine6, mine7, mine3, mine5]
+    near = [mine0, mine1, mine2, mine6, mine7, mine3, mine5, mine4]
     near += [theirs0, theirs1, theirs2, theirs6, theirs7]
-    near_plan = ((0, 7, 0), (1, 5, 0))
+    near_plan = ((0, 8, 0), (1, 5, 0))
     (near_theirs,) = scores_of(near, whole, (1,), near_plan)
     near_other = other_core(near_theirs)
     (near_mine,) = scores_of(near, whole, (0,), near_plan)
-    theirs3, theirs5 = next3[half:], next5[half:]
     last = [from_below(theirs5[:half]), from_above(theirs3[half:])]
     near_mine, *last = together(near_mine, *last)
-    mine4 = jnp.concatenate([next5[:half], next3[:half]], axis=0)
-    theirs4 = jnp.concatenate(last, axis=0)
-    far_theirs, far_mine = scores_of(
-        [theirs3, theirs5, theirs4, mine4], whole, (1, 0), ((1, 3, 0), (0, 1, 2 * CLS * 8))
-    )
-    scores, partial = norms(near_mine, near_other, far_mine, other_core(far_theirs))
+    far_panels, far_plan = [theirs3, theirs5, jnp.concatenate(last, axis=0)], ((1, 3, 0),)
+    (far_theirs,) = scores_of(far_panels, whole, (1,), far_plan)
+    far_other = other_core(far_theirs)
+    (far_mine,) = scores_of(far_panels, whole, (0,), far_plan)
+    scores, partial = norms(near_mine, near_other, far_mine, far_other)
     parts = lax.all_to_all(partial, "orient", 0, 0)
     evidence, posterior, mass = finish(parts, scores)
     masses = lax.all_to_all(mass, "dp", 0, 0)

time: 156 us -> 147 us (0.942)
  waiting for transfers between devices: 74.9 us -> 65.3 us
  starting transfers between devices: 55.6 us -> 60.4 us
  Pallas kernels: 20.5 us -> 17.1 us
    ppermute x22 -> x24, waiting for transfers between devices: 61.1 us -> 51.3 us  [permute(): return lax.ppermute(array, ('dp', 'orient'), pairs)]
    pallas_call x3 -> x4, Pallas kernels: 10.7 us -> 6.1 us  [scores_of(): pl.pallas_call(functools.partial(scores_kernel, owners, plan), out_shape=...]
    ppermute x22 -> x24, starting transfers between devices: 33.9 us -> 36.2 us  [permute(): return lax.ppermute(array, ('dp', 'orient'), pairs)]
    all_to_all x1, starting transfers between devices: 3.37 us -> 5.15 us  [per_device(): parts = lax.all_to_all(partial, 'orient', 0, 0)]
  transfers between devices with their start and end apart: 25 -> 27, of which waited for: 13 -> 15; matrix products, arithmetic and copies ran while one was open for 1% -> 1% of each run, Pallas kernels for 9% -> 5%
where the time goes in v4:
time: 147 us
  waiting for transfers between devices  65.3 us (44%)
  starting transfers between devices  60.4 us (41%)
  Pallas kernels  17.1 us (12%)
  local copies, waits for them, and re-layouts  2.64 us (2%)
    ppermute x24, waiting for transfers between devices, permute(): return lax.ppermute(array, ('dp', 'orient'), pairs)  51.3 us
    ppermute x24, starting transfers between devices, permute(): return lax.ppermute(array, ('dp', 'orient'), pairs)  36.2 us
    all_to_all x1, starting transfers between devices, per_device(): got = lax.all_to_all(sent, 'dp', 0, 0)  11.3 us
    all_to_all x1, starting transfers between devices, per_device(): masses = lax.all_to_all(mass, 'dp', 0, 0)  7.74 us
    all_to_all x1, waiting for transfers between devices, per_device(): masses = lax.all_to_all(mass, 'dp', 0, 0)  7.07 us
    all_to_all x1, waiting for transfers between devices, per_device(): parts = lax.all_to_all(partial, 'orient', 0, 0)  6.9 us
    pallas_call x4, Pallas kernels, scores_of(): pl.pallas_call(functools.partial(scores_kernel, owners, plan), out_shape=...  6.1 us
    all_to_all x1, starting transfers between devices, per_device(): parts = lax.all_to_all(partial, 'orient', 0, 0)  5.15 us
  transfers between devices with their start and end apart: 27, of which 15 were waited for; matrix products, arithmetic and copies ran while one was open for 1% of the time, Pallas kernels for 5%

profile of v4, /device:TPU:1, one launch (start us, length us, event | category | flops | bytes accessed | tf_op | source)
XLA Modules:
  0.0 146.7 jit_solution(11022805780783861520)
XLA Ops:
  0.6 3.8 %panel.1 = bf16[256,2176]{1,0:T(8,128)(2,1)} custom-call(s32[8]{0:T(128)} %owners_ref.1, f32[8]{0:T(128)} %priors_hbm.1, bf16[1,64,8448]{2,1,0:T(8,128)(2,1)} %slot_hbm.1, f32[64,4224]{1,0:T(8,128)} %contrast_ref.1, f32[4224]{0:T(1024)} %noise_hbm.1), custom_call_target="tpu_custom_call" | custom-call | tf_op jit(solution)/shard_map/panel/pallas_call | solution.py:163
  4.5 11.3 %all-to-all-start = ((bf16[32,8,2176]{2,1,0:T(8,128)(2,1)}), bf16[32,8,2176]{2,1,0:T(8,128)(2,1)}, u32[]{:S(2)}, u32[]{:S(2)}) async-start(bf16[32,8,2176]{2,1,0:T(8,128)(2,1)} %bitcast.32), calls=%async_computation | async-start | bytes 2228224 | tf_op jit(solution)/shard_map/all_to_all | solution.py:339
  16.0 1.1 weigh.1
  17.2 0.4 collective-permute-start
  17.6 1.7 %collective-permute-done = bf16[2,64,2176]{2,1,0:T(8,128)(2,1)S(1)} collective-permute-done((bf16[2,64,2176]{2,1,0:T(8,128)(2,1)S(1)}, bf16[2,64,2176]{2,1,0:T(8,128)(2,1)S(1)}, u32[]{:S(2)}, u32[]{:S(2)}) %collective-permute-start) | collective-permute-done | bytes 557088 | tf_op jit(solution)/shard_map/ppermute | solution.py:31
  19.3 1.3 collective-permute-start.1
  20.6 1.5 collective-permute-start.2
  22.1 2.6 %collective-permute-start.5 = (bf16[2,2,64,2176]{3,2,1,0:T(8,128)(2,1)S(1)}, bf16[2,2,64,2176]{3,2,1,0:T(8,128)(2,1)}, u32[]{:S(2)}, u32[]{:S(2)}) collective-permute-start(bf16[2,2,64,2176]{3,2,1,0:T(8,128)(2,1)S(1)} %pad_maximum_fusion.refs_13_.refs_3_), channel_id=1, source_target_pairs={{0,1},{1,0},{2,3},{3,2},{4,5},{5,4},{6,7},{7,6},{8,9},{9,8},{10,11... | collective-permute-start | bytes 3342344 | tf_op jit(solution)/shard_map/ppermute | solution.py:31
  24.7 21.9 %collective-permute-done.1.refs_19_.refs_9_ = bf16[2,2,64,2176]{3,2,1,0:T(8,128)(2,1)S(1)} collective-permute-done((bf16[2,2,64,2176]{3,2,1,0:T(8,128)(2,1)S(1)}, bf16[2,2,64,2176]{3,2,1,0:T(8,128)(2,1)S(1)}, u32[]{:S(2)}, u32[]{:S(2)}) %collective-permute-start.1) | collective-permute-done | bytes 1114144 | tf_op jit(solution)/shard_map/ppermute | solution.py:31
  46.6 1.5 %pick.1 = bf16[8,8,2176]{2,1,0:T(8,128)(2,1)S(1)} custom-call(s32[8]{0:T(128)S(1)} %copy-done.2, bf16[32,8,2176]{2,1,0:T(8,128)(2,1)} %all-to-all-done.got_ref), custom_call_target="tpu_custom_call" | custom-call | tf_op jit(solution)/shard_map/pick/pallas_call | solution.py:193
  48.1 2.7 %collective-permute-start.3 = (bf16[64,2176]{1,0:T(8,128)(2,1)S(1)}, bf16[64,2176]{1,0:T(8,128)(2,1)S(1)}, u32[]{:S(2)}, u32[]{:S(2)}) collective-permute-start(bf16[64,2176]{1,0:T(8,128)(2,1)S(1)} %bitcast.24), channel_id=1, source_target_pairs={{0,224},{1,225},{2,226},{3,227},{4,228},{5,229},{6,230},{7,231},{8... | collective-permute-start | bytes 835592 | tf_op jit(solution)/shard_map/ppermute | solution.py:31
  50.8 1.1 collective-permute-start.8
  51.9 6.0 %collective-permute-done.5.in_ref = bf16[2,2,64,2176]{3,2,1,0:T(8,128)(2,1)} collective-permute-done((bf16[2,2,64,2176]{3,2,1,0:T(8,128)(2,1)S(1)}, bf16[2,2,64,2176]{3,2,1,0:T(8,128)(2,1)}, u32[]{:S(2)}, u32[]{:S(2)}) %collective-permute-start.5) | collective-permute-done | bytes 1114144 | tf_op jit(solution)/shard_map/ppermute | solution.py:31
  57.9 0.9 collective-permute-done.4.refs_4_
  58.8 1.0 collective-permute-start.6
  59.8 0.4 collective-permute-start.7
  60.3 1.0 collective-permute-start.13
  61.3 1.8 %collective-permute-start.14 = (bf16[1,2,64,2176]{3,2,1,0:T(8,128)(2,1)S(1)}, bf16[1,2,64,2176]{3,2,1,0:T(8,128)(2,1)S(1)}, u32[]{:S(2)}, u32[]{:S(2)}) collective-permute-start(bf16[1,2,64,2176]{3,2,1,0:T(8,128)(2,1)S(1)} %slice.55), channel_id=1, source_target_pairs={{0,6},{1,7},{2,0},{3,1},{4,2},{5,3},{6,4},{7,5},{8,14},{9,15},{10,... | collective-permute-start | bytes 1671176 | tf_op jit(solution)/shard_map/ppermute | solution.py:31
  63.2 1.0 collective-permute-done.8.refs_8_
  64.1 0.5 collective-permute-done.6.refs_2_
  64.6 3.0 %collective-permute-done.7.refs_3_ = bf16[64,2176]{1,0:T(8,128)(2,1)S(1)} collective-permute-done((bf16[64,2176]{1,0:T(8,128)(2,1)S(1)}, bf16[64,2176]{1,0:T(8,128)(2,1)S(1)}, u32[]{:S(2)}, u32[]{:S(2)}) %collective-permute-start.7) | collective-permute-done | bytes 278560 | tf_op jit(solution)/shard_map/ppermute | solution.py:31
  67.9 2.7 %collective-permute-start.9 = (bf16[2,64,2176]{2,1,0:T(8,128)(2,1)S(1)}, bf16[2,64,2176]{2,1,0:T(8,128)(2,1)S(1)}, u32[]{:S(2)}, u32[]{:S(2)}) collective-permute-start(bf16[2,64,2176]{2,1,0:T(8,128)(2,1)S(1)} %get-tuple-element.66), channel_id=1, source_target_pairs={{0,224},{1,225},{2,226},{3,227},{4,228},{5,229},{6,230},{7,231},{8... | collective-permute-start | bytes 1671176 | tf_op jit(solution)/shard_map/ppermute | solution.py:31
  70.5 2.3 %collective-permute-done.13 = bf16[1,2,64,2176]{3,2,1,0:T(8,128)(2,1)S(1)} collective-permute-done((bf16[1,2,64,2176]{3,2,1,0:T(8,128)(2,1)S(1)}, bf16[1,2,64,2176]{3,2,1,0:T(8,128)(2,1)S(1)}, u32[]{:S(2)}, u32[]{:S(2)}) %collective-permute-start.13) | collective-permute-done | bytes 557088 | tf_op jit(solution)/shard_map/ppermute | solution.py:31
  72.9 2.5 %collective-permute-start.15 = (bf16[2,2,64,2176]{3,2,1,0:T(8,128)(2,1)}, bf16[2,2,64,2176]{3,2,1,0:T(8,128)(2,1)S(1)}, u32[]{:S(2)}, u32[]{:S(2)}) collective-permute-start(bf16[2,2,64,2176]{3,2,1,0:T(8,128)(2,1)} %collective-permute-done.5.in_ref), channel_id=1, source_target_pairs={{0,6},{1,7},{2,0},{3,1},{4,2},{5,3},{6,4},{7,5},{8,14},{9,15},{10,... | collective-permute-start | bytes 3342344 | tf_op jit(solution)/shard_map/ppermute | solution.py:31
  75.5 2.4 %collective-permute-start.16 = (bf16[2,2,64,2176]{3,2,1,0:T(8,128)(2,1)S(1)}, bf16[2,2,64,2176]{3,2,1,0:T(8,128)(2,1)S(1)}, u32[]{:S(2)}, u32[]{:S(2)}) collective-permute-start(bf16[2,2,64,2176]{3,2,1,0:T(8,128)(2,1)S(1)} %constant_dynamic-update-slice_fusion.refs_17_.refs_7_), channel_id=1, source_target_pairs={{0,1},{1,0},{2,3},{3,2},{4,5},{5,4},{6,7},{7,6},{8,9},{9,8},{10,11... | collective-permute-start | bytes 3342344 | tf_op jit(solution)/shard_map/ppermute | solution.py:31
  77.8 2.9 %collective-permute-done.10 = bf16[2,64,2176]{2,1,0:T(8,128)(2,1)S(1)} collective-permute-done((bf16[2,64,2176]{2,1,0:T(8,128)(2,1)S(1)}, bf16[2,64,2176]{2,1,0:T(8,128)(2,1)S(1)}, u32[]{:S(2)}, u32[]{:S(2)}) %collective-permute-start.10) | collective-permute-done | bytes 557088 | tf_op jit(solution)/shard_map/ppermute | solution.py:31
  81.0 2.7 %collective-permute-start.11 = (bf16[96,2176]{1,0:T(8,128)(2,1)S(1)}, bf16[96,2176]{1,0:T(8,128)(2,1)S(1)}, u32[]{:S(2)}, u32[]{:S(2)}) collective-permute-start(bf16[96,2176]{1,0:T(8,128)(2,1)S(1)} %pad_maximum_fusion.3), channel_id=1, source_target_pairs={{0,224},{1,225},{2,226},{3,227},{4,228},{5,229},{6,230},{7,231},{8... | collective-permute-start | bytes 1253384 | tf_op jit(solution)/shard_map/ppermute | solution.py:31
  83.8 1.3 settle.1.refs_14_.refs_4_
  85.0 4.9 %collective-permute-done.12 = bf16[96,2176]{1,0:T(8,128)(2,1)S(1)} collective-permute-done((bf16[96,2176]{1,0:T(8,128)(2,1)S(1)}, bf16[96,2176]{1,0:T(8,128)(2,1)S(1)}, u32[]{:S(2)}, u32[]{:S(2)}) %collective-permute-start.12) | collective-permute-done | bytes 417824 | tf_op jit(solution)/shard_map/ppermute | solution.py:31
  90.1 2.7 %collective-permute-start.20 = (bf16[64,2176]{1,0:T(8,128)(2,1)S(1)}, bf16[64,2176]{1,0:T(8,128)(2,1)S(1)}, u32[]{:S(2)}, u32[]{:S(2)}) collective-permute-start(bf16[64,2176]{1,0:T(8,128)(2,1)S(1)} %slice.52.refs_10_), channel_id=1, source_target_pairs={{0,224},{1,225},{2,226},{3,227},{4,228},{5,229},{6,230},{7,231},{8... | collective-permute-start | bytes 835592 | tf_op jit(solution)/shard_map/ppermute | solution.py:31
  92.8 4.2 %collective-permute-done.18.refs_1_ = bf16[64,2176]{1,0:T(8,128)(2,1)S(1)} collective-permute-done((bf16[64,2176]{1,0:T(8,128)(2,1)S(1)}, bf16[64,2176]{1,0:T(8,128)(2,1)S(1)}, u32[]{:S(2)}, u32[]{:S(2)}) %collective-permute-start.18) | collective-permute-done | bytes 278560 | tf_op jit(solution)/shard_map/ppermute | solution.py:31
  97.2 2.7 %collective-permute-start.21 = (bf16[32,2176]{1,0:T(8,128)(2,1)S(1)}, bf16[32,2176]{1,0:T(8,128)(2,1)S(1)}, u32[]{:S(2)}, u32[]{:S(2)}) collective-permute-start(bf16[32,2176]{1,0:T(8,128)(2,1)S(1)} %slice.61), channel_id=1, source_target_pairs={{0,224},{1,225},{2,226},{3,227},{4,228},{5,229},{6,230},{7,231},{8... | collective-permute-start | bytes 417800 | tf_op jit(solution)/shard_map/ppermute | solution.py:31
  99.9 2.2 %scores.4.near_ref = f32[512,512]{1,0:T(8,128)S(1)} custom-call(bf16[64,2176]{1,0:T(8,128)(2,1)S(1)} %bitcast.27, bf16[64,2176]{1,0:T(8,128)(2,1)S(1)} %collective-permute-done.3.refs_1_, bf16[64,2176]{1,0:T(8,128)(2,1)S(1)} %collective-permute-done.6.refs_2_, bf16[64,2176]{1,0:T(8,128)(2,1)S(1)} %collective-permute-done.7.refs_3_, ...), custom_call_target="tpu_custom_call" | custom-call | flops 1853882368 | bytes 8388608 | tf_op jit(solution)/shard_map/scores/pallas_call | solution.py:241
  102.1 1.2 collective-permute-done.19
  103.3 2.2 %scores.5 = f32[512,512]{1,0:T(8,128)S(1)} custom-call(bf16[64,2176]{1,0:T(8,128)(2,1)S(1)} %bitcast.28, bf16[64,2176]{1,0:T(8,128)(2,1)S(1)} %collective-permute-done.3.refs_1_, bf16[64,2176]{1,0:T(8,128)(2,1)S(1)} %collective-permute-done.6.refs_2_, bf16[64,2176]{1,0:T(8,128)(2,1)S(1)} %collective-permute-done.7.refs_3_, ...), custom_call_target="tpu_custom_call" | custom-call | flops 1853882368 | bytes 8388608 | tf_op jit(solution)/shard_map/scores/pallas_call | solution.py:241
  105.4 6.0 %collective-permute-start.22 = (f32[512,512]{1,0:T(8,128)S(1)}, f32[512,512]{1,0:T(8,128)S(1)}, u32[]{:S(2)}, u32[]{:S(2)}) collective-permute-start(f32[512,512]{1,0:T(8,128)S(1)} %scores.5), channel_id=1, source_target_pairs={{0,8},{1,9},{2,10},{3,11},{4,12},{5,13},{6,14},{7,15},{8,0},{9,1},... | collective-permute-start | bytes 3145736 | tf_op jit(solution)/shard_map/ppermute | solution.py:31
  111.5 0.9 scores.7
  112.7 0.9 scores.6.far_ref
  113.6 0.8 collective-permute-done.23.far_other_ref
  114.4 1.4 norms.1
  115.8 5.1 %all-to-all-start.1 = ((f32[8,8,512]{2,1,0:T(8,128)}), f32[8,8,512]{2,1,0:T(8,128)S(1)}, u32[]{:S(2)}, u32[]{:S(2)}) async-start(f32[8,8,512]{2,1,0:T(8,128)} %get-tuple-element.54), calls=%async_computation.1 | async-start | bytes 262144 | tf_op jit(solution)/shard_map/all_to_all | solution.py:385
  121.0 6.9 %all-to-all-done.1.parts_ref = f32[8,8,512]{2,1,0:T(8,128)S(1)} async-done(((f32[8,8,512]{2,1,0:T(8,128)}), f32[8,8,512]{2,1,0:T(8,128)S(1)}, u32[]{:S(2)}, u32[]{:S(2)}) %all-to-all-start.1) | async-done | bytes 131104 | tf_op jit(solution)/shard_map/all_to_all | solution.py:385
  127.9 1.9 %finish.1 = (f32[1,512]{1,0:T(1,128)S(1)}, f32[8,512]{1,0:T(8,128)S(1)}, f32[32,1,512]{2,1,0:T(1,128)}) custom-call(f32[8,8,512]{2,1,0:T(8,128)S(1)} %all-to-all-done.1.parts_ref, f32[512,512]{1,0:T(8,128)S(1)} %get-tuple-element.55.scores_ref), custom_call_target="tpu_custom_call" | custom-call | tf_op jit(solution)/shard_map/finish/pallas_call | solution.py:315
  129.8 7.7 %all-to-all-start.2 = ((f32[32,1,512]{2,1,0:T(1,128)}), f32[32,1,512]{2,1,0:T(1,128)S(1)}, u32[]{:S(2)}, u32[]{:S(2)}) async-start(f32[32,1,512]{2,1,0:T(1,128)} %get-tuple-element.58), calls=%async_computation.2 | async-start | bytes 131072 | tf_op jit(solution)/shard_map/all_to_all | solution.py:387
  137.5 0.6 dynamic-slice_bitcast_fusion
  138.1 0.7 constant_dynamic-slice_fusion
  138.8 7.1 %all-to-all-done.2 = f32[32,1,512]{2,1,0:T(1,128)S(1)} async-done(((f32[32,1,512]{2,1,0:T(1,128)}), f32[32,1,512]{2,1,0:T(1,128)S(1)}, u32[]{:S(2)}, u32[]{:S(2)}) %all-to-all-start.2) | async-done | bytes 65568 | tf_op jit(solution)/shard_map/all_to_all | solution.py:387
  146.1 0.7 reshape.32
  (57 shorter events, 1.8 us)
Async XLA Ops:
  4.4 11.4 %copy-start.3 = (f32[4224]{0:T(1024)S(1)}, f32[4224]{0:T(1024)}, u32[]{:S(2)}) copy-start(f32[4224]{0:T(1024)} %noise_hbm.1) | copy-start | bytes 50692
  4.4 11.4 %copy-start.4 = (s32[64]{0:T(128)S(1)}, s32[64]{0:T(128)}, u32[]{:S(2)}) copy-start(s32[64]{0:T(128)} %param.8) | copy-start | bytes 772
  4.5 11.5 %copy-start = (f32[64,4224]{1,0:T(8,128)S(1)}, f32[64,4224]{1,0:T(8,128)}, u32[]{:S(2)}) copy-start(f32[64,4224]{1,0:T(8,128)} %contrast_ref.1) | copy-start | bytes 3244036
  4.5 11.5 %copy-start.1 = (bf16[64,8448]{1,0:T(8,128)(2,1)S(1)}, bf16[64,8448]{1,0:T(8,128)(2,1)}, u32[]{:S(2)}) copy-start(bf16[64,8448]{1,0:T(8,128)(2,1)} %images_ref) | copy-start | bytes 3244036
  4.5 42.1 %all-to-all-start = ((bf16[32,8,2176]{2,1,0:T(8,128)(2,1)}), bf16[32,8,2176]{2,1,0:T(8,128)(2,1)}, u32[]{:S(2)}, u32[]{:S(2)}) async-start(bf16[32,8,2176]{2,1,0:T(8,128)(2,1)} %bitcast.32), calls=%async_computation | async-start | bytes 2228224 | tf_op jit(solution)/shard_map/all_to_all | solution.py:339
  17.2 2.0 %collective-permute-start = (bf16[2,64,2176]{2,1,0:T(8,128)(2,1)S(1)}, bf16[2,64,2176]{2,1,0:T(8,128)(2,1)S(1)}, u32[]{:S(2)}, u32[]{:S(2)}) collective-permute-start(bf16[2,64,2176]{2,1,0:T(8,128)(2,1)S(1)} %get-tuple-element.60), channel_id=1, source_target_pairs={{0,8},{1,9},{2,10},{3,11},{4,12},{5,13},{6,14},{7,15},{8,0},{9,1},... | collective-permute-start | bytes 1671176 | tf_op jit(solution)/shard_map/ppermute | solution.py:31
  19.2 27.4 %copy-start.2 = (s32[8]{0:T(128)S(1)}, s32[8]{0:T(128)}, u32[]{:S(2)}) copy-start(s32[8]{0:T(128)} %owners_ref.1) | copy-start | bytes 100
  19.3 27.3 %collective-permute-start.1 = (bf16[2,2,64,2176]{3,2,1,0:T(8,128)(2,1)S(1)}, bf16[2,2,64,2176]{3,2,1,0:T(8,128)(2,1)S(1)}, u32[]{:S(2)}, u32[]{:S(2)}) collective-permute-start(bf16[2,2,64,2176]{3,2,1,0:T(8,128)(2,1)S(1)} %pad_maximum_fusion.refs_13_.refs_3_), channel_id=1, source_target_pairs={{0,2},{1,3},{2,4},{3,5},{4,6},{5,7},{6,0},{7,1},{8,10},{9,11},{10,... | collective-permute-start | bytes 3342344 | tf_op jit(solution)/shard_map/ppermute | solution.py:31
  20.6 26.0 %collective-permute-start.2 = (bf16[2,2,64,2176]{3,2,1,0:T(8,128)(2,1)S(1)}, bf16[2,2,64,2176]{3,2,1,0:T(8,128)(2,1)S(1)}, u32[]{:S(2)}, u32[]{:S(2)}) collective-permute-start(bf16[2,2,64,2176]{3,2,1,0:T(8,128)(2,1)S(1)} %pad_maximum_fusion.refs_13_.refs_3_), channel_id=1, source_target_pairs={{0,6},{1,7},{2,0},{3,1},{4,2},{5,3},{6,4},{7,5},{8,14},{9,15},{10,... | collective-permute-start | bytes 3342344 | tf_op jit(solution)/shard_map/ppermute | solution.py:31
  22.1 35.8 %collective-permute-start.5 = (bf16[2,2,64,2176]{3,2,1,0:T(8,128)(2,1)S(1)}, bf16[2,2,64,2176]{3,2,1,0:T(8,128)(2,1)}, u32[]{:S(2)}, u32[]{:S(2)}) collective-permute-start(bf16[2,2,64,2176]{3,2,1,0:T(8,128)(2,1)S(1)} %pad_maximum_fusion.refs_13_.refs_3_), channel_id=1, source_target_pairs={{0,1},{1,0},{2,3},{3,2},{4,5},{5,4},{6,7},{7,6},{8,9},{9,8},{10,11... | collective-permute-start | bytes 3342344 | tf_op jit(solution)/shard_map/ppermute | solution.py:31
  48.1 9.8 %collective-permute-start.3 = (bf16[64,2176]{1,0:T(8,128)(2,1)S(1)}, bf16[64,2176]{1,0:T(8,128)(2,1)S(1)}, u32[]{:S(2)}, u32[]{:S(2)}) collective-permute-start(bf16[64,2176]{1,0:T(8,128)(2,1)S(1)} %bitcast.24), channel_id=1, source_target_pairs={{0,224},{1,225},{2,226},{3,227},{4,228},{5,229},{6,230},{7,231},{8... | collective-permute-start | bytes 835592 | tf_op jit(solution)/shard_map/ppermute | solution.py:31
  50.8 8.0 %collective-permute-start.4 = (bf16[64,2176]{1,0:T(8,128)(2,1)S(1)}, bf16[64,2176]{1,0:T(8,128)(2,1)S(1)}, u32[]{:S(2)}, u32[]{:S(2)}) collective-permute-start(bf16[64,2176]{1,0:T(8,128)(2,1)S(1)} %bitcast.25), channel_id=1, source_target_pairs={{0,32},{1,33},{2,34},{3,35},{4,36},{5,37},{6,38},{7,39},{8,40},{9,... | collective-permute-start | bytes 835592 | tf_op jit(solution)/shard_map/ppermute | solution.py:31
  50.8 13.3 %collective-permute-start.8 = (bf16[64,2176]{1,0:T(8,128)(2,1)S(1)}, bf16[64,2176]{1,0:T(8,128)(2,1)S(1)}, u32[]{:S(2)}, u32[]{:S(2)}) collective-permute-start(bf16[64,2176]{1,0:T(8,128)(2,1)S(1)} %bitcast.26), channel_id=1, source_target_pairs={{0,16},{1,17},{2,18},{3,19},{4,20},{5,21},{6,22},{7,23},{8,24},{9,... | collective-permute-start | bytes 835592 | tf_op jit(solution)/shard_map/ppermute | solution.py:31
  58.8 5.9 %collective-permute-start.6 = (bf16[64,2176]{1,0:T(8,128)(2,1)S(1)}, bf16[64,2176]{1,0:T(8,128)(2,1)S(1)}, u32[]{:S(2)}, u32[]{:S(2)}) collective-permute-start(bf16[64,2176]{1,0:T(8,128)(2,1)S(1)} %collective-permute-done.3.refs_1_), channel_id=1, source_target_pairs={{0,224},{1,225},{2,226},{3,227},{4,228},{5,229},{6,230},{7,231},{8... | collective-permute-start | bytes 835592 | tf_op jit(solution)/shard_map/ppermute | solution.py:31
  59.8 7.8 %collective-permute-start.7 = (bf16[64,2176]{1,0:T(8,128)(2,1)S(1)}, bf16[64,2176]{1,0:T(8,128)(2,1)S(1)}, u32[]{:S(2)}, u32[]{:S(2)}) collective-permute-start(bf16[64,2176]{1,0:T(8,128)(2,1)S(1)} %collective-permute-done.4.refs_4_), channel_id=1, source_target_pairs={{0,32},{1,33},{2,34},{3,35},{4,36},{5,37},{6,38},{7,39},{8,40},{9,... | collective-permute-start | bytes 835592 | tf_op jit(solution)/shard_map/ppermute | solution.py:31
  60.3 12.6 %collective-permute-start.13 = (bf16[1,2,64,2176]{3,2,1,0:T(8,128)(2,1)S(1)}, bf16[1,2,64,2176]{3,2,1,0:T(8,128)(2,1)S(1)}, u32[]{:S(2)}, u32[]{:S(2)}) collective-permute-start(bf16[1,2,64,2176]{3,2,1,0:T(8,128)(2,1)S(1)} %slice.54), channel_id=1, source_target_pairs={{0,2},{1,3},{2,4},{3,5},{4,6},{5,7},{6,0},{7,1},{8,10},{9,11},{10,... | collective-permute-start | bytes 1671176 | tf_op jit(solution)/shard_map/ppermute | solution.py:31
  61.3 11.5 %collective-permute-start.14 = (bf16[1,2,64,2176]{3,2,1,0:T(8,128)(2,1)S(1)}, bf16[1,2,64,2176]{3,2,1,0:T(8,128)(2,1)S(1)}, u32[]{:S(2)}, u32[]{:S(2)}) collective-permute-start(bf16[1,2,64,2176]{3,2,1,0:T(8,128)(2,1)S(1)} %slice.55), channel_id=1, source_target_pairs={{0,6},{1,7},{2,0},{3,1},{4,2},{5,3},{6,4},{7,5},{8,14},{9,15},{10,... | collective-permute-start | bytes 1671176 | tf_op jit(solution)/shard_map/ppermute | solution.py:31
  67.8 13.0 %collective-permute-start.10 = (bf16[2,64,2176]{2,1,0:T(8,128)(2,1)S(1)}, bf16[2,64,2176]{2,1,0:T(8,128)(2,1)S(1)}, u32[]{:S(2)}, u32[]{:S(2)}) collective-permute-start(bf16[2,64,2176]{2,1,0:T(8,128)(2,1)S(1)} %get-tuple-element.65), channel_id=1, source_target_pairs={{0,32},{1,33},{2,34},{3,35},{4,36},{5,37},{6,38},{7,39},{8,40},{9,... | collective-permute-start | bytes 1671176 | tf_op jit(solution)/shard_map/ppermute | solution.py:31
  67.9 12.9 %collective-permute-start.9 = (bf16[2,64,2176]{2,1,0:T(8,128)(2,1)S(1)}, bf16[2,64,2176]{2,1,0:T(8,128)(2,1)S(1)}, u32[]{:S(2)}, u32[]{:S(2)}) collective-permute-start(bf16[2,64,2176]{2,1,0:T(8,128)(2,1)S(1)} %get-tuple-element.66), channel_id=1, source_target_pairs={{0,224},{1,225},{2,226},{3,227},{4,228},{5,229},{6,230},{7,231},{8... | collective-permute-start | bytes 1671176 | tf_op jit(solution)/shard_map/ppermute | solution.py:31
  72.9 27.0 %collective-permute-start.15 = (bf16[2,2,64,2176]{3,2,1,0:T(8,128)(2,1)}, bf16[2,2,64,2176]{3,2,1,0:T(8,128)(2,1)S(1)}, u32[]{:S(2)}, u32[]{:S(2)}) collective-permute-start(bf16[2,2,64,2176]{3,2,1,0:T(8,128)(2,1)} %collective-permute-done.5.in_ref), channel_id=1, source_target_pairs={{0,6},{1,7},{2,0},{3,1},{4,2},{5,3},{6,4},{7,5},{8,14},{9,15},{10,... | collective-permute-start | bytes 3342344 | tf_op jit(solution)/shard_map/ppermute | solution.py:31
  75.4 24.5 %collective-permute-start.17 = (bf16[2,2,64,2176]{3,2,1,0:T(8,128)(2,1)}, bf16[2,2,64,2176]{3,2,1,0:T(8,128)(2,1)S(1)}, u32[]{:S(2)}, u32[]{:S(2)}) collective-permute-start(bf16[2,2,64,2176]{3,2,1,0:T(8,128)(2,1)} %collective-permute-done.5.in_ref), channel_id=1, source_target_pairs={{0,2},{1,3},{2,4},{3,5},{4,6},{5,7},{6,0},{7,1},{8,10},{9,11},{10,... | collective-permute-start | bytes 3342344 | tf_op jit(solution)/shard_map/ppermute | solution.py:31
  75.5 24.4 %collective-permute-start.16 = (bf16[2,2,64,2176]{3,2,1,0:T(8,128)(2,1)S(1)}, bf16[2,2,64,2176]{3,2,1,0:T(8,128)(2,1)S(1)}, u32[]{:S(2)}, u32[]{:S(2)}) collective-permute-start(bf16[2,2,64,2176]{3,2,1,0:T(8,128)(2,1)S(1)} %constant_dynamic-update-slice_fusion.refs_17_.refs_7_), channel_id=1, source_target_pairs={{0,1},{1,0},{2,3},{3,2},{4,5},{5,4},{6,7},{7,6},{8,9},{9,8},{10,11... | collective-permute-start | bytes 3342344 | tf_op jit(solution)/shard_map/ppermute | solution.py:31
  80.9 9.1 %collective-permute-start.12 = (bf16[96,2176]{1,0:T(8,128)(2,1)S(1)}, bf16[96,2176]{1,0:T(8,128)(2,1)S(1)}, u32[]{:S(2)}, u32[]{:S(2)}) collective-permute-start(bf16[96,2176]{1,0:T(8,128)(2,1)S(1)} %pad_maximum_fusion.4), channel_id=1, source_target_pairs={{0,32},{1,33},{2,34},{3,35},{4,36},{5,37},{6,38},{7,39},{8,40},{9,... | collective-permute-start | bytes 1253384 | tf_op jit(solution)/shard_map/ppermute | solution.py:31
  81.0 8.9 %collective-permute-start.11 = (bf16[96,2176]{1,0:T(8,128)(2,1)S(1)}, bf16[96,2176]{1,0:T(8,128)(2,1)S(1)}, u32[]{:S(2)}, u32[]{:S(2)}) collective-permute-start(bf16[96,2176]{1,0:T(8,128)(2,1)S(1)} %pad_maximum_fusion.3), channel_id=1, source_target_pairs={{0,224},{1,225},{2,226},{3,227},{4,228},{5,229},{6,230},{7,231},{8... | collective-permute-start | bytes 1253384 | tf_op jit(solution)/shard_map/ppermute | solution.py:31
  90.0 7.0 %collective-permute-start.18 = (bf16[64,2176]{1,0:T(8,128)(2,1)S(1)}, bf16[64,2176]{1,0:T(8,128)(2,1)S(1)}, u32[]{:S(2)}, u32[]{:S(2)}) collective-permute-start(bf16[64,2176]{1,0:T(8,128)(2,1)S(1)} %slice.53.refs_11_), channel_id=1, source_target_pairs={{0,32},{1,33},{2,34},{3,35},{4,36},{5,37},{6,38},{7,39},{8,40},{9,... | collective-permute-start | bytes 835592 | tf_op jit(solution)/shard_map/ppermute | solution.py:31
  90.1 7.0 %collective-permute-start.20 = (bf16[64,2176]{1,0:T(8,128)(2,1)S(1)}, bf16[64,2176]{1,0:T(8,128)(2,1)S(1)}, u32[]{:S(2)}, u32[]{:S(2)}) collective-permute-start(bf16[64,2176]{1,0:T(8,128)(2,1)S(1)} %slice.52.refs_10_), channel_id=1, source_target_pairs={{0,224},{1,225},{2,226},{3,227},{4,228},{5,229},{6,230},{7,231},{8... | collective-permute-start | bytes 835592 | tf_op jit(solution)/shard_map/ppermute | solution.py:31
  97.0 6.2 %collective-permute-start.19 = (bf16[32,2176]{1,0:T(8,128)(2,1)S(1)}, bf16[32,2176]{1,0:T(8,128)(2,1)S(1)}, u32[]{:S(2)}, u32[]{:S(2)}) collective-permute-start(bf16[32,2176]{1,0:T(8,128)(2,1)S(1)} %slice.60), channel_id=1, source_target_pairs={{0,32},{1,33},{2,34},{3,35},{4,36},{5,37},{6,38},{7,39},{8,40},{9,... | collective-permute-start | bytes 417800 | tf_op jit(solution)/shard_map/ppermute | solution.py:31
  97.2 6.1 %collective-permute-start.21 = (bf16[32,2176]{1,0:T(8,128)(2,1)S(1)}, bf16[32,2176]{1,0:T(8,128)(2,1)S(1)}, u32[]{:S(2)}, u32[]{:S(2)}) collective-permute-start(bf16[32,2176]{1,0:T(8,128)(2,1)S(1)} %slice.61), channel_id=1, source_target_pairs={{0,224},{1,225},{2,226},{3,227},{4,228},{5,229},{6,230},{7,231},{8... | collective-permute-start | bytes 417800 | tf_op jit(solution)/shard_map/ppermute | solution.py:31
  105.4 9.0 %collective-permute-start.22 = (f32[512,512]{1,0:T(8,128)S(1)}, f32[512,512]{1,0:T(8,128)S(1)}, u32[]{:S(2)}, u32[]{:S(2)}) collective-permute-start(f32[512,512]{1,0:T(8,128)S(1)} %scores.5), channel_id=1, source_target_pairs={{0,8},{1,9},{2,10},{3,11},{4,12},{5,13},{6,14},{7,15},{8,0},{9,1},... | collective-permute-start | bytes 3145736 | tf_op jit(solution)/shard_map/ppermute | solution.py:31
  112.4 2.0 %collective-permute-start.23 = (f32[192,512]{1,0:T(8,128)S(1)}, f32[192,512]{1,0:T(8,128)S(1)}, u32[]{:S(2)}, u32[]{:S(2)}) collective-permute-start(f32[192,512]{1,0:T(8,128)S(1)} %scores.7), channel_id=1, source_target_pairs={{0,8},{1,9},{2,10},{3,11},{4,12},{5,13},{6,14},{7,15},{8,0},{9,1},... | collective-permute-start | bytes 1179656 | tf_op jit(solution)/shard_map/ppermute | solution.py:31
  115.8 12.1 %all-to-all-start.1 = ((f32[8,8,512]{2,1,0:T(8,128)}), f32[8,8,512]{2,1,0:T(8,128)S(1)}, u32[]{:S(2)}, u32[]{:S(2)}) async-start(f32[8,8,512]{2,1,0:T(8,128)} %get-tuple-element.54), calls=%async_computation.1 | async-start | bytes 262144 | tf_op jit(solution)/shard_map/all_to_all | solution.py:385
  129.8 16.1 %all-to-all-start.2 = ((f32[32,1,512]{2,1,0:T(1,128)}), f32[32,1,512]{2,1,0:T(1,128)S(1)}, u32[]{:S(2)}, u32[]{:S(2)}) async-start(f32[32,1,512]{2,1,0:T(1,128)} %get-tuple-element.58), calls=%async_computation.2 | async-start | bytes 131072 | tf_op jit(solution)/shard_map/all_to_all | solution.py:387

commit v5 on v4

--- a/solution.py
+++ b/solution.py
@@ -49,6 +49,12 @@
 
 def from_above(array):
     return permute(array, lambda z, ylo, core, x, yhi: (z - 1, ylo, core, x, yhi))
+
+
+def both_ways_along_x(array):
+    return permute(
+        array, lambda z, ylo, core, x, yhi: (z, ylo, core, x + 1 - 2 * core, yhi)
+    )
 
 
 def from_left(array):
@@ -245,7 +251,7 @@
         out_specs=[vmem()] * outs,
         compiler_params=params(16),
         cost_estimate=pl.CostEstimate(
-            flops=2 * len(panels) * CLS * 8 * GROUP_ROWS * QUART * outs,
+            flops=8 * len(panels) * CLS * 8 * GROUP_ROWS * QUART * outs,
             bytes_accessed=8 * MIB,
             transcendentals=0,
         ),
@@ -347,16 +353,13 @@
     mine0 = pick(owners, got).reshape(CLS * 8, QUART)
     mine1, mine7 = from_above(mine0), from_below(mine0)
     theirs0 = other_ylo(mine0)
-    left, _ = together(left, mine0)
-    far0 = from_left(left[:1])
-    mine1, mine7, across, right = together(mine1, mine7, across, right)
-    far1 = from_right(right[1:])
+    turn, _ = together(jnp.where(lax.axis_index("dp") % 2 == 0, left, right), mine0)
+    far = both_ways_along_x(turn)
+    mine1, mine7, across = together(mine1, mine7, across)
     mine2, mine6 = from_above(mine1), from_below(mine7)
-    mine2, mine6, theirs0 = together(mine2, mine6, theirs0)
+    mine2, mine6, theirs0, across, far = together(mine2, mine6, theirs0, across, far)
     pair3 = from_above(jnp.stack([mine2, theirs0]))
     pair5 = from_below(jnp.stack([mine6, theirs0]))
-    far0, far1, across = together(far0, far1, across)
-    far = jnp.concatenate([far0, far1], axis=0)
     left_across, right_across, far_across = from_left(across), from_right(across), other_yhi(far)
     pair3, pair5 = together(pair3, pair5)
     mine3, theirs1 = pair3
@@ -366,6 +369,7 @@
     next4, next6 = together(next4, next6)
     theirs2, theirs6 = next4[half:], next6[half:]
     mine4 = jnp.concatenate([next6[:half], next4[:half]], axis=0)
+    theirs4 = other_ylo(mine4)
     theirs3, theirs5 = from_above(theirs2), from_below(theirs6)
     across = settle(across)
     whole = [own, across, right, right_across, far, far_across, left, left_across]
@@ -375,9 +379,8 @@
     (near_theirs,) = scores_of(near, whole, (1,), near_plan)
     near_other = other_core(near_theirs)
     (near_mine,) = scores_of(near, whole, (0,), near_plan)
-    last = [from_below(theirs5[:half]), from_above(theirs3[half:])]
-    near_mine, *last = together(near_mine, *last)
-    far_panels, far_plan = [theirs3, theirs5, jnp.concatenate(last, axis=0)], ((1, 3, 0),)
+    near_mine, theirs4 = together(near_mine, theirs4)
+    far_panels, far_plan = [theirs3, theirs5, theirs4], ((1, 3, 0),)
     (far_theirs,) = scores_of(far_panels, whole, (1,), far_plan)
     far_other = other_core(far_theirs)
     (far_mine,) = scores_of(far_panels, whole, (0,), far_plan)

time: 147 us -> 144 us (0.980)
  starting transfers between devices: 60.4 us -> 51.9 us
  waiting for transfers between devices: 65.3 us -> 70.2 us
    ppermute x24 -> x22, starting transfers between devices: 36.2 us -> 28.7 us  [permute(): return lax.ppermute(array, ('dp', 'orient'), pairs)]
    ppermute x24 -> x22, waiting for transfers between devices: 51.3 us -> 56.3 us  [permute(): return lax.ppermute(array, ('dp', 'orient'), pairs)]
  transfers between devices with their start and end apart: 27 -> 25, of which waited for: 15 -> 17; matrix products, arithmetic and copies ran while one was open for 1% -> 1% of each run, Pallas kernels for 5% -> 7%
where the time goes in v5:
time: 144 us; the launch traced here: 143 us
  waiting for transfers between devices  70.2 us (49%)
  starting transfers between devices  51.9 us (36%)
  Pallas kernels  17.1 us (12%)
  local copies, waits for them, and re-layouts  2.41 us (2%)
    ppermute x22, waiting for transfers between devices, permute(): return lax.ppermute(array, ('dp', 'orient'), pairs)  56.3 us
    ppermute x22, starting transfers between devices, permute(): return lax.ppermute(array, ('dp', 'orient'), pairs)  28.7 us
    all_to_all x1, starting transfers between devices, per_device(): got = lax.all_to_all(sent, 'dp', 0, 0)  11.3 us
    all_to_all x1, waiting for transfers between devices, per_device(): masses = lax.all_to_all(mass, 'dp', 0, 0)  7.08 us
    all_to_all x1, starting transfers between devices, per_device(): masses = lax.all_to_all(mass, 'dp', 0, 0)  6.97 us
    all_to_all x1, waiting for transfers between devices, per_device(): parts = lax.all_to_all(partial, 'orient', 0, 0)  6.79 us
    pallas_call x4, Pallas kernels, scores_of(): pl.pallas_call(functools.partial(scores_kernel, owners, plan), out_shape=...  6.1 us
    all_to_all x1, starting transfers between devices, per_device(): parts = lax.all_to_all(partial, 'orient', 0, 0)  4.98 us
  transfers between devices with their start and end apart: 25, of which 17 were waited for; matrix products, arithmetic and copies ran while one was open for 1% of the time, Pallas kernels for 7%

profile of v5, /device:TPU:1, one launch (start us, length us, event | category | flops | bytes accessed | tf_op | source)
XLA Modules:
  0.0 143.1 jit_solution(2880301802170679115)
XLA Ops:
  0.6 3.8 %panel.1 = bf16[256,2176]{1,0:T(8,128)(2,1)} custom-call(s32[8]{0:T(128)} %owners_ref.1, f32[8]{0:T(128)} %priors_hbm.1, bf16[1,64,8448]{2,1,0:T(8,128)(2,1)} %slot_hbm.1, f32[64,4224]{1,0:T(8,128)} %contrast_ref.1, f32[4224]{0:T(1024)} %noise_hbm.1), custom_call_target="tpu_custom_call" | custom-call | tf_op jit(solution)/shard_map/panel/pallas_call | solution.py:169
  4.5 11.3 %all-to-all-start = ((bf16[32,8,2176]{2,1,0:T(8,128)(2,1)}), bf16[32,8,2176]{2,1,0:T(8,128)(2,1)}, u32[]{:S(2)}, u32[]{:S(2)}) async-start(bf16[32,8,2176]{2,1,0:T(8,128)(2,1)} %bitcast.32), calls=%async_computation | async-start | bytes 2228224 | tf_op jit(solution)/shard_map/all_to_all | solution.py:345
  16.0 1.1 weigh.1
  17.2 0.4 collective-permute-start
  17.6 1.7 %collective-permute-done = bf16[2,64,2176]{2,1,0:T(8,128)(2,1)S(1)} collective-permute-done((bf16[2,64,2176]{2,1,0:T(8,128)(2,1)S(1)}, bf16[2,64,2176]{2,1,0:T(8,128)(2,1)S(1)}, u32[]{:S(2)}, u32[]{:S(2)}) %collective-permute-start) | collective-permute-done | bytes 557088 | tf_op jit(solution)/shard_map/ppermute | solution.py:31
  19.4 1.3 collective-permute-start.1
  20.7 1.5 %collective-permute-start.2 = (bf16[2,2,64,2176]{3,2,1,0:T(8,128)(2,1)S(1)}, bf16[2,2,64,2176]{3,2,1,0:T(8,128)(2,1)S(1)}, u32[]{:S(2)}, u32[]{:S(2)}) collective-permute-start(bf16[2,2,64,2176]{3,2,1,0:T(8,128)(2,1)S(1)} %pad_maximum_fusion.refs_13_.refs_3_), channel_id=1, source_target_pairs={{0,6},{1,7},{2,0},{3,1},{4,2},{5,3},{6,4},{7,5},{8,14},{9,15},{10,... | collective-permute-start | bytes 3342344 | tf_op jit(solution)/shard_map/ppermute | solution.py:31
  22.1 2.6 %collective-permute-start.5 = (bf16[2,2,64,2176]{3,2,1,0:T(8,128)(2,1)S(1)}, bf16[2,2,64,2176]{3,2,1,0:T(8,128)(2,1)}, u32[]{:S(2)}, u32[]{:S(2)}) collective-permute-start(bf16[2,2,64,2176]{3,2,1,0:T(8,128)(2,1)S(1)} %pad_maximum_fusion.refs_13_.refs_3_), channel_id=1, source_target_pairs={{0,1},{1,0},{2,3},{3,2},{4,5},{5,4},{6,7},{7,6},{8,9},{9,8},{10,11... | collective-permute-start | bytes 3342344 | tf_op jit(solution)/shard_map/ppermute | solution.py:31
  24.7 21.9 %collective-permute-done.1.refs_19_.refs_9_ = bf16[2,2,64,2176]{3,2,1,0:T(8,128)(2,1)S(1)} collective-permute-done((bf16[2,2,64,2176]{3,2,1,0:T(8,128)(2,1)S(1)}, bf16[2,2,64,2176]{3,2,1,0:T(8,128)(2,1)S(1)}, u32[]{:S(2)}, u32[]{:S(2)}) %collective-permute-start.1) | collective-permute-done | bytes 1114144 | tf_op jit(solution)/shard_map/ppermute | solution.py:31
  46.8 1.5 %pick.1 = bf16[8,8,2176]{2,1,0:T(8,128)(2,1)S(1)} custom-call(s32[8]{0:T(128)S(1)} %copy-done.2, bf16[32,8,2176]{2,1,0:T(8,128)(2,1)} %all-to-all-done.got_ref), custom_call_target="tpu_custom_call" | custom-call | tf_op jit(solution)/shard_map/pick/pallas_call | solution.py:199
  48.3 2.4 %collective-permute-start.9 = (bf16[2,2,64,2176]{3,2,1,0:T(8,128)(2,1)S(1)}, bf16[2,2,64,2176]{3,2,1,0:T(8,128)(2,1)S(1)}, u32[]{:S(2)}, u32[]{:S(2)}) collective-permute-start(bf16[2,2,64,2176]{3,2,1,0:T(8,128)(2,1)S(1)} %broadcast_select_fusion), channel_id=1, source_target_pairs={{0,2},{1,3},{2,4},{3,5},{4,6},{5,7},{6,0},{7,1},{8,14},{9,15},{10,... | collective-permute-start | bytes 3342344 | tf_op jit(solution)/shard_map/ppermute | solution.py:31
  50.7 2.6 %collective-permute-start.3 = (bf16[64,2176]{1,0:T(8,128)(2,1)S(1)}, bf16[64,2176]{1,0:T(8,128)(2,1)S(1)}, u32[]{:S(2)}, u32[]{:S(2)}) collective-permute-start(bf16[64,2176]{1,0:T(8,128)(2,1)S(1)} %bitcast.24), channel_id=1, source_target_pairs={{0,224},{1,225},{2,226},{3,227},{4,228},{5,229},{6,230},{7,231},{8... | collective-permute-start | bytes 835592 | tf_op jit(solution)/shard_map/ppermute | solution.py:31
  53.3 1.1 collective-permute-start.8
  54.4 3.5 %collective-permute-done.5.in_ref = bf16[2,2,64,2176]{3,2,1,0:T(8,128)(2,1)} collective-permute-done((bf16[2,2,64,2176]{3,2,1,0:T(8,128)(2,1)S(1)}, bf16[2,2,64,2176]{3,2,1,0:T(8,128)(2,1)}, u32[]{:S(2)}, u32[]{:S(2)}) %collective-permute-start.5) | collective-permute-done | bytes 1114144 | tf_op jit(solution)/shard_map/ppermute | solution.py:31
  57.9 1.2 collective-permute-done.3.refs_1_
  59.1 3.1 %collective-permute-done.4.refs_4_ = bf16[64,2176]{1,0:T(8,128)(2,1)S(1)} collective-permute-done((bf16[64,2176]{1,0:T(8,128)(2,1)S(1)}, bf16[64,2176]{1,0:T(8,128)(2,1)S(1)}, u32[]{:S(2)}, u32[]{:S(2)}) %collective-permute-start.4) | collective-permute-done | bytes 278560 | tf_op jit(solution)/shard_map/ppermute | solution.py:31
  62.5 1.1 collective-permute-start.7
  63.7 0.5 collective-permute-done.8.refs_8_
  64.1 4.9 %collective-permute-done.6.refs_2_ = bf16[64,2176]{1,0:T(8,128)(2,1)S(1)} collective-permute-done((bf16[64,2176]{1,0:T(8,128)(2,1)S(1)}, bf16[64,2176]{1,0:T(8,128)(2,1)S(1)}, u32[]{:S(2)}, u32[]{:S(2)}) %collective-permute-start.6) | collective-permute-done | bytes 278560 | tf_op jit(solution)/shard_map/ppermute | solution.py:31
  69.0 1.6 %collective-permute-done.7.refs_3_ = bf16[64,2176]{1,0:T(8,128)(2,1)S(1)} collective-permute-done((bf16[64,2176]{1,0:T(8,128)(2,1)S(1)}, bf16[64,2176]{1,0:T(8,128)(2,1)S(1)}, u32[]{:S(2)}, u32[]{:S(2)}) %collective-permute-start.7) | collective-permute-done | bytes 278560 | tf_op jit(solution)/shard_map/ppermute | solution.py:31
  71.0 1.2 collective-permute-start.11
  72.2 1.5 %collective-permute-start.16 = (bf16[2,2,64,2176]{3,2,1,0:T(8,128)(2,1)}, bf16[2,2,64,2176]{3,2,1,0:T(8,128)(2,1)S(1)}, u32[]{:S(2)}, u32[]{:S(2)}) collective-permute-start(bf16[2,2,64,2176]{3,2,1,0:T(8,128)(2,1)} %collective-permute-done.5.in_ref), channel_id=1, source_target_pairs={{0,2},{1,3},{2,4},{3,5},{4,6},{5,7},{6,0},{7,1},{8,10},{9,11},{10,... | collective-permute-start | bytes 3342344 | tf_op jit(solution)/shard_map/ppermute | solution.py:31
  73.7 2.3 %collective-permute-start.15 = (bf16[2,2,64,2176]{3,2,1,0:T(8,128)(2,1)S(1)}, bf16[2,2,64,2176]{3,2,1,0:T(8,128)(2,1)S(1)}, u32[]{:S(2)}, u32[]{:S(2)}) collective-permute-start(bf16[2,2,64,2176]{3,2,1,0:T(8,128)(2,1)S(1)} %collective-permute-done.9.refs_17_.refs_7_), channel_id=1, source_target_pairs={{0,1},{1,0},{2,3},{3,2},{4,5},{5,4},{6,7},{7,6},{8,9},{9,8},{10,11... | collective-permute-start | bytes 3342344 | tf_op jit(solution)/shard_map/ppermute | solution.py:31
  76.0 6.7 %collective-permute-done.10 = bf16[2,64,2176]{2,1,0:T(8,128)(2,1)S(1)} collective-permute-done((bf16[2,64,2176]{2,1,0:T(8,128)(2,1)S(1)}, bf16[2,64,2176]{2,1,0:T(8,128)(2,1)S(1)}, u32[]{:S(2)}, u32[]{:S(2)}) %collective-permute-start.10) | collective-permute-done | bytes 557088 | tf_op jit(solution)/shard_map/ppermute | solution.py:31
  82.6 1.5 %collective-permute-done.11 = bf16[2,64,2176]{2,1,0:T(8,128)(2,1)S(1)} collective-permute-done((bf16[2,64,2176]{2,1,0:T(8,128)(2,1)S(1)}, bf16[2,64,2176]{2,1,0:T(8,128)(2,1)S(1)}, u32[]{:S(2)}, u32[]{:S(2)}) %collective-permute-start.11) | collective-permute-done | bytes 557088 | tf_op jit(solution)/shard_map/ppermute | solution.py:31
  84.7 1.3 collective-permute-start.13
  85.9 1.3 settle.1.refs_14_.refs_4_
  87.2 5.1 %collective-permute-done.12 = bf16[96,2176]{1,0:T(8,128)(2,1)S(1)} collective-permute-done((bf16[96,2176]{1,0:T(8,128)(2,1)S(1)}, bf16[96,2176]{1,0:T(8,128)(2,1)S(1)}, u32[]{:S(2)}, u32[]{:S(2)}) %collective-permute-start.12) | collective-permute-done | bytes 417824 | tf_op jit(solution)/shard_map/ppermute | solution.py:31
  92.3 1.6 %collective-permute-done.13 = bf16[96,2176]{1,0:T(8,128)(2,1)S(1)} collective-permute-done((bf16[96,2176]{1,0:T(8,128)(2,1)S(1)}, bf16[96,2176]{1,0:T(8,128)(2,1)S(1)}, u32[]{:S(2)}, u32[]{:S(2)}) %collective-permute-start.13) | collective-permute-done | bytes 417824 | tf_op jit(solution)/shard_map/ppermute | solution.py:31
  94.1 0.7 collective-permute-start.17
  95.0 0.7 collective-permute-done.14.refs_16_.refs_6_
  95.7 0.6 collective-permute-start.20
  96.3 1.6 %collective-permute-done.15.refs_18_.refs_8_ = bf16[2,2,64,2176]{3,2,1,0:T(8,128)(2,1)S(1)} collective-permute-done((bf16[2,2,64,2176]{3,2,1,0:T(8,128)(2,1)S(1)}, bf16[2,2,64,2176]{3,2,1,0:T(8,128)(2,1)S(1)}, u32[]{:S(2)}, u32[]{:S(2)}) %collective-permute-start.15) | collective-permute-done | bytes 1114144 | tf_op jit(solution)/shard_map/ppermute | solution.py:31
  97.9 2.2 %scores.5 = f32[512,512]{1,0:T(8,128)S(1)} custom-call(bf16[64,2176]{1,0:T(8,128)(2,1)S(1)} %bitcast.27, bf16[64,2176]{1,0:T(8,128)(2,1)S(1)} %collective-permute-done.3.refs_1_, bf16[64,2176]{1,0:T(8,128)(2,1)S(1)} %collective-permute-done.6.refs_2_, bf16[64,2176]{1,0:T(8,128)(2,1)S(1)} %collective-permute-done.7.refs_3_, ...), custom_call_target="tpu_custom_call" | custom-call | flops 7415529472 | bytes 8388608 | tf_op jit(solution)/shard_map/scores/pallas_call | solution.py:247
  100.1 6.9 %collective-permute-start.18 = (f32[512,512]{1,0:T(8,128)S(1)}, f32[512,512]{1,0:T(8,128)S(1)}, u32[]{:S(2)}, u32[]{:S(2)}) collective-permute-start(f32[512,512]{1,0:T(8,128)S(1)} %scores.5), channel_id=1, source_target_pairs={{0,8},{1,9},{2,10},{3,11},{4,12},{5,13},{6,14},{7,15},{8,0},{9,1},... | collective-permute-start | bytes 3145736 | tf_op jit(solution)/shard_map/ppermute | solution.py:31
  106.9 2.2 %scores.4.near_ref = f32[512,512]{1,0:T(8,128)S(1)} custom-call(bf16[64,2176]{1,0:T(8,128)(2,1)S(1)} %bitcast.28, bf16[64,2176]{1,0:T(8,128)(2,1)S(1)} %collective-permute-done.3.refs_1_, bf16[64,2176]{1,0:T(8,128)(2,1)S(1)} %collective-permute-done.6.refs_2_, bf16[64,2176]{1,0:T(8,128)(2,1)S(1)} %collective-permute-done.7.refs_3_, ...), custom_call_target="tpu_custom_call" | custom-call | flops 7415529472 | bytes 8388608 | tf_op jit(solution)/shard_map/scores/pallas_call | solution.py:247
  109.1 0.9 scores.7
  110.1 0.9 scores.6.far_ref
  111.0 0.8 collective-permute-done.21.far_other_ref
  111.8 1.4 norms.1
  113.2 5.0 %all-to-all-start.1 = ((f32[8,8,512]{2,1,0:T(8,128)}), f32[8,8,512]{2,1,0:T(8,128)S(1)}, u32[]{:S(2)}, u32[]{:S(2)}) async-start(f32[8,8,512]{2,1,0:T(8,128)} %get-tuple-element.48), calls=%async_computation.1 | async-start | bytes 262144 | tf_op jit(solution)/shard_map/all_to_all | solution.py:388
  118.2 6.8 %all-to-all-done.1.parts_ref = f32[8,8,512]{2,1,0:T(8,128)S(1)} async-done(((f32[8,8,512]{2,1,0:T(8,128)}), f32[8,8,512]{2,1,0:T(8,128)S(1)}, u32[]{:S(2)}, u32[]{:S(2)}) %all-to-all-start.1) | async-done | bytes 131104 | tf_op jit(solution)/shard_map/all_to_all | solution.py:388
  125.0 1.9 %finish.1 = (f32[1,512]{1,0:T(1,128)S(1)}, f32[8,512]{1,0:T(8,128)S(1)}, f32[32,1,512]{2,1,0:T(1,128)}) custom-call(f32[8,8,512]{2,1,0:T(8,128)S(1)} %all-to-all-done.1.parts_ref, f32[512,512]{1,0:T(8,128)S(1)} %get-tuple-element.49.scores_ref), custom_call_target="tpu_custom_call" | custom-call | tf_op jit(solution)/shard_map/finish/pallas_call | solution.py:321
  126.9 7.0 %all-to-all-start.2 = ((f32[32,1,512]{2,1,0:T(1,128)}), f32[32,1,512]{2,1,0:T(1,128)S(1)}, u32[]{:S(2)}, u32[]{:S(2)}) async-start(f32[32,1,512]{2,1,0:T(1,128)} %get-tuple-element.52), calls=%async_computation.2 | async-start | bytes 131072 | tf_op jit(solution)/shard_map/all_to_all | solution.py:390
  133.9 0.6 dynamic-slice_bitcast_fusion
  134.5 0.7 constant_dynamic-slice_fusion
  135.2 7.1 %all-to-all-done.2 = f32[32,1,512]{2,1,0:T(1,128)S(1)} async-done(((f32[32,1,512]{2,1,0:T(1,128)}), f32[32,1,512]{2,1,0:T(1,128)S(1)}, u32[]{:S(2)}, u32[]{:S(2)}) %all-to-all-start.2) | async-done | bytes 65568 | tf_op jit(solution)/shard_map/all_to_all | solution.py:390
  142.4 0.7 reshape.32
  (46 shorter events, 2.3 us)
Async XLA Ops:
  4.4 11.4 %copy-start.3 = (f32[4224]{0:T(1024)S(1)}, f32[4224]{0:T(1024)}, u32[]{:S(2)}) copy-start(f32[4224]{0:T(1024)} %noise_hbm.1) | copy-start | bytes 50692
  4.4 11.4 %copy-start.4 = (s32[64]{0:T(128)S(1)}, s32[64]{0:T(128)}, u32[]{:S(2)}) copy-start(s32[64]{0:T(128)} %param.8) | copy-start | bytes 772
  4.5 11.5 %copy-start = (f32[64,4224]{1,0:T(8,128)S(1)}, f32[64,4224]{1,0:T(8,128)}, u32[]{:S(2)}) copy-start(f32[64,4224]{1,0:T(8,128)} %contrast_ref.1) | copy-start | bytes 3244036
  4.5 11.5 %copy-start.1 = (bf16[64,8448]{1,0:T(8,128)(2,1)S(1)}, bf16[64,8448]{1,0:T(8,128)(2,1)}, u32[]{:S(2)}) copy-start(bf16[64,8448]{1,0:T(8,128)(2,1)} %images_ref) | copy-start | bytes 3244036
  4.5 42.1 %all-to-all-start = ((bf16[32,8,2176]{2,1,0:T(8,128)(2,1)}), bf16[32,8,2176]{2,1,0:T(8,128)(2,1)}, u32[]{:S(2)}, u32[]{:S(2)}) async-start(bf16[32,8,2176]{2,1,0:T(8,128)(2,1)} %bitcast.32), calls=%async_computation | async-start | bytes 2228224 | tf_op jit(solution)/shard_map/all_to_all | solution.py:345
  17.2 2.0 %collective-permute-start = (bf16[2,64,2176]{2,1,0:T(8,128)(2,1)S(1)}, bf16[2,64,2176]{2,1,0:T(8,128)(2,1)S(1)}, u32[]{:S(2)}, u32[]{:S(2)}) collective-permute-start(bf16[2,64,2176]{2,1,0:T(8,128)(2,1)S(1)} %get-tuple-element.54), channel_id=1, source_target_pairs={{0,8},{1,9},{2,10},{3,11},{4,12},{5,13},{6,14},{7,15},{8,0},{9,1},... | collective-permute-start | bytes 1671176 | tf_op jit(solution)/shard_map/ppermute | solution.py:31
  19.4 27.3 %collective-permute-start.1 = (bf16[2,2,64,2176]{3,2,1,0:T(8,128)(2,1)S(1)}, bf16[2,2,64,2176]{3,2,1,0:T(8,128)(2,1)S(1)}, u32[]{:S(2)}, u32[]{:S(2)}) collective-permute-start(bf16[2,2,64,2176]{3,2,1,0:T(8,128)(2,1)S(1)} %pad_maximum_fusion.refs_13_.refs_3_), channel_id=1, source_target_pairs={{0,2},{1,3},{2,4},{3,5},{4,6},{5,7},{6,0},{7,1},{8,10},{9,11},{10,... | collective-permute-start | bytes 3342344 | tf_op jit(solution)/shard_map/ppermute | solution.py:31
  20.7 26.0 %collective-permute-start.2 = (bf16[2,2,64,2176]{3,2,1,0:T(8,128)(2,1)S(1)}, bf16[2,2,64,2176]{3,2,1,0:T(8,128)(2,1)S(1)}, u32[]{:S(2)}, u32[]{:S(2)}) collective-permute-start(bf16[2,2,64,2176]{3,2,1,0:T(8,128)(2,1)S(1)} %pad_maximum_fusion.refs_13_.refs_3_), channel_id=1, source_target_pairs={{0,6},{1,7},{2,0},{3,1},{4,2},{5,3},{6,4},{7,5},{8,14},{9,15},{10,... | collective-permute-start | bytes 3342344 | tf_op jit(solution)/shard_map/ppermute | solution.py:31
  22.1 24.6 %copy-start.2 = (s32[8]{0:T(128)S(1)}, s32[8]{0:T(128)}, u32[]{:S(2)}) copy-start(s32[8]{0:T(128)} %owners_ref.1) | copy-start | bytes 100
  22.1 35.8 %collective-permute-start.5 = (bf16[2,2,64,2176]{3,2,1,0:T(8,128)(2,1)S(1)}, bf16[2,2,64,2176]{3,2,1,0:T(8,128)(2,1)}, u32[]{:S(2)}, u32[]{:S(2)}) collective-permute-start(bf16[2,2,64,2176]{3,2,1,0:T(8,128)(2,1)S(1)} %pad_maximum_fusion.refs_13_.refs_3_), channel_id=1, source_target_pairs={{0,1},{1,0},{2,3},{3,2},{4,5},{5,4},{6,7},{7,6},{8,9},{9,8},{10,11... | collective-permute-start | bytes 3342344 | tf_op jit(solution)/shard_map/ppermute | solution.py:31
  48.3 22.3 %collective-permute-start.9 = (bf16[2,2,64,2176]{3,2,1,0:T(8,128)(2,1)S(1)}, bf16[2,2,64,2176]{3,2,1,0:T(8,128)(2,1)S(1)}, u32[]{:S(2)}, u32[]{:S(2)}) collective-permute-start(bf16[2,2,64,2176]{3,2,1,0:T(8,128)(2,1)S(1)} %broadcast_select_fusion), channel_id=1, source_target_pairs={{0,2},{1,3},{2,4},{3,5},{4,6},{5,7},{6,0},{7,1},{8,14},{9,15},{10,... | collective-permute-start | bytes 3342344 | tf_op jit(solution)/shard_map/ppermute | solution.py:31
  50.7 8.4 %collective-permute-start.3 = (bf16[64,2176]{1,0:T(8,128)(2,1)S(1)}, bf16[64,2176]{1,0:T(8,128)(2,1)S(1)}, u32[]{:S(2)}, u32[]{:S(2)}) collective-permute-start(bf16[64,2176]{1,0:T(8,128)(2,1)S(1)} %bitcast.24), channel_id=1, source_target_pairs={{0,224},{1,225},{2,226},{3,227},{4,228},{5,229},{6,230},{7,231},{8... | collective-permute-start | bytes 835592 | tf_op jit(solution)/shard_map/ppermute | solution.py:31
  53.3 8.9 %collective-permute-start.4 = (bf16[64,2176]{1,0:T(8,128)(2,1)S(1)}, bf16[64,2176]{1,0:T(8,128)(2,1)S(1)}, u32[]{:S(2)}, u32[]{:S(2)}) collective-permute-start(bf16[64,2176]{1,0:T(8,128)(2,1)S(1)} %bitcast.25), channel_id=1, source_target_pairs={{0,32},{1,33},{2,34},{3,35},{4,36},{5,37},{6,38},{7,39},{8,40},{9,... | collective-permute-start | bytes 835592 | tf_op jit(solution)/shard_map/ppermute | solution.py:31
  53.3 10.9 %collective-permute-start.8 = (bf16[64,2176]{1,0:T(8,128)(2,1)S(1)}, bf16[64,2176]{1,0:T(8,128)(2,1)S(1)}, u32[]{:S(2)}, u32[]{:S(2)}) collective-permute-start(bf16[64,2176]{1,0:T(8,128)(2,1)S(1)} %bitcast.26), channel_id=1, source_target_pairs={{0,16},{1,17},{2,18},{3,19},{4,20},{5,21},{6,22},{7,23},{8,24},{9,... | collective-permute-start | bytes 835592 | tf_op jit(solution)/shard_map/ppermute | solution.py:31
  62.2 6.8 %collective-permute-start.6 = (bf16[64,2176]{1,0:T(8,128)(2,1)S(1)}, bf16[64,2176]{1,0:T(8,128)(2,1)S(1)}, u32[]{:S(2)}, u32[]{:S(2)}) collective-permute-start(bf16[64,2176]{1,0:T(8,128)(2,1)S(1)} %collective-permute-done.3.refs_1_), channel_id=1, source_target_pairs={{0,224},{1,225},{2,226},{3,227},{4,228},{5,229},{6,230},{7,231},{8... | collective-permute-start | bytes 835592 | tf_op jit(solution)/shard_map/ppermute | solution.py:31
  62.5 8.0 %collective-permute-start.7 = (bf16[64,2176]{1,0:T(8,128)(2,1)S(1)}, bf16[64,2176]{1,0:T(8,128)(2,1)S(1)}, u32[]{:S(2)}, u32[]{:S(2)}) collective-permute-start(bf16[64,2176]{1,0:T(8,128)(2,1)S(1)} %collective-permute-done.4.refs_4_), channel_id=1, source_target_pairs={{0,32},{1,33},{2,34},{3,35},{4,36},{5,37},{6,38},{7,39},{8,40},{9,... | collective-permute-start | bytes 835592 | tf_op jit(solution)/shard_map/ppermute | solution.py:31
  70.7 12.0 %collective-permute-start.10 = (bf16[2,64,2176]{2,1,0:T(8,128)(2,1)S(1)}, bf16[2,64,2176]{2,1,0:T(8,128)(2,1)S(1)}, u32[]{:S(2)}, u32[]{:S(2)}) collective-permute-start(bf16[2,64,2176]{2,1,0:T(8,128)(2,1)S(1)} %get-tuple-element.60), channel_id=1, source_target_pairs={{0,224},{1,225},{2,226},{3,227},{4,228},{5,229},{6,230},{7,231},{8... | collective-permute-start | bytes 1671176 | tf_op jit(solution)/shard_map/ppermute | solution.py:31
  71.0 13.1 %collective-permute-start.11 = (bf16[2,64,2176]{2,1,0:T(8,128)(2,1)S(1)}, bf16[2,64,2176]{2,1,0:T(8,128)(2,1)S(1)}, u32[]{:S(2)}, u32[]{:S(2)}) collective-permute-start(bf16[2,64,2176]{2,1,0:T(8,128)(2,1)S(1)} %get-tuple-element.59), channel_id=1, source_target_pairs={{0,32},{1,33},{2,34},{3,35},{4,36},{5,37},{6,38},{7,39},{8,40},{9,... | collective-permute-start | bytes 1671176 | tf_op jit(solution)/shard_map/ppermute | solution.py:31
  72.2 23.5 %collective-permute-start.14 = (bf16[2,2,64,2176]{3,2,1,0:T(8,128)(2,1)}, bf16[2,2,64,2176]{3,2,1,0:T(8,128)(2,1)S(1)}, u32[]{:S(2)}, u32[]{:S(2)}) collective-permute-start(bf16[2,2,64,2176]{3,2,1,0:T(8,128)(2,1)} %collective-permute-done.5.in_ref), channel_id=1, source_target_pairs={{0,6},{1,7},{2,0},{3,1},{4,2},{5,3},{6,4},{7,5},{8,14},{9,15},{10,... | collective-permute-start | bytes 3342344 | tf_op jit(solution)/shard_map/ppermute | solution.py:31
  72.2 25.7 %collective-permute-start.16 = (bf16[2,2,64,2176]{3,2,1,0:T(8,128)(2,1)}, bf16[2,2,64,2176]{3,2,1,0:T(8,128)(2,1)S(1)}, u32[]{:S(2)}, u32[]{:S(2)}) collective-permute-start(bf16[2,2,64,2176]{3,2,1,0:T(8,128)(2,1)} %collective-permute-done.5.in_ref), channel_id=1, source_target_pairs={{0,2},{1,3},{2,4},{3,5},{4,6},{5,7},{6,0},{7,1},{8,10},{9,11},{10,... | collective-permute-start | bytes 3342344 | tf_op jit(solution)/shard_map/ppermute | solution.py:31
  73.7 24.2 %collective-permute-start.15 = (bf16[2,2,64,2176]{3,2,1,0:T(8,128)(2,1)S(1)}, bf16[2,2,64,2176]{3,2,1,0:T(8,128)(2,1)S(1)}, u32[]{:S(2)}, u32[]{:S(2)}) collective-permute-start(bf16[2,2,64,2176]{3,2,1,0:T(8,128)(2,1)S(1)} %collective-permute-done.9.refs_17_.refs_7_), channel_id=1, source_target_pairs={{0,1},{1,0},{2,3},{3,2},{4,5},{5,4},{6,7},{7,6},{8,9},{9,8},{10,11... | collective-permute-start | bytes 3342344 | tf_op jit(solution)/shard_map/ppermute | solution.py:31
  84.3 8.0 %collective-permute-start.12 = (bf16[96,2176]{1,0:T(8,128)(2,1)S(1)}, bf16[96,2176]{1,0:T(8,128)(2,1)S(1)}, u32[]{:S(2)}, u32[]{:S(2)}) collective-permute-start(bf16[96,2176]{1,0:T(8,128)(2,1)S(1)} %pad_maximum_fusion.3), channel_id=1, source_target_pairs={{0,224},{1,225},{2,226},{3,227},{4,228},{5,229},{6,230},{7,231},{8... | collective-permute-start | bytes 1253384 | tf_op jit(solution)/shard_map/ppermute | solution.py:31
  84.7 9.3 %collective-permute-start.13 = (bf16[96,2176]{1,0:T(8,128)(2,1)S(1)}, bf16[96,2176]{1,0:T(8,128)(2,1)S(1)}, u32[]{:S(2)}, u32[]{:S(2)}) collective-permute-start(bf16[96,2176]{1,0:T(8,128)(2,1)S(1)} %pad_maximum_fusion.4), channel_id=1, source_target_pairs={{0,32},{1,33},{2,34},{3,35},{4,36},{5,37},{6,38},{7,39},{8,40},{9,... | collective-permute-start | bytes 1253384 | tf_op jit(solution)/shard_map/ppermute | solution.py:31
  94.1 15.0 %collective-permute-start.17 = (bf16[64,2176]{1,0:T(8,128)(2,1)S(1)}, bf16[64,2176]{1,0:T(8,128)(2,1)S(1)}, u32[]{:S(2)}, u32[]{:S(2)}) collective-permute-start(bf16[64,2176]{1,0:T(8,128)(2,1)S(1)} %pad_maximum_fusion.5.refs_7_), channel_id=1, source_target_pairs={{0,16},{1,17},{2,18},{3,19},{4,20},{5,21},{6,22},{7,23},{8,24},{9,... | collective-permute-start | bytes 835592 | tf_op jit(solution)/shard_map/ppermute | solution.py:31
  94.8 14.3 %collective-permute-start.19 = (bf16[64,2176]{1,0:T(8,128)(2,1)S(1)}, bf16[64,2176]{1,0:T(8,128)(2,1)S(1)}, u32[]{:S(2)}, u32[]{:S(2)}) collective-permute-start(bf16[64,2176]{1,0:T(8,128)(2,1)S(1)} %slice.40.refs_10_), channel_id=1, source_target_pairs={{0,224},{1,225},{2,226},{3,227},{4,228},{5,229},{6,230},{7,231},{8... | collective-permute-start | bytes 835592 | tf_op jit(solution)/shard_map/ppermute | solution.py:31
  95.7 13.4 %collective-permute-start.20 = (bf16[64,2176]{1,0:T(8,128)(2,1)S(1)}, bf16[64,2176]{1,0:T(8,128)(2,1)S(1)}, u32[]{:S(2)}, u32[]{:S(2)}) collective-permute-start(bf16[64,2176]{1,0:T(8,128)(2,1)S(1)} %slice.41.refs_11_), channel_id=1, source_target_pairs={{0,32},{1,33},{2,34},{3,35},{4,36},{5,37},{6,38},{7,39},{8,40},{9,... | collective-permute-start | bytes 835592 | tf_op jit(solution)/shard_map/ppermute | solution.py:31
  100.1 11.8 %collective-permute-start.18 = (f32[512,512]{1,0:T(8,128)S(1)}, f32[512,512]{1,0:T(8,128)S(1)}, u32[]{:S(2)}, u32[]{:S(2)}) collective-permute-start(f32[512,512]{1,0:T(8,128)S(1)} %scores.5), channel_id=1, source_target_pairs={{0,8},{1,9},{2,10},{3,11},{4,12},{5,13},{6,14},{7,15},{8,0},{9,1},... | collective-permute-start | bytes 3145736 | tf_op jit(solution)/shard_map/ppermute | solution.py:31
  110.0 1.8 %collective-permute-start.21 = (f32[192,512]{1,0:T(8,128)S(1)}, f32[192,512]{1,0:T(8,128)S(1)}, u32[]{:S(2)}, u32[]{:S(2)}) collective-permute-start(f32[192,512]{1,0:T(8,128)S(1)} %scores.7), channel_id=1, source_target_pairs={{0,8},{1,9},{2,10},{3,11},{4,12},{5,13},{6,14},{7,15},{8,0},{9,1},... | collective-permute-start | bytes 1179656 | tf_op jit(solution)/shard_map/ppermute | solution.py:31
  113.2 11.8 %all-to-all-start.1 = ((f32[8,8,512]{2,1,0:T(8,128)}), f32[8,8,512]{2,1,0:T(8,128)S(1)}, u32[]{:S(2)}, u32[]{:S(2)}) async-start(f32[8,8,512]{2,1,0:T(8,128)} %get-tuple-element.48), calls=%async_computation.1 | async-start | bytes 262144 | tf_op jit(solution)/shard_map/all_to_all | solution.py:388
  126.9 15.3 %all-to-all-start.2 = ((f32[32,1,512]{2,1,0:T(1,128)}), f32[32,1,512]{2,1,0:T(1,128)S(1)}, u32[]{:S(2)}, u32[]{:S(2)}) async-start(f32[32,1,512]{2,1,0:T(1,128)} %get-tuple-element.52), calls=%async_computation.2 | async-start | bytes 131072 | tf_op jit(solution)/shard_map/all_to_all | solution.py:390

commit v6 on v5

--- a/solution.py
+++ b/solution.py
@@ -114,8 +114,8 @@
 
 
 def panel_kernel(
-    owners_hbm, priors_hbm, slot_hbm, contrast_hbm, noise_hbm, out_ref,
-    owners_ref, priors_ref, slot_ref, contrast_ref, noise_ref, sems,
+    owners_hbm, priors_hbm, slot_hbm, contrast_hbm, noise_hbm, out_hbm,
+    owners_ref, priors_ref, slot_ref, contrast_ref, noise_ref, out_ref, sems,
 ):
     pairs = [
         (slot_hbm.at[0], slot_ref),
@@ -139,11 +139,14 @@
                 if stop < start + QUART:
                     part = jnp.concatenate([part, ext[rows]], axis=1)
                 parts.append(part)
-            at = (z * 4 + ylo * 2) * 8
-            out_ref[at : at + 16, :] = jnp.concatenate(parts, axis=0).astype(jnp.bfloat16)
+            out_ref[ylo, z] = jnp.concatenate(parts, axis=0).astype(jnp.bfloat16)
+        target = out_hbm.at[:, 16 * ylo : 16 * ylo + 16]
+        copy = pltpu.make_async_copy(out_ref.at[ylo], target, sems.at[5 + ylo])
+        copy.start()
+        return copy
 
     copies[0].wait()
-    chunks(0, None)
+    out0 = chunks(0, None)
     for copy in copies[1:]:
         copy.wait()
     dp = lax.axis_index("dp")
@@ -162,22 +165,25 @@
     rest = table - first
     second = rest.astype(jnp.bfloat16).astype(jnp.float32)
     third = rest - second
-    chunks(1, jnp.concatenate([first, second, third, jnp.zeros_like(first)], axis=1))
+    out1 = chunks(1, jnp.concatenate([first, second, third, jnp.zeros_like(first)], axis=1))
+    out0.wait()
+    out1.wait()
 
 
 def panel(owners, priors, slots, contrast, noise):
     return pl.pallas_call(
         panel_kernel,
-        out_shape=jax.ShapeDtypeStruct((NDP * 8, QUART), jnp.bfloat16),
+        out_shape=jax.ShapeDtypeStruct((NZ, 32, QUART), jnp.bfloat16),
         in_specs=[anywhere()] * 5,
-        out_specs=vmem(),
+        out_specs=anywhere(),
         scratch_shapes=[
             pltpu.SMEM((CLS,), jnp.int32),
             pltpu.SMEM((CLS,), jnp.float32),
             pltpu.VMEM((ROWS, FEAT), jnp.bfloat16),
             pltpu.VMEM((GRP, PIX), jnp.float32),
             pltpu.VMEM((PIX,), jnp.float32),
-            pltpu.SemaphoreType.DMA((5,)),
+            pltpu.VMEM((2, NZ, 16, QUART), jnp.bfloat16),
+            pltpu.SemaphoreType.DMA((7,)),
         ],
         compiler_params=params(60),
         name="panel",
@@ -268,18 +274,22 @@
 
 
 def norms_kernel(near_ref, near_other_ref, far_ref, far_other_ref, scores_ref, parts_ref):
-    _, _, _, x, yhi = place()
+    z, _, _, x, yhi = place()
     near = near_ref[...] + near_other_ref[...]
     far = far_ref[...] + far_other_ref[...]
     step = CLS * 8
     rows = [near[k : k + step] for k in range(0, NZ * step, step)]
     for k in range(3):
         rows[5 + k] += far[k * step : (k + 1) * step]
-    scores = jnp.concatenate([rows[k] for k in (0, 1, 2, 5, 7, 6, 3, 4)], axis=0)
-    scores_ref[...] = scores
-    scores = scores.reshape(NZ, CLS, 8, GROUP_ROWS)
-    maximum = jnp.max(jnp.max(scores, axis=0), axis=1, keepdims=True)
-    totals = jnp.sum(jnp.sum(jnp.exp(scores - maximum[None]), axis=0), axis=1)
+    rows = [rows[k].reshape(CLS, 8, GROUP_ROWS) for k in (0, 1, 2, 5, 7, 6, 3, 4)]
+    for k in range(NZ):
+        at = pl.multiple_of(((z + k) % NZ) * 8, 8)
+        for c in range(CLS):
+            scores_ref[c, pl.ds(at, 8), :] = rows[k][c]
+    maximum = functools.reduce(jnp.maximum, rows)
+    maximum = jnp.max(maximum, axis=1, keepdims=True)
+    totals = sum(jnp.exp(part - maximum) for part in rows)
+    totals = jnp.sum(totals, axis=1)
     lse = swap_halves(maximum[:, 0, :] + jnp.log(totals), yhi)
     lse = pltpu.roll(lse, x * 2 * ROWS, 1)
     parts_ref[...] = jnp.broadcast_to(lse[None], parts_ref.shape)
@@ -289,7 +299,7 @@
     return pl.pallas_call(
         norms_kernel,
         out_shape=(
-            jax.ShapeDtypeStruct((NZ * CLS * 8, GROUP_ROWS), jnp.float32),
+            jax.ShapeDtypeStruct((CLS, ORI, GROUP_ROWS), jnp.float32),
             jax.ShapeDtypeStruct((NOR, CLS, GROUP_ROWS), jnp.float32),
         ),
         in_specs=[vmem()] * 4,
@@ -300,7 +310,7 @@
 
 
 def finish_kernel(parts_ref, scores_ref, evidence_ref, posterior_ref, mass_ref):
-    z, _, _, x, yhi = place()
+    _, _, _, x, yhi = place()
     parts = parts_ref[...]
     maximum = jnp.max(parts, axis=0)
     class_lse = maximum + jnp.log(jnp.sum(jnp.exp(parts - maximum[None]), axis=0))
@@ -309,10 +319,14 @@
     evidence_ref[...] = evidence
     posterior_ref[...] = jnp.exp(class_lse - evidence)
     here = swap_halves(pltpu.roll(evidence, ((NX - x) % NX) * 2 * ROWS, 1), yhi)
-    terms = jnp.exp(scores_ref[...] - here)
-    ones = jnp.ones((8, GROUP_ROWS), jnp.float32)
-    mass = lax.dot_general(ones, terms, NT, precision=HIGH, preferred_element_type=jnp.float32)
-    mass = pltpu.roll(mass, z * CLS * 8, 1)[:1]
+    terms = jnp.exp(scores_ref[...].reshape(CLS * ORI, GROUP_ROWS) - here)
+    ones = jnp.ones((8, GROUP_ROWS), jnp.bfloat16)
+    mass = jnp.zeros((8, terms.shape[0]), jnp.float32)
+    for _ in range(3):
+        piece = terms.astype(jnp.bfloat16)
+        mass += lax.dot_general(ones, piece, NT, preferred_element_type=jnp.float32)
+        terms = terms - piece.astype(jnp.float32)
+    mass = mass[:1] * (CLS * ORI * NOR / (ROWS * NOR * NDP))
     for k in range(NDP):
         mass_ref[k] = mass
 
@@ -323,7 +337,7 @@
         out_shape=(
             jax.ShapeDtypeStruct((1, GROUP_ROWS), jnp.float32),
             jax.ShapeDtypeStruct((CLS, GROUP_ROWS), jnp.float32),
-            jax.ShapeDtypeStruct((NDP, 1, NZ * CLS * 8), jnp.float32),
+            jax.ShapeDtypeStruct((NDP, 1, CLS * ORI), jnp.float32),
         ),
         in_specs=[vmem(), vmem()],
         out_specs=(vmem(), vmem(), vmem()),
@@ -353,7 +367,7 @@
     mine0 = pick(owners, got).reshape(CLS * 8, QUART)
     mine1, mine7 = from_above(mine0), from_below(mine0)
     theirs0 = other_ylo(mine0)
-    turn, _ = together(jnp.where(lax.axis_index("dp") % 2 == 0, left, right), mine0)
+    turn = jnp.where(lax.axis_index("dp") % 2 == 0, left, right)
     far = both_ways_along_x(turn)
     mine1, mine7, across = together(mine1, mine7, across)
     mine2, mine6 = from_above(mine1), from_below(mine7)
@@ -388,9 +402,7 @@
     parts = lax.all_to_all(partial, "orient", 0, 0)
     evidence, posterior, mass = finish(parts, scores)
     masses = lax.all_to_all(mass, "dp", 0, 0)
-    normalise = CLS * ORI * NOR / (ROWS * NOR * NDP)
-    total = jnp.sum(masses, axis=(0, 1)) * normalise
-    orientation_mass = total.reshape(NZ, CLS, 8).transpose(1, 0, 2).reshape(CLS, ORI)
+    orientation_mass = jnp.sum(masses, axis=(0, 1)).reshape(CLS, ORI)
     log_evidence = lax.dynamic_slice_in_dim(evidence[0], orient * ROWS, ROWS, 0)
     class_posterior = lax.dynamic_slice_in_dim(posterior, orient * ROWS, ROWS, 1)
     return (log_evidence, class_posterior, orientation_mass)

time: 144 us -> 143 us (level)
  no operation moved by 1% of the time
where the time goes in v6:
time: 143 us; the launch traced here: 142 us
  waiting for transfers between devices  70.3 us (49%)
  starting transfers between devices  51.9 us (36%)
  Pallas kernels  16.4 us (11%)
  local copies, waits for them, and re-layouts  2.31 us (2%)
    ppermute x22, waiting for transfers between devices, permute(): return lax.ppermute(array, ('dp', 'orient'), pairs)  56.4 us
    ppermute x22, starting transfers between devices, permute(): return lax.ppermute(array, ('dp', 'orient'), pairs)  28.7 us
    all_to_all x1, starting transfers between devices, per_device(): got = lax.all_to_all(sent, 'dp', 0, 0)  11.3 us
    all_to_all x1, waiting for transfers between devices, per_device(): masses = lax.all_to_all(mass, 'dp', 0, 0)  7.08 us
    all_to_all x1, starting transfers between devices, per_device(): masses = lax.all_to_all(mass, 'dp', 0, 0)  6.86 us
    all_to_all x1, waiting for transfers between devices, per_device(): parts = lax.all_to_all(partial, 'orient', 0, 0)  6.79 us
    pallas_call x4, Pallas kernels, scores_of(): pl.pallas_call(functools.partial(scores_kernel, owners, plan), out_shape=...  6.1 us
    all_to_all x1, starting transfers between devices, per_device(): parts = lax.all_to_all(partial, 'orient', 0, 0)  5.02 us
  transfers between devices with their start and end apart: 25, of which 17 were waited for; matrix products, arithmetic and copies ran while one was open for 1% of the time, Pallas kernels for 7%

profile of v6, /device:TPU:1, one launch (start us, length us, event | category | flops | bytes accessed | tf_op | source)
XLA Modules:
  0.0 142.3 jit_solution(15431205492386482310)
XLA Ops:
  0.6 3.6 %panel.1 = bf16[8,32,2176]{2,1,0:T(8,128)(2,1)} custom-call(s32[8]{0:T(128)} %owners_ref.1, f32[8]{0:T(128)} %priors_hbm.1, bf16[1,64,8448]{2,1,0:T(8,128)(2,1)} %slot_hbm.1, f32[64,4224]{1,0:T(8,128)} %contrast_ref.1, f32[4224]{0:T(1024)} %noise_hbm.1), custom_call_target="tpu_custom_call" | custom-call | tf_op jit(solution)/shard_map/panel/pallas_call | solution.py:174
  4.3 11.3 %all-to-all-start = ((bf16[32,8,2176]{2,1,0:T(8,128)(2,1)}), bf16[32,8,2176]{2,1,0:T(8,128)(2,1)}, u32[]{:S(2)}, u32[]{:S(2)}) async-start(bf16[32,8,2176]{2,1,0:T(8,128)(2,1)} %bitcast.31), calls=%async_computation | async-start | bytes 2228224 | tf_op jit(solution)/shard_map/all_to_all | solution.py:359
  15.8 1.1 weigh.1
  17.0 0.4 collective-permute-start
  17.4 1.6 %collective-permute-done = bf16[2,64,2176]{2,1,0:T(8,128)(2,1)S(1)} collective-permute-done((bf16[2,64,2176]{2,1,0:T(8,128)(2,1)S(1)}, bf16[2,64,2176]{2,1,0:T(8,128)(2,1)S(1)}, u32[]{:S(2)}, u32[]{:S(2)}) %collective-permute-start) | collective-permute-done | bytes 557088 | tf_op jit(solution)/shard_map/ppermute | solution.py:31
  19.2 1.3 collective-permute-start.1
  20.5 1.5 %collective-permute-start.2 = (bf16[2,2,64,2176]{3,2,1,0:T(8,128)(2,1)S(1)}, bf16[2,2,64,2176]{3,2,1,0:T(8,128)(2,1)S(1)}, u32[]{:S(2)}, u32[]{:S(2)}) collective-permute-start(bf16[2,2,64,2176]{3,2,1,0:T(8,128)(2,1)S(1)} %pad_maximum_fusion.refs_13_.refs_3_), channel_id=1, source_target_pairs={{0,6},{1,7},{2,0},{3,1},{4,2},{5,3},{6,4},{7,5},{8,14},{9,15},{10,... | collective-permute-start | bytes 3342344 | tf_op jit(solution)/shard_map/ppermute | solution.py:31
  21.9 2.6 %collective-permute-start.5 = (bf16[2,2,64,2176]{3,2,1,0:T(8,128)(2,1)S(1)}, bf16[2,2,64,2176]{3,2,1,0:T(8,128)(2,1)}, u32[]{:S(2)}, u32[]{:S(2)}) collective-permute-start(bf16[2,2,64,2176]{3,2,1,0:T(8,128)(2,1)S(1)} %pad_maximum_fusion.refs_13_.refs_3_), channel_id=1, source_target_pairs={{0,1},{1,0},{2,3},{3,2},{4,5},{5,4},{6,7},{7,6},{8,9},{9,8},{10,11... | collective-permute-start | bytes 3342344 | tf_op jit(solution)/shard_map/ppermute | solution.py:31
  24.6 21.9 %collective-permute-done.1.refs_19_.refs_9_ = bf16[2,2,64,2176]{3,2,1,0:T(8,128)(2,1)S(1)} collective-permute-done((bf16[2,2,64,2176]{3,2,1,0:T(8,128)(2,1)S(1)}, bf16[2,2,64,2176]{3,2,1,0:T(8,128)(2,1)S(1)}, u32[]{:S(2)}, u32[]{:S(2)}) %collective-permute-start.1) | collective-permute-done | bytes 1114144 | tf_op jit(solution)/shard_map/ppermute | solution.py:31
  46.6 2.4 %collective-permute-start.9 = (bf16[2,2,64,2176]{3,2,1,0:T(8,128)(2,1)S(1)}, bf16[2,2,64,2176]{3,2,1,0:T(8,128)(2,1)S(1)}, u32[]{:S(2)}, u32[]{:S(2)}) collective-permute-start(bf16[2,2,64,2176]{3,2,1,0:T(8,128)(2,1)S(1)} %broadcast_select_fusion), channel_id=1, source_target_pairs={{0,2},{1,3},{2,4},{3,5},{4,6},{5,7},{6,0},{7,1},{8,14},{9,15},{10,... | collective-permute-start | bytes 3342344 | tf_op jit(solution)/shard_map/ppermute | solution.py:31
  49.0 1.5 %pick.1 = bf16[8,8,2176]{2,1,0:T(8,128)(2,1)S(1)} custom-call(s32[8]{0:T(128)S(1)} %copy-done.2, bf16[32,8,2176]{2,1,0:T(8,128)(2,1)} %all-to-all-done.got_ref), custom_call_target="tpu_custom_call" | custom-call | tf_op jit(solution)/shard_map/pick/pallas_call | solution.py:205
  50.5 2.7 %collective-permute-start.3 = (bf16[64,2176]{1,0:T(8,128)(2,1)S(1)}, bf16[64,2176]{1,0:T(8,128)(2,1)S(1)}, u32[]{:S(2)}, u32[]{:S(2)}) collective-permute-start(bf16[64,2176]{1,0:T(8,128)(2,1)S(1)} %bitcast.23), channel_id=1, source_target_pairs={{0,224},{1,225},{2,226},{3,227},{4,228},{5,229},{6,230},{7,231},{8... | collective-permute-start | bytes 835592 | tf_op jit(solution)/shard_map/ppermute | solution.py:31
  53.2 1.1 collective-permute-start.8
  54.3 3.4 %collective-permute-done.5.in_ref = bf16[2,2,64,2176]{3,2,1,0:T(8,128)(2,1)} collective-permute-done((bf16[2,2,64,2176]{3,2,1,0:T(8,128)(2,1)S(1)}, bf16[2,2,64,2176]{3,2,1,0:T(8,128)(2,1)}, u32[]{:S(2)}, u32[]{:S(2)}) %collective-permute-start.5) | collective-permute-done | bytes 1114144 | tf_op jit(solution)/shard_map/ppermute | solution.py:31
  57.7 1.3 collective-permute-done.3.refs_1_
  59.0 3.1 %collective-permute-done.4.refs_4_ = bf16[64,2176]{1,0:T(8,128)(2,1)S(1)} collective-permute-done((bf16[64,2176]{1,0:T(8,128)(2,1)S(1)}, bf16[64,2176]{1,0:T(8,128)(2,1)S(1)}, u32[]{:S(2)}, u32[]{:S(2)}) %collective-permute-start.4) | collective-permute-done | bytes 278560 | tf_op jit(solution)/shard_map/ppermute | solution.py:31
  62.5 1.1 collective-permute-start.7
  63.6 0.4 collective-permute-done.8.refs_8_
  64.0 5.0 %collective-permute-done.6.refs_2_ = bf16[64,2176]{1,0:T(8,128)(2,1)S(1)} collective-permute-done((bf16[64,2176]{1,0:T(8,128)(2,1)S(1)}, bf16[64,2176]{1,0:T(8,128)(2,1)S(1)}, u32[]{:S(2)}, u32[]{:S(2)}) %collective-permute-start.6) | collective-permute-done | bytes 278560 | tf_op jit(solution)/shard_map/ppermute | solution.py:31
  69.0 1.6 %collective-permute-done.7.refs_3_ = bf16[64,2176]{1,0:T(8,128)(2,1)S(1)} collective-permute-done((bf16[64,2176]{1,0:T(8,128)(2,1)S(1)}, bf16[64,2176]{1,0:T(8,128)(2,1)S(1)}, u32[]{:S(2)}, u32[]{:S(2)}) %collective-permute-start.7) | collective-permute-done | bytes 278560 | tf_op jit(solution)/shard_map/ppermute | solution.py:31
  71.0 1.2 collective-permute-start.11
  72.2 1.5 %collective-permute-start.16 = (bf16[2,2,64,2176]{3,2,1,0:T(8,128)(2,1)}, bf16[2,2,64,2176]{3,2,1,0:T(8,128)(2,1)S(1)}, u32[]{:S(2)}, u32[]{:S(2)}) collective-permute-start(bf16[2,2,64,2176]{3,2,1,0:T(8,128)(2,1)} %collective-permute-done.5.in_ref), channel_id=1, source_target_pairs={{0,2},{1,3},{2,4},{3,5},{4,6},{5,7},{6,0},{7,1},{8,10},{9,11},{10,... | collective-permute-start | bytes 3342344 | tf_op jit(solution)/shard_map/ppermute | solution.py:31
  73.6 2.3 %collective-permute-start.15 = (bf16[2,2,64,2176]{3,2,1,0:T(8,128)(2,1)S(1)}, bf16[2,2,64,2176]{3,2,1,0:T(8,128)(2,1)S(1)}, u32[]{:S(2)}, u32[]{:S(2)}) collective-permute-start(bf16[2,2,64,2176]{3,2,1,0:T(8,128)(2,1)S(1)} %collective-permute-done.9.refs_17_.refs_7_), channel_id=1, source_target_pairs={{0,1},{1,0},{2,3},{3,2},{4,5},{5,4},{6,7},{7,6},{8,9},{9,8},{10,11... | collective-permute-start | bytes 3342344 | tf_op jit(solution)/shard_map/ppermute | solution.py:31
  75.9 6.7 %collective-permute-done.10 = bf16[2,64,2176]{2,1,0:T(8,128)(2,1)S(1)} collective-permute-done((bf16[2,64,2176]{2,1,0:T(8,128)(2,1)S(1)}, bf16[2,64,2176]{2,1,0:T(8,128)(2,1)S(1)}, u32[]{:S(2)}, u32[]{:S(2)}) %collective-permute-start.10) | collective-permute-done | bytes 557088 | tf_op jit(solution)/shard_map/ppermute | solution.py:31
  82.6 1.5 %collective-permute-done.11 = bf16[2,64,2176]{2,1,0:T(8,128)(2,1)S(1)} collective-permute-done((bf16[2,64,2176]{2,1,0:T(8,128)(2,1)S(1)}, bf16[2,64,2176]{2,1,0:T(8,128)(2,1)S(1)}, u32[]{:S(2)}, u32[]{:S(2)}) %collective-permute-start.11) | collective-permute-done | bytes 557088 | tf_op jit(solution)/shard_map/ppermute | solution.py:31
  84.7 1.3 collective-permute-start.13
  85.9 1.3 settle.1.refs_14_.refs_4_
  87.2 5.2 %collective-permute-done.12 = bf16[96,2176]{1,0:T(8,128)(2,1)S(1)} collective-permute-done((bf16[96,2176]{1,0:T(8,128)(2,1)S(1)}, bf16[96,2176]{1,0:T(8,128)(2,1)S(1)}, u32[]{:S(2)}, u32[]{:S(2)}) %collective-permute-start.12) | collective-permute-done | bytes 417824 | tf_op jit(solution)/shard_map/ppermute | solution.py:31
  92.3 1.6 %collective-permute-done.13 = bf16[96,2176]{1,0:T(8,128)(2,1)S(1)} collective-permute-done((bf16[96,2176]{1,0:T(8,128)(2,1)S(1)}, bf16[96,2176]{1,0:T(8,128)(2,1)S(1)}, u32[]{:S(2)}, u32[]{:S(2)}) %collective-permute-start.13) | collective-permute-done | bytes 417824 | tf_op jit(solution)/shard_map/ppermute | solution.py:31
  94.1 0.7 collective-permute-start.17
  94.9 0.7 collective-permute-done.14.refs_16_.refs_6_
  95.7 0.6 collective-permute-start.20
  96.2 1.6 %collective-permute-done.15.refs_18_.refs_8_ = bf16[2,2,64,2176]{3,2,1,0:T(8,128)(2,1)S(1)} collective-permute-done((bf16[2,2,64,2176]{3,2,1,0:T(8,128)(2,1)S(1)}, bf16[2,2,64,2176]{3,2,1,0:T(8,128)(2,1)S(1)}, u32[]{:S(2)}, u32[]{:S(2)}) %collective-permute-start.15) | collective-permute-done | bytes 1114144 | tf_op jit(solution)/shard_map/ppermute | solution.py:31
  97.9 2.2 %scores.5 = f32[512,512]{1,0:T(8,128)S(1)} custom-call(bf16[64,2176]{1,0:T(8,128)(2,1)S(1)} %bitcast.26, bf16[64,2176]{1,0:T(8,128)(2,1)S(1)} %collective-permute-done.3.refs_1_, bf16[64,2176]{1,0:T(8,128)(2,1)S(1)} %collective-permute-done.6.refs_2_, bf16[64,2176]{1,0:T(8,128)(2,1)S(1)} %collective-permute-done.7.refs_3_, ...), custom_call_target="tpu_custom_call" | custom-call | flops 7415529472 | bytes 8388608 | tf_op jit(solution)/shard_map/scores/pallas_call | solution.py:253
  100.0 6.8 %collective-permute-start.18 = (f32[512,512]{1,0:T(8,128)S(1)}, f32[512,512]{1,0:T(8,128)S(1)}, u32[]{:S(2)}, u32[]{:S(2)}) collective-permute-start(f32[512,512]{1,0:T(8,128)S(1)} %scores.5), channel_id=1, source_target_pairs={{0,8},{1,9},{2,10},{3,11},{4,12},{5,13},{6,14},{7,15},{8,0},{9,1},... | collective-permute-start | bytes 3145736 | tf_op jit(solution)/shard_map/ppermute | solution.py:31
  106.8 2.2 %scores.4.near_ref = f32[512,512]{1,0:T(8,128)S(1)} custom-call(bf16[64,2176]{1,0:T(8,128)(2,1)S(1)} %bitcast.27, bf16[64,2176]{1,0:T(8,128)(2,1)S(1)} %collective-permute-done.3.refs_1_, bf16[64,2176]{1,0:T(8,128)(2,1)S(1)} %collective-permute-done.6.refs_2_, bf16[64,2176]{1,0:T(8,128)(2,1)S(1)} %collective-permute-done.7.refs_3_, ...), custom_call_target="tpu_custom_call" | custom-call | flops 7415529472 | bytes 8388608 | tf_op jit(solution)/shard_map/scores/pallas_call | solution.py:253
  109.0 0.9 scores.7
  110.0 0.9 scores.6.far_ref
  110.9 0.8 collective-permute-done.21.far_other_ref
  111.8 1.3 norms.1
  113.1 5.0 %all-to-all-start.1 = ((f32[8,8,512]{2,1,0:T(8,128)}), f32[8,8,512]{2,1,0:T(8,128)S(1)}, u32[]{:S(2)}, u32[]{:S(2)}) async-start(f32[8,8,512]{2,1,0:T(8,128)} %get-tuple-element.46), calls=%async_computation.1 | async-start | bytes 262144 | tf_op jit(solution)/shard_map/all_to_all | solution.py:402
  118.1 6.8 %all-to-all-done.1.parts_ref = f32[8,8,512]{2,1,0:T(8,128)S(1)} async-done(((f32[8,8,512]{2,1,0:T(8,128)}), f32[8,8,512]{2,1,0:T(8,128)S(1)}, u32[]{:S(2)}, u32[]{:S(2)}) %all-to-all-start.1) | async-done | bytes 131104 | tf_op jit(solution)/shard_map/all_to_all | solution.py:402
  124.9 1.5 %finish.1 = (f32[1,512]{1,0:T(1,128)S(1)}, f32[8,512]{1,0:T(8,128)S(1)}, f32[32,1,512]{2,1,0:T(1,128)}) custom-call(f32[8,8,512]{2,1,0:T(8,128)S(1)} %all-to-all-done.1.parts_ref, f32[8,64,512]{2,1,0:T(8,128)S(1)} %get-tuple-element.47.scores_ref), custom_call_target="tpu_custom_call" | custom-call | tf_op jit(solution)/shard_map/finish/pallas_call | solution.py:335
  126.4 6.9 %all-to-all-start.2 = ((f32[32,1,512]{2,1,0:T(1,128)}), f32[32,1,512]{2,1,0:T(1,128)S(1)}, u32[]{:S(2)}, u32[]{:S(2)}) async-start(f32[32,1,512]{2,1,0:T(1,128)} %get-tuple-element.50), calls=%async_computation.2 | async-start | bytes 131072 | tf_op jit(solution)/shard_map/all_to_all | solution.py:404
  133.2 0.6 dynamic-slice_bitcast_fusion
  133.8 0.7 constant_dynamic-slice_fusion
  134.5 7.1 %all-to-all-done.2 = f32[32,1,512]{2,1,0:T(1,128)S(1)} async-done(((f32[32,1,512]{2,1,0:T(1,128)}), f32[32,1,512]{2,1,0:T(1,128)S(1)}, u32[]{:S(2)}, u32[]{:S(2)}) %all-to-all-start.2) | async-done | bytes 65568 | tf_op jit(solution)/shard_map/all_to_all | solution.py:404
  141.6 0.7 reshape.28
  (43 shorter events, 2.2 us)
Async XLA Ops:
  4.3 11.4 %copy-start.3 = (f32[4224]{0:T(1024)S(1)}, f32[4224]{0:T(1024)}, u32[]{:S(2)}) copy-start(f32[4224]{0:T(1024)} %noise_hbm.1) | copy-start | bytes 50692
  4.3 11.4 %copy-start.4 = (s32[64]{0:T(128)S(1)}, s32[64]{0:T(128)}, u32[]{:S(2)}) copy-start(s32[64]{0:T(128)} %param.8) | copy-start | bytes 772
  4.3 11.5 %copy-start = (f32[64,4224]{1,0:T(8,128)S(1)}, f32[64,4224]{1,0:T(8,128)}, u32[]{:S(2)}) copy-start(f32[64,4224]{1,0:T(8,128)} %contrast_ref.1) | copy-start | bytes 3244036
  4.3 11.5 %copy-start.1 = (bf16[64,8448]{1,0:T(8,128)(2,1)S(1)}, bf16[64,8448]{1,0:T(8,128)(2,1)}, u32[]{:S(2)}) copy-start(bf16[64,8448]{1,0:T(8,128)(2,1)} %images_ref) | copy-start | bytes 3244036
  4.3 42.1 %all-to-all-start = ((bf16[32,8,2176]{2,1,0:T(8,128)(2,1)}), bf16[32,8,2176]{2,1,0:T(8,128)(2,1)}, u32[]{:S(2)}, u32[]{:S(2)}) async-start(bf16[32,8,2176]{2,1,0:T(8,128)(2,1)} %bitcast.31), calls=%async_computation | async-start | bytes 2228224 | tf_op jit(solution)/shard_map/all_to_all | solution.py:359
  17.0 2.0 %collective-permute-start = (bf16[2,64,2176]{2,1,0:T(8,128)(2,1)S(1)}, bf16[2,64,2176]{2,1,0:T(8,128)(2,1)S(1)}, u32[]{:S(2)}, u32[]{:S(2)}) collective-permute-start(bf16[2,64,2176]{2,1,0:T(8,128)(2,1)S(1)} %get-tuple-element.52), channel_id=1, source_target_pairs={{0,8},{1,9},{2,10},{3,11},{4,12},{5,13},{6,14},{7,15},{8,0},{9,1},... | collective-permute-start | bytes 1671176 | tf_op jit(solution)/shard_map/ppermute | solution.py:31
  19.2 27.2 %collective-permute-start.1 = (bf16[2,2,64,2176]{3,2,1,0:T(8,128)(2,1)S(1)}, bf16[2,2,64,2176]{3,2,1,0:T(8,128)(2,1)S(1)}, u32[]{:S(2)}, u32[]{:S(2)}) collective-permute-start(bf16[2,2,64,2176]{3,2,1,0:T(8,128)(2,1)S(1)} %pad_maximum_fusion.refs_13_.refs_3_), channel_id=1, source_target_pairs={{0,2},{1,3},{2,4},{3,5},{4,6},{5,7},{6,0},{7,1},{8,10},{9,11},{10,... | collective-permute-start | bytes 3342344 | tf_op jit(solution)/shard_map/ppermute | solution.py:31
  20.5 26.0 %collective-permute-start.2 = (bf16[2,2,64,2176]{3,2,1,0:T(8,128)(2,1)S(1)}, bf16[2,2,64,2176]{3,2,1,0:T(8,128)(2,1)S(1)}, u32[]{:S(2)}, u32[]{:S(2)}) collective-permute-start(bf16[2,2,64,2176]{3,2,1,0:T(8,128)(2,1)S(1)} %pad_maximum_fusion.refs_13_.refs_3_), channel_id=1, source_target_pairs={{0,6},{1,7},{2,0},{3,1},{4,2},{5,3},{6,4},{7,5},{8,14},{9,15},{10,... | collective-permute-start | bytes 3342344 | tf_op jit(solution)/shard_map/ppermute | solution.py:31
  21.9 27.1 %copy-start.2 = (s32[8]{0:T(128)S(1)}, s32[8]{0:T(128)}, u32[]{:S(2)}) copy-start(s32[8]{0:T(128)} %owners_ref.1) | copy-start | bytes 100
  21.9 35.8 %collective-permute-start.5 = (bf16[2,2,64,2176]{3,2,1,0:T(8,128)(2,1)S(1)}, bf16[2,2,64,2176]{3,2,1,0:T(8,128)(2,1)}, u32[]{:S(2)}, u32[]{:S(2)}) collective-permute-start(bf16[2,2,64,2176]{3,2,1,0:T(8,128)(2,1)S(1)} %pad_maximum_fusion.refs_13_.refs_3_), channel_id=1, source_target_pairs={{0,1},{1,0},{2,3},{3,2},{4,5},{5,4},{6,7},{7,6},{8,9},{9,8},{10,11... | collective-permute-start | bytes 3342344 | tf_op jit(solution)/shard_map/ppermute | solution.py:31
  46.6 24.0 %collective-permute-start.9 = (bf16[2,2,64,2176]{3,2,1,0:T(8,128)(2,1)S(1)}, bf16[2,2,64,2176]{3,2,1,0:T(8,128)(2,1)S(1)}, u32[]{:S(2)}, u32[]{:S(2)}) collective-permute-start(bf16[2,2,64,2176]{3,2,1,0:T(8,128)(2,1)S(1)} %broadcast_select_fusion), channel_id=1, source_target_pairs={{0,2},{1,3},{2,4},{3,5},{4,6},{5,7},{6,0},{7,1},{8,14},{9,15},{10,... | collective-permute-start | bytes 3342344 | tf_op jit(solution)/shard_map/ppermute | solution.py:31
  50.5 8.5 %collective-permute-start.3 = (bf16[64,2176]{1,0:T(8,128)(2,1)S(1)}, bf16[64,2176]{1,0:T(8,128)(2,1)S(1)}, u32[]{:S(2)}, u32[]{:S(2)}) collective-permute-start(bf16[64,2176]{1,0:T(8,128)(2,1)S(1)} %bitcast.23), channel_id=1, source_target_pairs={{0,224},{1,225},{2,226},{3,227},{4,228},{5,229},{6,230},{7,231},{8... | collective-permute-start | bytes 835592 | tf_op jit(solution)/shard_map/ppermute | solution.py:31
  53.2 8.9 %collective-permute-start.4 = (bf16[64,2176]{1,0:T(8,128)(2,1)S(1)}, bf16[64,2176]{1,0:T(8,128)(2,1)S(1)}, u32[]{:S(2)}, u32[]{:S(2)}) collective-permute-start(bf16[64,2176]{1,0:T(8,128)(2,1)S(1)} %bitcast.24), channel_id=1, source_target_pairs={{0,32},{1,33},{2,34},{3,35},{4,36},{5,37},{6,38},{7,39},{8,40},{9,... | collective-permute-start | bytes 835592 | tf_op jit(solution)/shard_map/ppermute | solution.py:31
  53.2 10.8 %collective-permute-start.8 = (bf16[64,2176]{1,0:T(8,128)(2,1)S(1)}, bf16[64,2176]{1,0:T(8,128)(2,1)S(1)}, u32[]{:S(2)}, u32[]{:S(2)}) collective-permute-start(bf16[64,2176]{1,0:T(8,128)(2,1)S(1)} %bitcast.25), channel_id=1, source_target_pairs={{0,16},{1,17},{2,18},{3,19},{4,20},{5,21},{6,22},{7,23},{8,24},{9,... | collective-permute-start | bytes 835592 | tf_op jit(solution)/shard_map/ppermute | solution.py:31
  62.1 6.8 %collective-permute-start.6 = (bf16[64,2176]{1,0:T(8,128)(2,1)S(1)}, bf16[64,2176]{1,0:T(8,128)(2,1)S(1)}, u32[]{:S(2)}, u32[]{:S(2)}) collective-permute-start(bf16[64,2176]{1,0:T(8,128)(2,1)S(1)} %collective-permute-done.3.refs_1_), channel_id=1, source_target_pairs={{0,224},{1,225},{2,226},{3,227},{4,228},{5,229},{6,230},{7,231},{8... | collective-permute-start | bytes 835592 | tf_op jit(solution)/shard_map/ppermute | solution.py:31
  62.5 8.1 %collective-permute-start.7 = (bf16[64,2176]{1,0:T(8,128)(2,1)S(1)}, bf16[64,2176]{1,0:T(8,128)(2,1)S(1)}, u32[]{:S(2)}, u32[]{:S(2)}) collective-permute-start(bf16[64,2176]{1,0:T(8,128)(2,1)S(1)} %collective-permute-done.4.refs_4_), channel_id=1, source_target_pairs={{0,32},{1,33},{2,34},{3,35},{4,36},{5,37},{6,38},{7,39},{8,40},{9,... | collective-permute-start | bytes 835592 | tf_op jit(solution)/shard_map/ppermute | solution.py:31
  70.6 12.0 %collective-permute-start.10 = (bf16[2,64,2176]{2,1,0:T(8,128)(2,1)S(1)}, bf16[2,64,2176]{2,1,0:T(8,128)(2,1)S(1)}, u32[]{:S(2)}, u32[]{:S(2)}) collective-permute-start(bf16[2,64,2176]{2,1,0:T(8,128)(2,1)S(1)} %get-tuple-element.58), channel_id=1, source_target_pairs={{0,224},{1,225},{2,226},{3,227},{4,228},{5,229},{6,230},{7,231},{8... | collective-permute-start | bytes 1671176 | tf_op jit(solution)/shard_map/ppermute | solution.py:31
  71.0 13.1 %collective-permute-start.11 = (bf16[2,64,2176]{2,1,0:T(8,128)(2,1)S(1)}, bf16[2,64,2176]{2,1,0:T(8,128)(2,1)S(1)}, u32[]{:S(2)}, u32[]{:S(2)}) collective-permute-start(bf16[2,64,2176]{2,1,0:T(8,128)(2,1)S(1)} %get-tuple-element.57), channel_id=1, source_target_pairs={{0,32},{1,33},{2,34},{3,35},{4,36},{5,37},{6,38},{7,39},{8,40},{9,... | collective-permute-start | bytes 1671176 | tf_op jit(solution)/shard_map/ppermute | solution.py:31
  72.2 23.5 %collective-permute-start.14 = (bf16[2,2,64,2176]{3,2,1,0:T(8,128)(2,1)}, bf16[2,2,64,2176]{3,2,1,0:T(8,128)(2,1)S(1)}, u32[]{:S(2)}, u32[]{:S(2)}) collective-permute-start(bf16[2,2,64,2176]{3,2,1,0:T(8,128)(2,1)} %collective-permute-done.5.in_ref), channel_id=1, source_target_pairs={{0,6},{1,7},{2,0},{3,1},{4,2},{5,3},{6,4},{7,5},{8,14},{9,15},{10,... | collective-permute-start | bytes 3342344 | tf_op jit(solution)/shard_map/ppermute | solution.py:31
  72.2 25.7 %collective-permute-start.16 = (bf16[2,2,64,2176]{3,2,1,0:T(8,128)(2,1)}, bf16[2,2,64,2176]{3,2,1,0:T(8,128)(2,1)S(1)}, u32[]{:S(2)}, u32[]{:S(2)}) collective-permute-start(bf16[2,2,64,2176]{3,2,1,0:T(8,128)(2,1)} %collective-permute-done.5.in_ref), channel_id=1, source_target_pairs={{0,2},{1,3},{2,4},{3,5},{4,6},{5,7},{6,0},{7,1},{8,10},{9,11},{10,... | collective-permute-start | bytes 3342344 | tf_op jit(solution)/shard_map/ppermute | solution.py:31
  73.6 24.2 %collective-permute-start.15 = (bf16[2,2,64,2176]{3,2,1,0:T(8,128)(2,1)S(1)}, bf16[2,2,64,2176]{3,2,1,0:T(8,128)(2,1)S(1)}, u32[]{:S(2)}, u32[]{:S(2)}) collective-permute-start(bf16[2,2,64,2176]{3,2,1,0:T(8,128)(2,1)S(1)} %collective-permute-done.9.refs_17_.refs_7_), channel_id=1, source_target_pairs={{0,1},{1,0},{2,3},{3,2},{4,5},{5,4},{6,7},{7,6},{8,9},{9,8},{10,11... | collective-permute-start | bytes 3342344 | tf_op jit(solution)/shard_map/ppermute | solution.py:31
  84.3 8.1 %collective-permute-start.12 = (bf16[96,2176]{1,0:T(8,128)(2,1)S(1)}, bf16[96,2176]{1,0:T(8,128)(2,1)S(1)}, u32[]{:S(2)}, u32[]{:S(2)}) collective-permute-start(bf16[96,2176]{1,0:T(8,128)(2,1)S(1)} %pad_maximum_fusion.3), channel_id=1, source_target_pairs={{0,224},{1,225},{2,226},{3,227},{4,228},{5,229},{6,230},{7,231},{8... | collective-permute-start | bytes 1253384 | tf_op jit(solution)/shard_map/ppermute | solution.py:31
  84.7 9.3 %collective-permute-start.13 = (bf16[96,2176]{1,0:T(8,128)(2,1)S(1)}, bf16[96,2176]{1,0:T(8,128)(2,1)S(1)}, u32[]{:S(2)}, u32[]{:S(2)}) collective-permute-start(bf16[96,2176]{1,0:T(8,128)(2,1)S(1)} %pad_maximum_fusion.4), channel_id=1, source_target_pairs={{0,32},{1,33},{2,34},{3,35},{4,36},{5,37},{6,38},{7,39},{8,40},{9,... | collective-permute-start | bytes 1253384 | tf_op jit(solution)/shard_map/ppermute | solution.py:31
  94.1 15.0 %collective-permute-start.17 = (bf16[64,2176]{1,0:T(8,128)(2,1)S(1)}, bf16[64,2176]{1,0:T(8,128)(2,1)S(1)}, u32[]{:S(2)}, u32[]{:S(2)}) collective-permute-start(bf16[64,2176]{1,0:T(8,128)(2,1)S(1)} %pad_maximum_fusion.5.refs_7_), channel_id=1, source_target_pairs={{0,16},{1,17},{2,18},{3,19},{4,20},{5,21},{6,22},{7,23},{8,24},{9,... | collective-permute-start | bytes 835592 | tf_op jit(solution)/shard_map/ppermute | solution.py:31
  94.8 14.3 %collective-permute-start.19 = (bf16[64,2176]{1,0:T(8,128)(2,1)S(1)}, bf16[64,2176]{1,0:T(8,128)(2,1)S(1)}, u32[]{:S(2)}, u32[]{:S(2)}) collective-permute-start(bf16[64,2176]{1,0:T(8,128)(2,1)S(1)} %slice.40.refs_10_), channel_id=1, source_target_pairs={{0,224},{1,225},{2,226},{3,227},{4,228},{5,229},{6,230},{7,231},{8... | collective-permute-start | bytes 835592 | tf_op jit(solution)/shard_map/ppermute | solution.py:31
  95.7 13.4 %collective-permute-start.20 = (bf16[64,2176]{1,0:T(8,128)(2,1)S(1)}, bf16[64,2176]{1,0:T(8,128)(2,1)S(1)}, u32[]{:S(2)}, u32[]{:S(2)}) collective-permute-start(bf16[64,2176]{1,0:T(8,128)(2,1)S(1)} %slice.41.refs_11_), channel_id=1, source_target_pairs={{0,32},{1,33},{2,34},{3,35},{4,36},{5,37},{6,38},{7,39},{8,40},{9,... | collective-permute-start | bytes 835592 | tf_op jit(solution)/shard_map/ppermute | solution.py:31
  100.0 11.7 %collective-permute-start.18 = (f32[512,512]{1,0:T(8,128)S(1)}, f32[512,512]{1,0:T(8,128)S(1)}, u32[]{:S(2)}, u32[]{:S(2)}) collective-permute-start(f32[512,512]{1,0:T(8,128)S(1)} %scores.5), channel_id=1, source_target_pairs={{0,8},{1,9},{2,10},{3,11},{4,12},{5,13},{6,14},{7,15},{8,0},{9,1},... | collective-permute-start | bytes 3145736 | tf_op jit(solution)/shard_map/ppermute | solution.py:31
  109.9 1.8 %collective-permute-start.21 = (f32[192,512]{1,0:T(8,128)S(1)}, f32[192,512]{1,0:T(8,128)S(1)}, u32[]{:S(2)}, u32[]{:S(2)}) collective-permute-start(f32[192,512]{1,0:T(8,128)S(1)} %scores.7), channel_id=1, source_target_pairs={{0,8},{1,9},{2,10},{3,11},{4,12},{5,13},{6,14},{7,15},{8,0},{9,1},... | collective-permute-start | bytes 1179656 | tf_op jit(solution)/shard_map/ppermute | solution.py:31
  113.1 11.8 %all-to-all-start.1 = ((f32[8,8,512]{2,1,0:T(8,128)}), f32[8,8,512]{2,1,0:T(8,128)S(1)}, u32[]{:S(2)}, u32[]{:S(2)}) async-start(f32[8,8,512]{2,1,0:T(8,128)} %get-tuple-element.46), calls=%async_computation.1 | async-start | bytes 262144 | tf_op jit(solution)/shard_map/all_to_all | solution.py:402
  126.4 15.2 %all-to-all-start.2 = ((f32[32,1,512]{2,1,0:T(1,128)}), f32[32,1,512]{2,1,0:T(1,128)S(1)}, u32[]{:S(2)}, u32[]{:S(2)}) async-start(f32[32,1,512]{2,1,0:T(1,128)} %get-tuple-element.50), calls=%async_computation.2 | async-start | bytes 131072 | tf_op jit(solution)/shard_map/all_to_all | solution.py:404

commit v7 on v6

--- a/solution.py
+++ b/solution.py
@@ -390,9 +390,8 @@
     near = [mine0, mine1, mine2, mine6, mine7, mine3, mine5, mine4]
     near += [theirs0, theirs1, theirs2, theirs6, theirs7]
     near_plan = ((0, 8, 0), (1, 5, 0))
-    (near_theirs,) = scores_of(near, whole, (1,), near_plan)
+    near_theirs, near_mine = scores_of(near, whole, (1, 0), near_plan)
     near_other = other_core(near_theirs)
-    (near_mine,) = scores_of(near, whole, (0,), near_plan)
     near_mine, theirs4 = together(near_mine, theirs4)
     far_panels, far_plan = [theirs3, theirs5, theirs4], ((1, 3, 0),)
     (far_theirs,) = scores_of(far_panels, whole, (1,), far_plan)

time: 143 us -> 152 us (1.063)
  waiting for transfers between devices: 70.3 us -> 79.2 us
    ppermute x22, waiting for transfers between devices: 56.4 us -> 65.2 us  [permute(): return lax.ppermute(array, ('dp', 'orient'), pairs)]
    pallas_call x4 -> x3, Pallas kernels: 6.1 us -> 5.9 us  [scores_of(): pl.pallas_call(functools.partial(scores_kernel, owners, plan), out_shape=...]
  transfers between devices with their start and end apart: 25 -> 25, of which waited for: 17 -> 19; matrix products, arithmetic and copies ran while one was open for 1% -> 1% of each run, Pallas kernels for 7% -> 4%
where the time goes in v7:
time: 152 us
  waiting for transfers between devices  79.2 us (52%)
  starting transfers between devices  52.5 us (35%)
  Pallas kernels  16.2 us (11%)
  local copies, waits for them, and re-layouts  2.31 us (2%)
    ppermute x22, waiting for transfers between devices, permute(): return lax.ppermute(array, ('dp', 'orient'), pairs)  65.2 us
    ppermute x22, starting transfers between devices, permute(): return lax.ppermute(array, ('dp', 'orient'), pairs)  29.8 us
    all_to_all x1, starting transfers between devices, per_device(): got = lax.all_to_all(sent, 'dp', 0, 0)  11.3 us
    all_to_all x1, waiting for transfers between devices, per_device(): masses = lax.all_to_all(mass, 'dp', 0, 0)  7.08 us
    all_to_all x1, waiting for transfers between devices, per_device(): parts = lax.all_to_all(partial, 'orient', 0, 0)  6.94 us
    all_to_all x1, starting transfers between devices, per_device(): masses = lax.all_to_all(mass, 'dp', 0, 0)  6.29 us
    pallas_call x3, Pallas kernels, scores_of(): pl.pallas_call(functools.partial(scores_kernel, owners, plan), out_shape=...  5.9 us
    all_to_all x1, starting transfers between devices, per_device(): parts = lax.all_to_all(partial, 'orient', 0, 0)  5.08 us
  transfers between devices with their start and end apart: 25, of which 19 were waited for; matrix products, arithmetic and copies ran while one was open for 1% of the time, Pallas kernels for 4%

profile of v7, /device:TPU:1, one launch (start us, length us, event | category | flops | bytes accessed | tf_op | source)
XLA Modules:
  0.0 151.6 jit_solution(15947615155222732480)
XLA Ops:
  0.6 3.6 %panel.1 = bf16[8,32,2176]{2,1,0:T(8,128)(2,1)} custom-call(s32[8]{0:T(128)} %owners_ref.1, f32[8]{0:T(128)} %priors_hbm.1, bf16[1,64,8448]{2,1,0:T(8,128)(2,1)} %slot_hbm.1, f32[64,4224]{1,0:T(8,128)} %contrast_ref.1, f32[4224]{0:T(1024)} %noise_hbm.1), custom_call_target="tpu_custom_call" | custom-call | tf_op jit(solution)/shard_map/panel/pallas_call | solution.py:174
  4.3 11.3 %all-to-all-start = ((bf16[32,8,2176]{2,1,0:T(8,128)(2,1)}), bf16[32,8,2176]{2,1,0:T(8,128)(2,1)}, u32[]{:S(2)}, u32[]{:S(2)}) async-start(bf16[32,8,2176]{2,1,0:T(8,128)(2,1)} %bitcast.30), calls=%async_computation | async-start | bytes 2228224 | tf_op jit(solution)/shard_map/all_to_all | solution.py:359
  15.8 1.1 weigh.1
  17.4 1.7 %collective-permute-done = bf16[2,64,2176]{2,1,0:T(8,128)(2,1)S(1)} collective-permute-done((bf16[2,64,2176]{2,1,0:T(8,128)(2,1)S(1)}, bf16[2,64,2176]{2,1,0:T(8,128)(2,1)S(1)}, u32[]{:S(2)}, u32[]{:S(2)}) %collective-permute-start) | collective-permute-done | bytes 557088 | tf_op jit(solution)/shard_map/ppermute | solution.py:31
  19.2 1.3 collective-permute-start.1
  20.5 1.5 collective-permute-start.2
  22.0 2.6 %collective-permute-start.5 = (bf16[2,2,64,2176]{3,2,1,0:T(8,128)(2,1)S(1)}, bf16[2,2,64,2176]{3,2,1,0:T(8,128)(2,1)}, u32[]{:S(2)}, u32[]{:S(2)}) collective-permute-start(bf16[2,2,64,2176]{3,2,1,0:T(8,128)(2,1)S(1)} %pad_maximum_fusion.refs_13_.refs_3_), channel_id=1, source_target_pairs={{0,1},{1,0},{2,3},{3,2},{4,5},{5,4},{6,7},{7,6},{8,9},{9,8},{10,11... | collective-permute-start | bytes 3342344 | tf_op jit(solution)/shard_map/ppermute | solution.py:31
  24.6 21.9 %collective-permute-done.1.refs_19_.refs_9_ = bf16[2,2,64,2176]{3,2,1,0:T(8,128)(2,1)S(1)} collective-permute-done((bf16[2,2,64,2176]{3,2,1,0:T(8,128)(2,1)S(1)}, bf16[2,2,64,2176]{3,2,1,0:T(8,128)(2,1)S(1)}, u32[]{:S(2)}, u32[]{:S(2)}) %collective-permute-start.1) | collective-permute-done | bytes 1114144 | tf_op jit(solution)/shard_map/ppermute | solution.py:31
  46.6 2.4 %collective-permute-start.9 = (bf16[2,2,64,2176]{3,2,1,0:T(8,128)(2,1)S(1)}, bf16[2,2,64,2176]{3,2,1,0:T(8,128)(2,1)S(1)}, u32[]{:S(2)}, u32[]{:S(2)}) collective-permute-start(bf16[2,2,64,2176]{3,2,1,0:T(8,128)(2,1)S(1)} %broadcast_select_fusion), channel_id=1, source_target_pairs={{0,2},{1,3},{2,4},{3,5},{4,6},{5,7},{6,0},{7,1},{8,14},{9,15},{10,... | collective-permute-start | bytes 3342344 | tf_op jit(solution)/shard_map/ppermute | solution.py:31
  49.0 1.5 pick.1
  50.5 2.7 %collective-permute-start.3 = (bf16[64,2176]{1,0:T(8,128)(2,1)S(1)}, bf16[64,2176]{1,0:T(8,128)(2,1)S(1)}, u32[]{:S(2)}, u32[]{:S(2)}) collective-permute-start(bf16[64,2176]{1,0:T(8,128)(2,1)S(1)} %bitcast.23), channel_id=1, source_target_pairs={{0,224},{1,225},{2,226},{3,227},{4,228},{5,229},{6,230},{7,231},{8... | collective-permute-start | bytes 835592 | tf_op jit(solution)/shard_map/ppermute | solution.py:31
  53.2 1.1 collective-permute-start.8
  54.3 3.4 %collective-permute-done.5.in_ref = bf16[2,2,64,2176]{3,2,1,0:T(8,128)(2,1)} collective-permute-done((bf16[2,2,64,2176]{3,2,1,0:T(8,128)(2,1)S(1)}, bf16[2,2,64,2176]{3,2,1,0:T(8,128)(2,1)}, u32[]{:S(2)}, u32[]{:S(2)}) %collective-permute-start.5) | collective-permute-done | bytes 1114144 | tf_op jit(solution)/shard_map/ppermute | solution.py:31
  57.7 1.3 collective-permute-done.3.refs_1_
  59.1 3.1 %collective-permute-done.4.refs_4_ = bf16[64,2176]{1,0:T(8,128)(2,1)S(1)} collective-permute-done((bf16[64,2176]{1,0:T(8,128)(2,1)S(1)}, bf16[64,2176]{1,0:T(8,128)(2,1)S(1)}, u32[]{:S(2)}, u32[]{:S(2)}) %collective-permute-start.4) | collective-permute-done | bytes 278560 | tf_op jit(solution)/shard_map/ppermute | solution.py:31
  62.5 1.1 collective-permute-start.7
  64.0 5.0 %collective-permute-done.6.refs_2_ = bf16[64,2176]{1,0:T(8,128)(2,1)S(1)} collective-permute-done((bf16[64,2176]{1,0:T(8,128)(2,1)S(1)}, bf16[64,2176]{1,0:T(8,128)(2,1)S(1)}, u32[]{:S(2)}, u32[]{:S(2)}) %collective-permute-start.6) | collective-permute-done | bytes 278560 | tf_op jit(solution)/shard_map/ppermute | solution.py:31
  69.0 1.6 %collective-permute-done.7.refs_3_ = bf16[64,2176]{1,0:T(8,128)(2,1)S(1)} collective-permute-done((bf16[64,2176]{1,0:T(8,128)(2,1)S(1)}, bf16[64,2176]{1,0:T(8,128)(2,1)S(1)}, u32[]{:S(2)}, u32[]{:S(2)}) %collective-permute-start.7) | collective-permute-done | bytes 278560 | tf_op jit(solution)/shard_map/ppermute | solution.py:31
  71.0 1.2 collective-permute-start.11
  72.2 1.5 collective-permute-start.16
  73.7 2.2 %collective-permute-start.15 = (bf16[2,2,64,2176]{3,2,1,0:T(8,128)(2,1)S(1)}, bf16[2,2,64,2176]{3,2,1,0:T(8,128)(2,1)S(1)}, u32[]{:S(2)}, u32[]{:S(2)}) collective-permute-start(bf16[2,2,64,2176]{3,2,1,0:T(8,128)(2,1)S(1)} %collective-permute-done.9.refs_17_.refs_7_), channel_id=1, source_target_pairs={{0,1},{1,0},{2,3},{3,2},{4,5},{5,4},{6,7},{7,6},{8,9},{9,8},{10,11... | collective-permute-start | bytes 3342344 | tf_op jit(solution)/shard_map/ppermute | solution.py:31
  75.9 6.8 %collective-permute-done.10 = bf16[2,64,2176]{2,1,0:T(8,128)(2,1)S(1)} collective-permute-done((bf16[2,64,2176]{2,1,0:T(8,128)(2,1)S(1)}, bf16[2,64,2176]{2,1,0:T(8,128)(2,1)S(1)}, u32[]{:S(2)}, u32[]{:S(2)}) %collective-permute-start.10) | collective-permute-done | bytes 557088 | tf_op jit(solution)/shard_map/ppermute | solution.py:31
  82.7 1.5 collective-permute-done.11
  84.5 2.7 %collective-permute-start.12 = (bf16[96,2176]{1,0:T(8,128)(2,1)S(1)}, bf16[96,2176]{1,0:T(8,128)(2,1)S(1)}, u32[]{:S(2)}, u32[]{:S(2)}) collective-permute-start(bf16[96,2176]{1,0:T(8,128)(2,1)S(1)} %pad_maximum_fusion.3), channel_id=1, source_target_pairs={{0,224},{1,225},{2,226},{3,227},{4,228},{5,229},{6,230},{7,231},{8... | collective-permute-start | bytes 1253384 | tf_op jit(solution)/shard_map/ppermute | solution.py:31
  87.2 1.3 settle.1.refs_14_.refs_4_
  88.4 5.2 %collective-permute-done.13 = bf16[96,2176]{1,0:T(8,128)(2,1)S(1)} collective-permute-done((bf16[96,2176]{1,0:T(8,128)(2,1)S(1)}, bf16[96,2176]{1,0:T(8,128)(2,1)S(1)}, u32[]{:S(2)}, u32[]{:S(2)}) %collective-permute-start.13) | collective-permute-done | bytes 417824 | tf_op jit(solution)/shard_map/ppermute | solution.py:31
  93.7 2.0 %collective-permute-done.14.refs_16_.refs_6_ = bf16[2,2,64,2176]{3,2,1,0:T(8,128)(2,1)S(1)} collective-permute-done((bf16[2,2,64,2176]{3,2,1,0:T(8,128)(2,1)}, bf16[2,2,64,2176]{3,2,1,0:T(8,128)(2,1)S(1)}, u32[]{:S(2)}, u32[]{:S(2)}) %collective-permute-start.14) | collective-permute-done | bytes 1114144 | tf_op jit(solution)/shard_map/ppermute | solution.py:31
  95.7 2.2 %collective-permute-done.15.refs_18_.refs_8_ = bf16[2,2,64,2176]{3,2,1,0:T(8,128)(2,1)S(1)} collective-permute-done((bf16[2,2,64,2176]{3,2,1,0:T(8,128)(2,1)S(1)}, bf16[2,2,64,2176]{3,2,1,0:T(8,128)(2,1)S(1)}, u32[]{:S(2)}, u32[]{:S(2)}) %collective-permute-start.15) | collective-permute-done | bytes 1114144 | tf_op jit(solution)/shard_map/ppermute | solution.py:31
  97.9 4.1 %scores.3 = (f32[512,512]{1,0:T(8,128)S(1)}, f32[512,512]{1,0:T(8,128)S(1)}) custom-call(bf16[64,2176]{1,0:T(8,128)(2,1)S(1)} %bitcast.26, bf16[64,2176]{1,0:T(8,128)(2,1)S(1)} %collective-permute-done.3.refs_1_, bf16[64,2176]{1,0:T(8,128)(2,1)S(1)} %collective-permute-done.6.refs_2_, bf16[64,2176]{1,0:T(8,128)(2,1)S(1)} %collective-permute-done.7.refs_3_, ...), custom_call_target="tpu_custom_call" | custom-call | flops 14831058944 | bytes 8388608 | tf_op jit(solution)/shard_map/scores/pallas_call | solution.py:253
  102.1 4.3 %collective-permute-start.18 = (f32[512,512]{1,0:T(8,128)S(1)}, f32[512,512]{1,0:T(8,128)S(1)}, u32[]{:S(2)}, u32[]{:S(2)}) collective-permute-start(f32[512,512]{1,0:T(8,128)S(1)} %get-tuple-element.48), channel_id=1, source_target_pairs={{0,8},{1,9},{2,10},{3,11},{4,12},{5,13},{6,14},{7,15},{8,0},{9,1},... | collective-permute-start | bytes 3145736 | tf_op jit(solution)/shard_map/ppermute | solution.py:31
  106.4 0.9 collective-permute-start.17
  107.3 1.5 collective-permute-start.19
  108.8 5.9 %collective-permute-done.17.refs_2_ = bf16[64,2176]{1,0:T(8,128)(2,1)S(1)} collective-permute-done((bf16[64,2176]{1,0:T(8,128)(2,1)S(1)}, bf16[64,2176]{1,0:T(8,128)(2,1)S(1)}, u32[]{:S(2)}, u32[]{:S(2)}) %collective-permute-start.17) | collective-permute-done | bytes 278560 | tf_op jit(solution)/shard_map/ppermute | solution.py:31
  114.6 0.5 collective-permute-done.19.refs_0_
  115.2 2.4 %collective-permute-done.20.refs_1_ = bf16[64,2176]{1,0:T(8,128)(2,1)S(1)} collective-permute-done((bf16[64,2176]{1,0:T(8,128)(2,1)S(1)}, bf16[64,2176]{1,0:T(8,128)(2,1)S(1)}, u32[]{:S(2)}, u32[]{:S(2)}) %collective-permute-start.20) | collective-permute-done | bytes 278560 | tf_op jit(solution)/shard_map/ppermute | solution.py:31
  117.5 0.9 scores.5
  118.4 1.6 %collective-permute-start.21 = (f32[192,512]{1,0:T(8,128)S(1)}, f32[192,512]{1,0:T(8,128)S(1)}, u32[]{:S(2)}, u32[]{:S(2)}) collective-permute-start(f32[192,512]{1,0:T(8,128)S(1)} %scores.5), channel_id=1, source_target_pairs={{0,8},{1,9},{2,10},{3,11},{4,12},{5,13},{6,14},{7,15},{8,0},{9,1},... | collective-permute-start | bytes 1179656 | tf_op jit(solution)/shard_map/ppermute | solution.py:31
  120.0 0.9 scores.4.far_ref
  120.9 0.5 collective-permute-done.21.far_other_ref
  121.4 1.3 norms.1
  122.7 5.1 %all-to-all-start.1 = ((f32[8,8,512]{2,1,0:T(8,128)}), f32[8,8,512]{2,1,0:T(8,128)S(1)}, u32[]{:S(2)}, u32[]{:S(2)}) async-start(f32[8,8,512]{2,1,0:T(8,128)} %get-tuple-element.50), calls=%async_computation.1 | async-start | bytes 262144 | tf_op jit(solution)/shard_map/all_to_all | solution.py:401
  127.8 6.9 %all-to-all-done.1.parts_ref = f32[8,8,512]{2,1,0:T(8,128)S(1)} async-done(((f32[8,8,512]{2,1,0:T(8,128)}), f32[8,8,512]{2,1,0:T(8,128)S(1)}, u32[]{:S(2)}, u32[]{:S(2)}) %all-to-all-start.1) | async-done | bytes 131104 | tf_op jit(solution)/shard_map/all_to_all | solution.py:401
  134.7 1.5 finish.1
  136.2 6.3 %all-to-all-start.2 = ((f32[32,1,512]{2,1,0:T(1,128)}), f32[32,1,512]{2,1,0:T(1,128)S(1)}, u32[]{:S(2)}, u32[]{:S(2)}) async-start(f32[32,1,512]{2,1,0:T(1,128)} %get-tuple-element.54), calls=%async_computation.2 | async-start | bytes 131072 | tf_op jit(solution)/shard_map/all_to_all | solution.py:403
  142.5 0.6 dynamic-slice_bitcast_fusion
  143.1 0.7 constant_dynamic-slice_fusion
  143.7 7.1 %all-to-all-done.2 = f32[32,1,512]{2,1,0:T(1,128)S(1)} async-done(((f32[32,1,512]{2,1,0:T(1,128)}), f32[32,1,512]{2,1,0:T(1,128)S(1)}, u32[]{:S(2)}, u32[]{:S(2)}) %all-to-all-start.2) | async-done | bytes 65568 | tf_op jit(solution)/shard_map/all_to_all | solution.py:403
  150.9 0.7 reshape.28
  (42 shorter events, 2.4 us)
Async XLA Ops:
  4.3 11.4 %copy-start.3 = (f32[4224]{0:T(1024)S(1)}, f32[4224]{0:T(1024)}, u32[]{:S(2)}) copy-start(f32[4224]{0:T(1024)} %noise_hbm.1) | copy-start | bytes 50692
  4.3 11.4 %copy-start.4 = (s32[64]{0:T(128)S(1)}, s32[64]{0:T(128)}, u32[]{:S(2)}) copy-start(s32[64]{0:T(128)} %param.8) | copy-start | bytes 772
  4.3 11.5 %copy-start = (f32[64,4224]{1,0:T(8,128)S(1)}, f32[64,4224]{1,0:T(8,128)}, u32[]{:S(2)}) copy-start(f32[64,4224]{1,0:T(8,128)} %contrast_ref.1) | copy-start | bytes 3244036
  4.3 11.5 %copy-start.1 = (bf16[64,8448]{1,0:T(8,128)(2,1)S(1)}, bf16[64,8448]{1,0:T(8,128)(2,1)}, u32[]{:S(2)}) copy-start(bf16[64,8448]{1,0:T(8,128)(2,1)} %images_ref) | copy-start | bytes 3244036
  4.3 42.1 %all-to-all-start = ((bf16[32,8,2176]{2,1,0:T(8,128)(2,1)}), bf16[32,8,2176]{2,1,0:T(8,128)(2,1)}, u32[]{:S(2)}, u32[]{:S(2)}) async-start(bf16[32,8,2176]{2,1,0:T(8,128)(2,1)} %bitcast.30), calls=%async_computation | async-start | bytes 2228224 | tf_op jit(solution)/shard_map/all_to_all | solution.py:359
  17.0 2.0 %collective-permute-start = (bf16[2,64,2176]{2,1,0:T(8,128)(2,1)S(1)}, bf16[2,64,2176]{2,1,0:T(8,128)(2,1)S(1)}, u32[]{:S(2)}, u32[]{:S(2)}) collective-permute-start(bf16[2,64,2176]{2,1,0:T(8,128)(2,1)S(1)} %get-tuple-element.56), channel_id=1, source_target_pairs={{0,8},{1,9},{2,10},{3,11},{4,12},{5,13},{6,14},{7,15},{8,0},{9,1},... | collective-permute-start | bytes 1671176 | tf_op jit(solution)/shard_map/ppermute | solution.py:31
  19.2 27.3 %collective-permute-start.1 = (bf16[2,2,64,2176]{3,2,1,0:T(8,128)(2,1)S(1)}, bf16[2,2,64,2176]{3,2,1,0:T(8,128)(2,1)S(1)}, u32[]{:S(2)}, u32[]{:S(2)}) collective-permute-start(bf16[2,2,64,2176]{3,2,1,0:T(8,128)(2,1)S(1)} %pad_maximum_fusion.refs_13_.refs_3_), channel_id=1, source_target_pairs={{0,2},{1,3},{2,4},{3,5},{4,6},{5,7},{6,0},{7,1},{8,10},{9,11},{10,... | collective-permute-start | bytes 3342344 | tf_op jit(solution)/shard_map/ppermute | solution.py:31
  20.5 26.0 %collective-permute-start.2 = (bf16[2,2,64,2176]{3,2,1,0:T(8,128)(2,1)S(1)}, bf16[2,2,64,2176]{3,2,1,0:T(8,128)(2,1)S(1)}, u32[]{:S(2)}, u32[]{:S(2)}) collective-permute-start(bf16[2,2,64,2176]{3,2,1,0:T(8,128)(2,1)S(1)} %pad_maximum_fusion.refs_13_.refs_3_), channel_id=1, source_target_pairs={{0,6},{1,7},{2,0},{3,1},{4,2},{5,3},{6,4},{7,5},{8,14},{9,15},{10,... | collective-permute-start | bytes 3342344 | tf_op jit(solution)/shard_map/ppermute | solution.py:31
  22.0 27.1 %copy-start.2 = (s32[8]{0:T(128)S(1)}, s32[8]{0:T(128)}, u32[]{:S(2)}) copy-start(s32[8]{0:T(128)} %owners_ref.1) | copy-start | bytes 100
  22.0 35.8 %collective-permute-start.5 = (bf16[2,2,64,2176]{3,2,1,0:T(8,128)(2,1)S(1)}, bf16[2,2,64,2176]{3,2,1,0:T(8,128)(2,1)}, u32[]{:S(2)}, u32[]{:S(2)}) collective-permute-start(bf16[2,2,64,2176]{3,2,1,0:T(8,128)(2,1)S(1)} %pad_maximum_fusion.refs_13_.refs_3_), channel_id=1, source_target_pairs={{0,1},{1,0},{2,3},{3,2},{4,5},{5,4},{6,7},{7,6},{8,9},{9,8},{10,11... | collective-permute-start | bytes 3342344 | tf_op jit(solution)/shard_map/ppermute | solution.py:31
  46.6 24.0 %collective-permute-start.9 = (bf16[2,2,64,2176]{3,2,1,0:T(8,128)(2,1)S(1)}, bf16[2,2,64,2176]{3,2,1,0:T(8,128)(2,1)S(1)}, u32[]{:S(2)}, u32[]{:S(2)}) collective-permute-start(bf16[2,2,64,2176]{3,2,1,0:T(8,128)(2,1)S(1)} %broadcast_select_fusion), channel_id=1, source_target_pairs={{0,2},{1,3},{2,4},{3,5},{4,6},{5,7},{6,0},{7,1},{8,14},{9,15},{10,... | collective-permute-start | bytes 3342344 | tf_op jit(solution)/shard_map/ppermute | solution.py:31
  50.5 8.6 %collective-permute-start.3 = (bf16[64,2176]{1,0:T(8,128)(2,1)S(1)}, bf16[64,2176]{1,0:T(8,128)(2,1)S(1)}, u32[]{:S(2)}, u32[]{:S(2)}) collective-permute-start(bf16[64,2176]{1,0:T(8,128)(2,1)S(1)} %bitcast.23), channel_id=1, source_target_pairs={{0,224},{1,225},{2,226},{3,227},{4,228},{5,229},{6,230},{7,231},{8... | collective-permute-start | bytes 835592 | tf_op jit(solution)/shard_map/ppermute | solution.py:31
  53.2 9.0 %collective-permute-start.4 = (bf16[64,2176]{1,0:T(8,128)(2,1)S(1)}, bf16[64,2176]{1,0:T(8,128)(2,1)S(1)}, u32[]{:S(2)}, u32[]{:S(2)}) collective-permute-start(bf16[64,2176]{1,0:T(8,128)(2,1)S(1)} %bitcast.24), channel_id=1, source_target_pairs={{0,32},{1,33},{2,34},{3,35},{4,36},{5,37},{6,38},{7,39},{8,40},{9,... | collective-permute-start | bytes 835592 | tf_op jit(solution)/shard_map/ppermute | solution.py:31
  53.2 10.8 %collective-permute-start.8 = (bf16[64,2176]{1,0:T(8,128)(2,1)S(1)}, bf16[64,2176]{1,0:T(8,128)(2,1)S(1)}, u32[]{:S(2)}, u32[]{:S(2)}) collective-permute-start(bf16[64,2176]{1,0:T(8,128)(2,1)S(1)} %bitcast.25), channel_id=1, source_target_pairs={{0,16},{1,17},{2,18},{3,19},{4,20},{5,21},{6,22},{7,23},{8,24},{9,... | collective-permute-start | bytes 835592 | tf_op jit(solution)/shard_map/ppermute | solution.py:31
  62.2 6.8 %collective-permute-start.6 = (bf16[64,2176]{1,0:T(8,128)(2,1)S(1)}, bf16[64,2176]{1,0:T(8,128)(2,1)S(1)}, u32[]{:S(2)}, u32[]{:S(2)}) collective-permute-start(bf16[64,2176]{1,0:T(8,128)(2,1)S(1)} %collective-permute-done.3.refs_1_), channel_id=1, source_target_pairs={{0,224},{1,225},{2,226},{3,227},{4,228},{5,229},{6,230},{7,231},{8... | collective-permute-start | bytes 835592 | tf_op jit(solution)/shard_map/ppermute | solution.py:31
  62.5 8.1 %collective-permute-start.7 = (bf16[64,2176]{1,0:T(8,128)(2,1)S(1)}, bf16[64,2176]{1,0:T(8,128)(2,1)S(1)}, u32[]{:S(2)}, u32[]{:S(2)}) collective-permute-start(bf16[64,2176]{1,0:T(8,128)(2,1)S(1)} %collective-permute-done.4.refs_4_), channel_id=1, source_target_pairs={{0,32},{1,33},{2,34},{3,35},{4,36},{5,37},{6,38},{7,39},{8,40},{9,... | collective-permute-start | bytes 835592 | tf_op jit(solution)/shard_map/ppermute | solution.py:31
  70.7 12.0 %collective-permute-start.10 = (bf16[2,64,2176]{2,1,0:T(8,128)(2,1)S(1)}, bf16[2,64,2176]{2,1,0:T(8,128)(2,1)S(1)}, u32[]{:S(2)}, u32[]{:S(2)}) collective-permute-start(bf16[2,64,2176]{2,1,0:T(8,128)(2,1)S(1)} %get-tuple-element.62), channel_id=1, source_target_pairs={{0,224},{1,225},{2,226},{3,227},{4,228},{5,229},{6,230},{7,231},{8... | collective-permute-start | bytes 1671176 | tf_op jit(solution)/shard_map/ppermute | solution.py:31
  71.0 13.1 %collective-permute-start.11 = (bf16[2,64,2176]{2,1,0:T(8,128)(2,1)S(1)}, bf16[2,64,2176]{2,1,0:T(8,128)(2,1)S(1)}, u32[]{:S(2)}, u32[]{:S(2)}) collective-permute-start(bf16[2,64,2176]{2,1,0:T(8,128)(2,1)S(1)} %get-tuple-element.61), channel_id=1, source_target_pairs={{0,32},{1,33},{2,34},{3,35},{4,36},{5,37},{6,38},{7,39},{8,40},{9,... | collective-permute-start | bytes 1671176 | tf_op jit(solution)/shard_map/ppermute | solution.py:31
  72.2 23.5 %collective-permute-start.14 = (bf16[2,2,64,2176]{3,2,1,0:T(8,128)(2,1)}, bf16[2,2,64,2176]{3,2,1,0:T(8,128)(2,1)S(1)}, u32[]{:S(2)}, u32[]{:S(2)}) collective-permute-start(bf16[2,2,64,2176]{3,2,1,0:T(8,128)(2,1)} %collective-permute-done.5.in_ref), channel_id=1, source_target_pairs={{0,6},{1,7},{2,0},{3,1},{4,2},{5,3},{6,4},{7,5},{8,14},{9,15},{10,... | collective-permute-start | bytes 3342344 | tf_op jit(solution)/shard_map/ppermute | solution.py:31
  72.2 25.7 %collective-permute-start.16 = (bf16[2,2,64,2176]{3,2,1,0:T(8,128)(2,1)}, bf16[2,2,64,2176]{3,2,1,0:T(8,128)(2,1)S(1)}, u32[]{:S(2)}, u32[]{:S(2)}) collective-permute-start(bf16[2,2,64,2176]{3,2,1,0:T(8,128)(2,1)} %collective-permute-done.5.in_ref), channel_id=1, source_target_pairs={{0,2},{1,3},{2,4},{3,5},{4,6},{5,7},{6,0},{7,1},{8,10},{9,11},{10,... | collective-permute-start | bytes 3342344 | tf_op jit(solution)/shard_map/ppermute | solution.py:31
  73.7 24.2 %collective-permute-start.15 = (bf16[2,2,64,2176]{3,2,1,0:T(8,128)(2,1)S(1)}, bf16[2,2,64,2176]{3,2,1,0:T(8,128)(2,1)S(1)}, u32[]{:S(2)}, u32[]{:S(2)}) collective-permute-start(bf16[2,2,64,2176]{3,2,1,0:T(8,128)(2,1)S(1)} %collective-permute-done.9.refs_17_.refs_7_), channel_id=1, source_target_pairs={{0,1},{1,0},{2,3},{3,2},{4,5},{5,4},{6,7},{7,6},{8,9},{9,8},{10,11... | collective-permute-start | bytes 3342344 | tf_op jit(solution)/shard_map/ppermute | solution.py:31
  84.3 9.3 %collective-permute-start.13 = (bf16[96,2176]{1,0:T(8,128)(2,1)S(1)}, bf16[96,2176]{1,0:T(8,128)(2,1)S(1)}, u32[]{:S(2)}, u32[]{:S(2)}) collective-permute-start(bf16[96,2176]{1,0:T(8,128)(2,1)S(1)} %pad_maximum_fusion.4), channel_id=1, source_target_pairs={{0,32},{1,33},{2,34},{3,35},{4,36},{5,37},{6,38},{7,39},{8,40},{9,... | collective-permute-start | bytes 1253384 | tf_op jit(solution)/shard_map/ppermute | solution.py:31
  84.5 9.2 %collective-permute-start.12 = (bf16[96,2176]{1,0:T(8,128)(2,1)S(1)}, bf16[96,2176]{1,0:T(8,128)(2,1)S(1)}, u32[]{:S(2)}, u32[]{:S(2)}) collective-permute-start(bf16[96,2176]{1,0:T(8,128)(2,1)S(1)} %pad_maximum_fusion.3), channel_id=1, source_target_pairs={{0,224},{1,225},{2,226},{3,227},{4,228},{5,229},{6,230},{7,231},{8... | collective-permute-start | bytes 1253384 | tf_op jit(solution)/shard_map/ppermute | solution.py:31
  102.1 19.3 %collective-permute-start.18 = (f32[512,512]{1,0:T(8,128)S(1)}, f32[512,512]{1,0:T(8,128)S(1)}, u32[]{:S(2)}, u32[]{:S(2)}) collective-permute-start(f32[512,512]{1,0:T(8,128)S(1)} %get-tuple-element.48), channel_id=1, source_target_pairs={{0,8},{1,9},{2,10},{3,11},{4,12},{5,13},{6,14},{7,15},{8,0},{9,1},... | collective-permute-start | bytes 3145736 | tf_op jit(solution)/shard_map/ppermute | solution.py:31
  106.4 8.2 %collective-permute-start.17 = (bf16[64,2176]{1,0:T(8,128)(2,1)S(1)}, bf16[64,2176]{1,0:T(8,128)(2,1)S(1)}, u32[]{:S(2)}, u32[]{:S(2)}) collective-permute-start(bf16[64,2176]{1,0:T(8,128)(2,1)S(1)} %pad_maximum_fusion.5.refs_7_), channel_id=1, source_target_pairs={{0,16},{1,17},{2,18},{3,19},{4,20},{5,21},{6,22},{7,23},{8,24},{9,... | collective-permute-start | bytes 835592 | tf_op jit(solution)/shard_map/ppermute | solution.py:31
  107.3 7.9 %collective-permute-start.19 = (bf16[64,2176]{1,0:T(8,128)(2,1)S(1)}, bf16[64,2176]{1,0:T(8,128)(2,1)S(1)}, u32[]{:S(2)}, u32[]{:S(2)}) collective-permute-start(bf16[64,2176]{1,0:T(8,128)(2,1)S(1)} %slice.40.refs_10_), channel_id=1, source_target_pairs={{0,224},{1,225},{2,226},{3,227},{4,228},{5,229},{6,230},{7,231},{8... | collective-permute-start | bytes 835592 | tf_op jit(solution)/shard_map/ppermute | solution.py:31
  108.8 8.8 %collective-permute-start.20 = (bf16[64,2176]{1,0:T(8,128)(2,1)S(1)}, bf16[64,2176]{1,0:T(8,128)(2,1)S(1)}, u32[]{:S(2)}, u32[]{:S(2)}) collective-permute-start(bf16[64,2176]{1,0:T(8,128)(2,1)S(1)} %slice.41.refs_11_), channel_id=1, source_target_pairs={{0,32},{1,33},{2,34},{3,35},{4,36},{5,37},{6,38},{7,39},{8,40},{9,... | collective-permute-start | bytes 835592 | tf_op jit(solution)/shard_map/ppermute | solution.py:31
  118.4 2.9 %collective-permute-start.21 = (f32[192,512]{1,0:T(8,128)S(1)}, f32[192,512]{1,0:T(8,128)S(1)}, u32[]{:S(2)}, u32[]{:S(2)}) collective-permute-start(f32[192,512]{1,0:T(8,128)S(1)} %scores.5), channel_id=1, source_target_pairs={{0,8},{1,9},{2,10},{3,11},{4,12},{5,13},{6,14},{7,15},{8,0},{9,1},... | collective-permute-start | bytes 1179656 | tf_op jit(solution)/shard_map/ppermute | solution.py:31
  122.7 12.0 %all-to-all-start.1 = ((f32[8,8,512]{2,1,0:T(8,128)}), f32[8,8,512]{2,1,0:T(8,128)S(1)}, u32[]{:S(2)}, u32[]{:S(2)}) async-start(f32[8,8,512]{2,1,0:T(8,128)} %get-tuple-element.50), calls=%async_computation.1 | async-start | bytes 262144 | tf_op jit(solution)/shard_map/all_to_all | solution.py:401
  136.2 14.6 %all-to-all-start.2 = ((f32[32,1,512]{2,1,0:T(1,128)}), f32[32,1,512]{2,1,0:T(1,128)S(1)}, u32[]{:S(2)}, u32[]{:S(2)}) async-start(f32[32,1,512]{2,1,0:T(1,128)} %get-tuple-element.54), calls=%async_computation.2 | async-start | bytes 131072 | tf_op jit(solution)/shard_map/all_to_all | solution.py:403
